TPU v7x, 256 devices: a whole 4x4x8 slice. The times are simulated.
256 devices in a mesh: tm: 32 (over y, z), row: 2 (over x_lo), col: 4 (over x_hi, core).
Axes of the slice: x: 4 (x_hi: 2, x_lo: 2; x = x_hi * 2 + x_lo), y: 4, z: 8, core: 2. Of those that a mesh axis runs over, the one named last changes fastest.
Arguments:
- latent: bfloat16 [32, 90, 64, 256], P('tm', 'row', 'col'), may hold values from -6 to 6
- conv1_weight: bfloat16 [3, 3, 3, 256, 256], replicated, may hold values from -0.078125 to 0.078125
- conv1_bias: float32 [256], replicated, may hold values from -3 to 3
- conv2_weight: bfloat16 [3, 3, 3, 256, 256], replicated, may hold values from -0.078125 to 0.078125
- conv2_bias: float32 [256], replicated, may hold values from -3 to 3
Outputs:
- mixed: bfloat16 [32, 90, 64, 256], P('tm', 'row', 'col')
All inputs are finite; a program needn't handle non-finite values.
Results may differ from a plain program's by a relative error of at most 0.0032.
Values may be sent and summed in bfloat16 or wider, within the bound.
No kernel may reach another device: no remote copies, remote signals or barrier semaphores. Data moves between devices by JAX's collectives and lax.ppermute only.
A program may use at most 64 MiB of HBM per device.

v0:
```python
import jax
import jax.numpy as jnp
from jax import lax
from jax.sharding import PartitionSpec as P


def passed_along(value, axis, steps):
    count = lax.axis_size(axis)
    leading, last = (max(0, -steps), min(count, count - steps))
    return lax.ppermute(value, axis, [(source, source + steps) for source in range(leading, last)])


def with_halo(cells, sides, width):
    for axis, dim in sides:
        count = lax.axis_size(axis)
        ends = count - 1
        head = lax.slice_in_dim(cells, 0, width, axis=dim)
        tail = lax.slice_in_dim(cells, cells.shape[dim] - width, cells.shape[dim], axis=dim)
        cells = jnp.concatenate(
            [
                lax.ppermute(tail, axis, [(i, (i + 1) % count) for i in range(ends)]),
                cells,
                lax.ppermute(head, axis, [((i + 1) % count, i) for i in range(ends)]),
            ],
            axis=dim,
        )
    return cells


def convolve(frames, weight, bias):
    in_channels = weight.shape[3]
    out_channels = weight.shape[4]
    taps = weight.reshape(3, 3, 3 * in_channels, out_channels)
    out_rows = frames[0].shape[0] - 2
    out_cols = frames[0].shape[1] - 2
    total = jnp.zeros((out_rows * out_cols, out_channels), jnp.float32)
    for tap_time in range(3):
        for tap_row in range(3):
            band = frames[tap_time][tap_row : tap_row + out_rows]
            joined = jnp.concatenate(
                [band[:, tap_col : tap_col + out_cols] for tap_col in range(3)], axis=-1
            )
            joined = joined.reshape(out_rows * out_cols, 3 * in_channels)
            total = total + jnp.dot(
                joined, taps[tap_time, tap_row], preferred_element_type=jnp.float32
            )
    return (total + bias).reshape(out_rows, out_cols, out_channels)


def clamp_one(values, margin, dimension, device_index, device_count):
    extent = values.shape[dimension]
    position = lax.broadcasted_iota(jnp.int32, values.shape, dimension)
    lower_edge = lax.slice_in_dim(values, margin, margin + 1, axis=dimension)
    upper_edge = lax.slice_in_dim(values, extent - margin - 1, extent - margin, axis=dimension)
    values = jnp.where((device_index == 0) & (position < margin), lower_edge, values)
    values = jnp.where(
        (device_index == device_count - 1) & (position >= extent - margin), upper_edge, values
    )
    return values


def clamp_edges(values, margin, first_dim):
    values = clamp_one(values, margin, first_dim, lax.axis_index("row"), lax.axis_size("row"))
    values = clamp_one(values, margin, first_dim + 1, lax.axis_index("col"), lax.axis_size("col"))
    return values


def time_frames(current):
    earlier = passed_along(current, "tm", 1)
    earliest = passed_along(current, "tm", 2)
    position = lax.axis_index("tm")
    earlier = jnp.where(position >= 1, earlier, current)
    earliest = jnp.where(position >= 2, earliest, earlier)
    return (earliest, earlier, current)


def local(latent, conv1_weight, conv1_bias, conv2_weight, conv2_bias):
    source = latent[0]
    active = jax.nn.silu(source.astype(jnp.float32)).astype(jnp.bfloat16)

    def padded_frames(current):
        stacked = jnp.stack(time_frames(current))
        grown = with_halo(stacked, (("row", 1), ("col", 2)), 1)
        grown = clamp_edges(grown, 1, 1)
        return (grown[0], grown[1], grown[2])

    hidden = jax.nn.silu(convolve(padded_frames(active), conv1_weight, conv1_bias)).astype(
        jnp.bfloat16
    )
    result = convolve(padded_frames(hidden), conv2_weight, conv2_bias)
    mixed = (source.astype(jnp.float32) + result).astype(jnp.bfloat16)
    return mixed[None]


def solution(mesh):
    in_specs = (P("tm", "row", "col", None), P(), P(), P(), P())
    out_specs = P("tm", "row", "col", None)
    return jax.shard_map(local, mesh=mesh, in_specs=in_specs, out_specs=out_specs, check_vma=False)
```

profile of v0, /device:TPU:6, one launch (start us, length us, event | category | flops | bytes accessed | tf_op | source)
XLA Modules:
  0.0 132.0 jit_solution(8889794570032897514)
XLA Ops:
  0.0 1.3 fusion.7
  1.3 5.2 %collective-permute-start = (bf16[45,16,256]{2,1,0:T(8,128)(2,1)S(1)}, bf16[45,16,256]{2,1,0:T(8,128)(2,1)S(1)}, u32[]{:S(2)}, u32[]{:S(2)}) collective-permute-start(bf16[45,16,256]{2,1,0:T(8,128)(2,1)S(1)} %fusion.7), channel_id=1, source_target_pairs={{0,16},{8,24},{16,32},{24,40},{32,48},{40,56},{48,64},{56,72},{64,... | collective-permute-start | bytes 1105928 | tf_op jit(solution)/shard_map/ppermute | solution.py:10
  6.5 3.8 %collective-permute-start.1 = (bf16[45,16,256]{2,1,0:T(8,128)(2,1)S(1)}, bf16[45,16,256]{2,1,0:T(8,128)(2,1)S(1)}, u32[]{:S(2)}, u32[]{:S(2)}) collective-permute-start(bf16[45,16,256]{2,1,0:T(8,128)(2,1)S(1)} %fusion.7), channel_id=1, source_target_pairs={{0,8},{8,16},{16,24},{24,32},{32,40},{40,48},{48,56},{56,64},{64,7... | collective-permute-start | bytes 1105928 | tf_op jit(solution)/shard_map/ppermute | solution.py:10
  10.4 1.2 fusion.14
  11.6 6.5 %collective-permute-done = bf16[45,16,256]{2,1,0:T(8,128)(2,1)S(1)} collective-permute-done((bf16[45,16,256]{2,1,0:T(8,128)(2,1)S(1)}, bf16[45,16,256]{2,1,0:T(8,128)(2,1)S(1)}, u32[]{:S(2)}, u32[]{:S(2)}) %collective-permute-start) | collective-permute-done | bytes 368672 | tf_op jit(solution)/shard_map/ppermute | solution.py:10
  18.1 12.1 %collective-permute-done.1 = bf16[45,16,256]{2,1,0:T(8,128)(2,1)S(1)} collective-permute-done((bf16[45,16,256]{2,1,0:T(8,128)(2,1)S(1)}, bf16[45,16,256]{2,1,0:T(8,128)(2,1)S(1)}, u32[]{:S(2)}, u32[]{:S(2)}) %collective-permute-start.1) | collective-permute-done | bytes 368672 | tf_op jit(solution)/shard_map/ppermute | solution.py:10
  30.5 2.7 %collective-permute-start.3 = (bf16[3,1,16,256]{3,2,0,1:T(8,128)(2,1)S(1)}, bf16[3,1,16,256]{3,2,0,1:T(8,128)(2,1)S(1)}, u32[]{:S(2)}, u32[]{:S(2)}) collective-permute-start(bf16[3,1,16,256]{3,2,0,1:T(8,128)(2,1)S(1)} %get-tuple-element.38), channel_id=1, source_target_pairs={{4,0},{5,1},{6,2},{7,3},{12,8},{13,9},{14,10},{15,11},{20,16},{21,... | collective-permute-start | bytes 73736 | tf_op jit(solution)/shard_map/ppermute | solution.py:23
  33.3 1.3 collective-permute-start.2
  34.8 4.2 %collective-permute-done.2 = bf16[3,1,16,256]{3,2,0,1:T(8,128)(2,1)S(1)} collective-permute-done((bf16[3,1,16,256]{3,2,0,1:T(8,128)(2,1)S(1)}, bf16[3,1,16,256]{3,2,0,1:T(8,128)(2,1)S(1)}, u32[]{:S(2)}, u32[]{:S(2)}) %collective-permute-start.2) | collective-permute-done | bytes 24608 | tf_op jit(solution)/shard_map/ppermute | solution.py:21
  39.3 1.9 %collective-permute-start.5 = (bf16[3,47,1,256]{3,2,0,1:T(2,128)(2,1)S(1)}, bf16[3,47,1,256]{3,2,0,1:T(2,128)(2,1)S(1)}, u32[]{:S(2)}, u32[]{:S(2)}) collective-permute-start(bf16[3,47,1,256]{3,2,0,1:T(2,128)(2,1)S(1)} %get-tuple-element.34), channel_id=1, source_target_pairs={{1,0},{2,1},{3,2},{5,4},{6,5},{7,6},{9,8},{10,9},{11,10},{13,12},{... | collective-permute-start | bytes 216584 | tf_op jit(solution)/shard_map/ppermute | solution.py:23
  41.2 2.4 %collective-permute-start.4 = (bf16[3,47,1,256]{3,2,0,1:T(2,128)(2,1)S(1)}, bf16[3,47,1,256]{3,2,0,1:T(2,128)(2,1)S(1)}, u32[]{:S(2)}, u32[]{:S(2)}) collective-permute-start(bf16[3,47,1,256]{3,2,0,1:T(2,128)(2,1)S(1)} %get-tuple-element.33), channel_id=1, source_target_pairs={{0,1},{1,2},{2,3},{4,5},{5,6},{6,7},{8,9},{9,10},{10,11},{12,13},{... | collective-permute-start | bytes 216584 | tf_op jit(solution)/shard_map/ppermute | solution.py:21
  43.8 5.3 %collective-permute-done.4 = bf16[3,47,1,256]{3,2,0,1:T(2,128)(2,1)S(1)} collective-permute-done((bf16[3,47,1,256]{3,2,0,1:T(2,128)(2,1)S(1)}, bf16[3,47,1,256]{3,2,0,1:T(2,128)(2,1)S(1)}, u32[]{:S(2)}, u32[]{:S(2)}) %collective-permute-start.4) | collective-permute-done | bytes 72224 | tf_op jit(solution)/shard_map/ppermute | solution.py:21
  49.1 1.4 %pad_maximum_fusion = bf16[3,47,18,256]{3,2,0,1:T(8,128)(2,1)S(1)} fusion(bf16[3,47,1,256]{3,2,0,1:T(2,128)(2,1)S(1)} %collective-permute-done.5, bf16[3,1,16,256]{3,2,0,1:T(8,128)(2,1)S(1)} %collective-permute-done.3, bf16[1,45,16,256]{3,2,0,1:T(8,128)(2,1)S(1)} %fusion.14, bf16[1,45,16,256]{3,2,0,1:T(8,128)(2,1)S(1)} %get-tuple-element.42, ...), kind=kLoop, calls=%fused_computation | loop fusion | flops 9096192 | bytes 2598912 | tf_op jit(solution)/shard_map/concatenate | solution.py:19
  50.6 3.2 %select_select_fusion.3 = bf16[3,47,18,256]{3,2,0,1:T(8,128)(2,1)S(1)} fusion(pred[47]{0:T(512)(128)(4,1)S(1)} %get-tuple-element.97, pred[47]{0:T(512)(128)(4,1)S(1)} %get-tuple-element.98, bf16[3,18,256]{2,1,0:T(8,128)(2,1)S(1)} %get-tuple-element.30, bf16[3,18,256]{2,1,0:T(8,128)(2,1)S(1)} %get-tuple-element.29, ...), kind=kLoop, calls=%fused_computation.5 | loop fusion | flops 10395648 | bytes 2654302 | tf_op jit(solution)/shard_map/jit(_where)/select_n | solution.py:56
  54.2 4.1 %select_select_fusion.2 = bf16[3,47,18,256]{3,2,0,1:T(8,128)(2,1)S(1)} fusion(pred[18]{0:T(512)(128)(4,1)S(1)} %get-tuple-element.99, pred[18]{0:T(512)(128)(4,1)S(1)} %get-tuple-element.100, bf16[3,47,256]{2,0,1:T(4,128)(2,1)S(1)} %copy.26, bf16[3,47,256]{2,0,1:T(4,128)(2,1)S(1)} %copy.24, bf16[3,18,256]{2,1,0:T(8,128)(2,1)S(1)} %get-tuple-element.30, ...), kind=kLoop, calls=%fused_computation.4 | loop fusion | flops 11695104 | bytes 2798722 | tf_op jit(solution)/shard_map/jit(_where)/select_n | solution.py:56
  61.1 1.6 %copy-done.1 = bf16[3,3,3,256,256]{4,3,2,1,0:T(8,128)(2,1)S(1)} copy-done((bf16[3,3,3,256,256]{4,3,2,1,0:T(8,128)(2,1)S(1)}, bf16[3,3,3,256,256]{4,3,2,1,0:T(8,128)(2,1)}, u32[]{:S(2)}) %copy-start.1) | copy-done | bytes 3538968
  63.3 0.5 convolution_add_fusion.15
  63.9 0.5 convolution_add_fusion.14
  64.4 0.5 convolution_add_fusion.13
  65.0 0.5 convolution_add_fusion.12
  66.1 0.5 convolution_add_fusion.10
  66.6 0.5 convolution_add_fusion.9
  67.2 0.6 copy-done.3
  67.8 0.5 fusion.1
  68.5 6.3 %collective-permute-start.6 = (bf16[45,16,256]{2,1,0:T(8,128)(2,1)S(1)}, bf16[45,16,256]{2,1,0:T(8,128)(2,1)S(1)}, u32[]{:S(2)}, u32[]{:S(2)}) collective-permute-start(bf16[45,16,256]{2,1,0:T(8,128)(2,1)S(1)} %multiply_convert_fusion.1), channel_id=1, source_target_pairs={{0,16},{8,24},{16,32},{24,40},{32,48},{40,56},{48,64},{56,72},{64,... | collective-permute-start | bytes 1105928 | tf_op jit(solution)/shard_map/ppermute | solution.py:10
  74.7 4.4 %collective-permute-start.7 = (bf16[45,16,256]{2,1,0:T(8,128)(2,1)S(1)}, bf16[45,16,256]{2,1,0:T(8,128)(2,1)S(1)}, u32[]{:S(2)}, u32[]{:S(2)}) collective-permute-start(bf16[45,16,256]{2,1,0:T(8,128)(2,1)S(1)} %multiply_convert_fusion.1), channel_id=1, source_target_pairs={{0,8},{8,16},{16,24},{24,32},{32,40},{40,48},{48,56},{56,64},{64,7... | collective-permute-start | bytes 1105928 | tf_op jit(solution)/shard_map/ppermute | solution.py:10
  79.4 8.4 %collective-permute-done.6 = bf16[45,16,256]{2,1,0:T(8,128)(2,1)S(1)} collective-permute-done((bf16[45,16,256]{2,1,0:T(8,128)(2,1)S(1)}, bf16[45,16,256]{2,1,0:T(8,128)(2,1)S(1)}, u32[]{:S(2)}, u32[]{:S(2)}) %collective-permute-start.6) | collective-permute-done | bytes 368672 | tf_op jit(solution)/shard_map/ppermute | solution.py:10
  87.8 6.6 %collective-permute-done.7 = bf16[45,16,256]{2,1,0:T(8,128)(2,1)S(1)} collective-permute-done((bf16[45,16,256]{2,1,0:T(8,128)(2,1)S(1)}, bf16[45,16,256]{2,1,0:T(8,128)(2,1)S(1)}, u32[]{:S(2)}, u32[]{:S(2)}) %collective-permute-start.7) | collective-permute-done | bytes 368672 | tf_op jit(solution)/shard_map/ppermute | solution.py:10
  94.7 1.6 %collective-permute-start.9 = (bf16[3,1,16,256]{3,2,0,1:T(8,128)(2,1)S(1)}, bf16[3,1,16,256]{3,2,0,1:T(8,128)(2,1)S(1)}, u32[]{:S(2)}, u32[]{:S(2)}) collective-permute-start(bf16[3,1,16,256]{3,2,0,1:T(8,128)(2,1)S(1)} %get-tuple-element.36), channel_id=1, source_target_pairs={{4,0},{5,1},{6,2},{7,3},{12,8},{13,9},{14,10},{15,11},{20,16},{21,... | collective-permute-start | bytes 73736 | tf_op jit(solution)/shard_map/ppermute | solution.py:23
  96.3 1.3 collective-permute-start.8
  97.8 4.2 %collective-permute-done.8 = bf16[3,1,16,256]{3,2,0,1:T(8,128)(2,1)S(1)} collective-permute-done((bf16[3,1,16,256]{3,2,0,1:T(8,128)(2,1)S(1)}, bf16[3,1,16,256]{3,2,0,1:T(8,128)(2,1)S(1)}, u32[]{:S(2)}, u32[]{:S(2)}) %collective-permute-start.8) | collective-permute-done | bytes 24608 | tf_op jit(solution)/shard_map/ppermute | solution.py:21
  102.3 2.0 %collective-permute-start.11 = (bf16[3,47,1,256]{3,2,0,1:T(2,128)(2,1)S(1)}, bf16[3,47,1,256]{3,2,0,1:T(2,128)(2,1)S(1)}, u32[]{:S(2)}, u32[]{:S(2)}) collective-permute-start(bf16[3,47,1,256]{3,2,0,1:T(2,128)(2,1)S(1)} %get-tuple-element.32), channel_id=1, source_target_pairs={{1,0},{2,1},{3,2},{5,4},{6,5},{7,6},{9,8},{10,9},{11,10},{13,12},{... | collective-permute-start | bytes 216584 | tf_op jit(solution)/shard_map/ppermute | solution.py:23
  104.3 2.4 %collective-permute-start.10 = (bf16[3,47,1,256]{3,2,0,1:T(2,128)(2,1)S(1)}, bf16[3,47,1,256]{3,2,0,1:T(2,128)(2,1)S(1)}, u32[]{:S(2)}, u32[]{:S(2)}) collective-permute-start(bf16[3,47,1,256]{3,2,0,1:T(2,128)(2,1)S(1)} %get-tuple-element.31), channel_id=1, source_target_pairs={{0,1},{1,2},{2,3},{4,5},{5,6},{6,7},{8,9},{9,10},{10,11},{12,13},{... | collective-permute-start | bytes 216584 | tf_op jit(solution)/shard_map/ppermute | solution.py:21
  106.9 5.3 %collective-permute-done.10 = bf16[3,47,1,256]{3,2,0,1:T(2,128)(2,1)S(1)} collective-permute-done((bf16[3,47,1,256]{3,2,0,1:T(2,128)(2,1)S(1)}, bf16[3,47,1,256]{3,2,0,1:T(2,128)(2,1)S(1)}, u32[]{:S(2)}, u32[]{:S(2)}) %collective-permute-start.10) | collective-permute-done | bytes 72224 | tf_op jit(solution)/shard_map/ppermute | solution.py:21
  112.2 1.4 %pad_maximum_fusion.1 = bf16[3,47,18,256]{3,2,0,1:T(8,128)(2,1)S(1)} fusion(bf16[3,47,1,256]{3,2,0,1:T(2,128)(2,1)S(1)} %collective-permute-done.11, bf16[3,1,16,256]{3,2,0,1:T(8,128)(2,1)S(1)} %collective-permute-done.9, bf16[1,45,16,256]{3,2,0,1:T(8,128)(2,1)S(1)} %multiply_convert_fusion, bf16[1,45,16,256]{3,2,0,1:T(8,128)(2,1)S(1)} %get-tuple-element.40, ...), kind=kLoop, calls=%fused_computation.1 | loop fusion | flops 9096192 | bytes 2598912 | tf_op jit(solution)/shard_map/concatenate | solution.py:19
  113.7 3.2 %select_select_fusion.1 = bf16[3,47,18,256]{3,2,0,1:T(8,128)(2,1)S(1)} fusion(pred[47]{0:T(512)(128)(4,1)S(1)} %get-tuple-element.97, pred[47]{0:T(512)(128)(4,1)S(1)} %get-tuple-element.98, bf16[3,18,256]{2,1,0:T(8,128)(2,1)S(1)} %get-tuple-element.17, bf16[3,18,256]{2,1,0:T(8,128)(2,1)S(1)} %get-tuple-element.16, ...), kind=kLoop, calls=%fused_computation.3 | loop fusion | flops 10395648 | bytes 2654302 | tf_op jit(solution)/shard_map/jit(_where)/select_n | solution.py:56
  117.3 3.9 %select_select_fusion = bf16[3,47,18,256]{3,2,0,1:T(8,128)(2,1)S(1)} fusion(pred[18]{0:T(512)(128)(4,1)S(1)} %get-tuple-element.99, pred[18]{0:T(512)(128)(4,1)S(1)} %get-tuple-element.100, bf16[3,47,256]{2,0,1:T(4,128)(2,1)S(1)} %copy.34, bf16[3,47,256]{2,0,1:T(4,128)(2,1)S(1)} %copy.32, bf16[3,18,256]{2,1,0:T(8,128)(2,1)S(1)} %get-tuple-element.17, ...), kind=kLoop, calls=%fused_computation.2 | loop fusion | flops 11695104 | bytes 2798722 | tf_op jit(solution)/shard_map/jit(_where)/select_n | solution.py:56
  124.0 1.6 %copy-done.2 = bf16[3,3,3,256,256]{4,3,2,1,0:T(8,128)(2,1)S(1)} copy-done((bf16[3,3,3,256,256]{4,3,2,1,0:T(8,128)(2,1)S(1)}, bf16[3,3,3,256,256]{4,3,2,1,0:T(8,128)(2,1)}, u32[]{:S(2)}) %copy-start.2) | copy-done | bytes 3538968
  126.2 0.5 convolution_add_fusion.7
  126.7 0.5 convolution_add_fusion.6
  127.3 0.5 convolution_add_fusion.5
  127.8 0.5 convolution_add_fusion.4
  128.4 0.5 convolution_add_fusion.3
  128.9 0.5 convolution_add_fusion.2
  129.5 0.5 convolution_add_fusion.1
  130.1 0.6 copy-done.4
  130.7 0.5 fusion
  131.1 0.9 fusion.13
  (73 shorter events, 11.2 us)
Async XLA Ops:
  0.0 30.2 %copy-start = (bf16[1,45,16,256]{3,2,1,0:T(8,128)(2,1)S(1)}, bf16[1,45,16,256]{3,2,1,0:T(8,128)(2,1)}, u32[]{:S(2)}) copy-start(bf16[1,45,16,256]{3,2,1,0:T(8,128)(2,1)} %param.5) | copy-start | bytes 1105924
  1.3 16.8 %collective-permute-start = (bf16[45,16,256]{2,1,0:T(8,128)(2,1)S(1)}, bf16[45,16,256]{2,1,0:T(8,128)(2,1)S(1)}, u32[]{:S(2)}, u32[]{:S(2)}) collective-permute-start(bf16[45,16,256]{2,1,0:T(8,128)(2,1)S(1)} %fusion.7), channel_id=1, source_target_pairs={{0,16},{8,24},{16,32},{24,40},{32,48},{40,56},{48,64},{56,72},{64,... | collective-permute-start | bytes 1105928 | tf_op jit(solution)/shard_map/ppermute | solution.py:10
  6.5 23.7 %collective-permute-start.1 = (bf16[45,16,256]{2,1,0:T(8,128)(2,1)S(1)}, bf16[45,16,256]{2,1,0:T(8,128)(2,1)S(1)}, u32[]{:S(2)}, u32[]{:S(2)}) collective-permute-start(bf16[45,16,256]{2,1,0:T(8,128)(2,1)S(1)} %fusion.7), channel_id=1, source_target_pairs={{0,8},{8,16},{16,24},{24,32},{32,40},{40,48},{48,56},{56,64},{64,7... | collective-permute-start | bytes 1105928 | tf_op jit(solution)/shard_map/ppermute | solution.py:10
  30.5 4.2 %collective-permute-start.3 = (bf16[3,1,16,256]{3,2,0,1:T(8,128)(2,1)S(1)}, bf16[3,1,16,256]{3,2,0,1:T(8,128)(2,1)S(1)}, u32[]{:S(2)}, u32[]{:S(2)}) collective-permute-start(bf16[3,1,16,256]{3,2,0,1:T(8,128)(2,1)S(1)} %get-tuple-element.38), channel_id=1, source_target_pairs={{4,0},{5,1},{6,2},{7,3},{12,8},{13,9},{14,10},{15,11},{20,16},{21,... | collective-permute-start | bytes 73736 | tf_op jit(solution)/shard_map/ppermute | solution.py:23
  33.3 5.7 %collective-permute-start.2 = (bf16[3,1,16,256]{3,2,0,1:T(8,128)(2,1)S(1)}, bf16[3,1,16,256]{3,2,0,1:T(8,128)(2,1)S(1)}, u32[]{:S(2)}, u32[]{:S(2)}) collective-permute-start(bf16[3,1,16,256]{3,2,0,1:T(8,128)(2,1)S(1)} %get-tuple-element.37), channel_id=1, source_target_pairs={{0,4},{1,5},{2,6},{3,7},{8,12},{9,13},{10,14},{11,15},{16,20},{17,... | collective-permute-start | bytes 73736 | tf_op jit(solution)/shard_map/ppermute | solution.py:21
  39.3 4.6 %collective-permute-start.5 = (bf16[3,47,1,256]{3,2,0,1:T(2,128)(2,1)S(1)}, bf16[3,47,1,256]{3,2,0,1:T(2,128)(2,1)S(1)}, u32[]{:S(2)}, u32[]{:S(2)}) collective-permute-start(bf16[3,47,1,256]{3,2,0,1:T(2,128)(2,1)S(1)} %get-tuple-element.34), channel_id=1, source_target_pairs={{1,0},{2,1},{3,2},{5,4},{6,5},{7,6},{9,8},{10,9},{11,10},{13,12},{... | collective-permute-start | bytes 216584 | tf_op jit(solution)/shard_map/ppermute | solution.py:23
  41.2 7.9 %collective-permute-start.4 = (bf16[3,47,1,256]{3,2,0,1:T(2,128)(2,1)S(1)}, bf16[3,47,1,256]{3,2,0,1:T(2,128)(2,1)S(1)}, u32[]{:S(2)}, u32[]{:S(2)}) collective-permute-start(bf16[3,47,1,256]{3,2,0,1:T(2,128)(2,1)S(1)} %get-tuple-element.33), channel_id=1, source_target_pairs={{0,1},{1,2},{2,3},{4,5},{5,6},{6,7},{8,9},{9,10},{10,11},{12,13},{... | collective-permute-start | bytes 216584 | tf_op jit(solution)/shard_map/ppermute | solution.py:21
  60.7 2.0 %copy-start.1 = (bf16[3,3,3,256,256]{4,3,2,1,0:T(8,128)(2,1)S(1)}, bf16[3,3,3,256,256]{4,3,2,1,0:T(8,128)(2,1)}, u32[]{:S(2)}) copy-start(bf16[3,3,3,256,256]{4,3,2,1,0:T(8,128)(2,1)} %param.6) | copy-start | bytes 10616836
  67.1 0.7 copy-start.3
  68.5 19.3 %collective-permute-start.6 = (bf16[45,16,256]{2,1,0:T(8,128)(2,1)S(1)}, bf16[45,16,256]{2,1,0:T(8,128)(2,1)S(1)}, u32[]{:S(2)}, u32[]{:S(2)}) collective-permute-start(bf16[45,16,256]{2,1,0:T(8,128)(2,1)S(1)} %multiply_convert_fusion.1), channel_id=1, source_target_pairs={{0,16},{8,24},{16,32},{24,40},{32,48},{40,56},{48,64},{56,72},{64,... | collective-permute-start | bytes 1105928 | tf_op jit(solution)/shard_map/ppermute | solution.py:10
  74.7 19.6 %collective-permute-start.7 = (bf16[45,16,256]{2,1,0:T(8,128)(2,1)S(1)}, bf16[45,16,256]{2,1,0:T(8,128)(2,1)S(1)}, u32[]{:S(2)}, u32[]{:S(2)}) collective-permute-start(bf16[45,16,256]{2,1,0:T(8,128)(2,1)S(1)} %multiply_convert_fusion.1), channel_id=1, source_target_pairs={{0,8},{8,16},{16,24},{24,32},{32,40},{40,48},{48,56},{56,64},{64,7... | collective-permute-start | bytes 1105928 | tf_op jit(solution)/shard_map/ppermute | solution.py:10
  94.7 3.1 %collective-permute-start.9 = (bf16[3,1,16,256]{3,2,0,1:T(8,128)(2,1)S(1)}, bf16[3,1,16,256]{3,2,0,1:T(8,128)(2,1)S(1)}, u32[]{:S(2)}, u32[]{:S(2)}) collective-permute-start(bf16[3,1,16,256]{3,2,0,1:T(8,128)(2,1)S(1)} %get-tuple-element.36), channel_id=1, source_target_pairs={{4,0},{5,1},{6,2},{7,3},{12,8},{13,9},{14,10},{15,11},{20,16},{21,... | collective-permute-start | bytes 73736 | tf_op jit(solution)/shard_map/ppermute | solution.py:23
  96.3 5.7 %collective-permute-start.8 = (bf16[3,1,16,256]{3,2,0,1:T(8,128)(2,1)S(1)}, bf16[3,1,16,256]{3,2,0,1:T(8,128)(2,1)S(1)}, u32[]{:S(2)}, u32[]{:S(2)}) collective-permute-start(bf16[3,1,16,256]{3,2,0,1:T(8,128)(2,1)S(1)} %get-tuple-element.35), channel_id=1, source_target_pairs={{0,4},{1,5},{2,6},{3,7},{8,12},{9,13},{10,14},{11,15},{16,20},{17,... | collective-permute-start | bytes 73736 | tf_op jit(solution)/shard_map/ppermute | solution.py:21
  102.3 4.6 %collective-permute-start.11 = (bf16[3,47,1,256]{3,2,0,1:T(2,128)(2,1)S(1)}, bf16[3,47,1,256]{3,2,0,1:T(2,128)(2,1)S(1)}, u32[]{:S(2)}, u32[]{:S(2)}) collective-permute-start(bf16[3,47,1,256]{3,2,0,1:T(2,128)(2,1)S(1)} %get-tuple-element.32), channel_id=1, source_target_pairs={{1,0},{2,1},{3,2},{5,4},{6,5},{7,6},{9,8},{10,9},{11,10},{13,12},{... | collective-permute-start | bytes 216584 | tf_op jit(solution)/shard_map/ppermute | solution.py:23
  104.3 7.9 %collective-permute-start.10 = (bf16[3,47,1,256]{3,2,0,1:T(2,128)(2,1)S(1)}, bf16[3,47,1,256]{3,2,0,1:T(2,128)(2,1)S(1)}, u32[]{:S(2)}, u32[]{:S(2)}) collective-permute-start(bf16[3,47,1,256]{3,2,0,1:T(2,128)(2,1)S(1)} %get-tuple-element.31), channel_id=1, source_target_pairs={{0,1},{1,2},{2,3},{4,5},{5,6},{6,7},{8,9},{9,10},{10,11},{12,13},{... | collective-permute-start | bytes 216584 | tf_op jit(solution)/shard_map/ppermute | solution.py:21
  123.6 2.0 %copy-start.2 = (bf16[3,3,3,256,256]{4,3,2,1,0:T(8,128)(2,1)S(1)}, bf16[3,3,3,256,256]{4,3,2,1,0:T(8,128)(2,1)}, u32[]{:S(2)}) copy-start(bf16[3,3,3,256,256]{4,3,2,1,0:T(8,128)(2,1)} %param.8) | copy-start | bytes 10616836
  130.0 0.7 copy-start.4
where the time goes:
time: 135 us; the launch traced here: 132 us
  waiting for transfers between devices  53.5 us (40%)
  starting transfers between devices  35.3 us (26%)
  other arithmetic  23.6 us (17%)
  local copies, waits for them, and re-layouts  10.5 us (8%)
  matrix products  8.37 us (6%)
    ppermute x4, waiting for transfers between devices, passed_along(): lax.ppermute(value, axis, [(source, source + steps) for source in range(l...  33.6 us
    ppermute x4, starting transfers between devices, passed_along(): lax.ppermute(value, axis, [(source, source + steps) for source in range(l...  19.7 us
    ppermute x4, waiting for transfers between devices, with_halo(): lax.ppermute(tail, axis, [(i, (i + 1) % count) for i in range(ends)])  19.1 us
    select_n x4, other arithmetic, clamp_one(): jnp.where((device_index == device_count - 1) & (position >= extent - marg...  14.4 us
    dot_general x18, matrix products, convolve(): jnp.dot(joined, taps[tap_time, tap_row], preferred_element_type=jnp.float32)  8.37 us
    ppermute x4, starting transfers between devices, with_halo(): lax.ppermute(head, axis, [((i + 1) % count, i) for i in range(ends)])  8.24 us
    ppermute x4, starting transfers between devices, with_halo(): lax.ppermute(tail, axis, [(i, (i + 1) % count) for i in range(ends)])  7.37 us
    slice x18, local copies, waits for them, and re-layouts, convolve(): band[:, tap_col:tap_col + out_cols]  4.68 us
  transfers between devices with their start and end apart: 12, of which 12 were waited for; matrix products, arithmetic and copies ran while one was open for 1% of the time, Pallas kernels for 0%

commit v1 on v0

v1 whole, which is shorter than its diff:
```python
import functools

import jax
import jax.numpy as jnp
from jax import lax
from jax.experimental import pallas as pl
from jax.experimental.pallas import tpu as pltpu
from jax.sharding import PartitionSpec as P

RING = 8
CH = 256
ROWS, COLS = 45, 16
WIDE = 32
PR = ROWS + 3
HR = ROWS + 1
MAIN = HR * COLS
SIDE = PR
ACC = MAIN + 2 * SIDE
BF, F32 = jnp.bfloat16, jnp.float32


def shifted(count, steps):
    return [(i, (i + steps) % count) for i in range(count)]


def backward_place(source, steps, count):
    block, place = divmod(source, RING)
    if place >= steps:
        return ((block + 1) * RING + place - steps) % count
    return block * RING + place + RING - steps


def backward(count, done, steps):
    return [
        (
            backward_place(i, done, count) if done else i,
            backward_place(i, done + steps, count),
        )
        for i in range(count)
    ]


def silu(v):
    return v / (1.0 + jnp.exp(-v))


def rounded(v):
    return v.astype(BF).astype(F32)


def take(work, start, size, stride=None):
    return jnp.concatenate([work[h, pl.ds(start, size, stride), :] for h in range(2)], axis=1)


def put(work, start, size, value, stride=None):
    for h in range(2):
        work[h, pl.ds(start, size, stride), :] = value[:, h * 128 : (h + 1) * 128]


def pack_kernel(meta, main, halo, out_core, out_far, work):
    row, col = meta[1], meta[2]
    first = 1 + row
    for r in range(ROWS):
        put(work, pl.multiple_of((first + r) * COLS, COLS), COLS, main[pl.ds(r * COLS, COLS), :].astype(F32))
    place = jnp.where(row == 0, ROWS + 1, 0)
    put(work, pl.multiple_of(place * COLS, COLS), 2 * COLS, halo[...].astype(F32))
    src = jnp.where(row == 0, 1, ROWS + 1)
    dst = jnp.where(row == 0, 0, ROWS + 2)
    edge = take(work, pl.multiple_of(src * COLS, COLS), COLS)
    put(work, pl.multiple_of(dst * COLS, COLS), COLS, edge)
    even = lax.rem(col, 2) == 0
    for i in range(2):
        left = take(work, i, PR, COLS)
        right = take(work, COLS - 2 + i, PR, COLS)
        out_core[pl.ds(i * PR, PR), :] = jnp.where(even, right, left).astype(BF)
        out_far[pl.ds(i * PR, PR), :] = jnp.where(even, left, right).astype(BF)


def shift_columns(work, x, rows):
    for r in range(rows):
        for kw in range(3):
            x[kw, pl.ds(r * COLS, COLS), :] = take(work, r * WIDE + 7 + kw, COLS).astype(BF)


def build_frame(meta, main, strips, work, edge, x, side):
    row, col = meta[1], meta[2]
    first = 1 + row
    for r in range(ROWS):
        v = rounded(silu(main[pl.ds(r * COLS, COLS), :].astype(F32)))
        put(work, pl.multiple_of((first + r) * WIDE + 8, 8), COLS, v)
    place = jnp.where(row == 0, ROWS + 1, 0)
    for r in range(2):
        v = rounded(silu(strips[pl.ds(r * COLS, COLS), :].astype(F32)))
        put(work, pl.multiple_of((place + r) * WIDE + 8, 8), COLS, v)
    src = jnp.where(row == 0, 1, ROWS + 1)
    dst = jnp.where(row == 0, 0, ROWS + 2)
    copied = take(work, pl.multiple_of(src * WIDE + 8, 8), COLS)
    put(work, pl.multiple_of(dst * WIDE + 8, 8), COLS, copied)
    even = lax.rem(col, 2) == 0
    west = take(work, 8, PR, WIDE)
    east = take(work, 8 + COLS - 1, PR, WIDE)
    for i in range(2):
        near = rounded(silu(strips[pl.ds(2 * COLS + i * PR, PR), :].astype(F32)))
        far = rounded(silu(strips[pl.ds(2 * COLS + (2 + i) * PR, PR), :].astype(F32)))
        left = jnp.where(col == 0, west, jnp.where(even, far, near))
        right = jnp.where(col == 3, east, jnp.where(even, near, far))
        put(work, 6 + i, PR, left, WIDE)
        put(work, 8 + COLS + i, PR, right, WIDE)
        edge[i, pl.ds(0, PR), :] = left
        edge[4 + i, pl.ds(0, PR), :] = right
    edge[2, pl.ds(0, PR), :] = west
    edge[3, pl.ds(0, PR), :] = east
    for c in range(6):
        edge[c, pl.ds(PR, 8), :] = jnp.zeros((8, CH), F32)
    shift_columns(work, x, PR)
    for kh in range(3):
        for s in range(2):
            for kw in range(3):
                side[kh, kw, pl.ds(s * SIDE, SIDE), :] = edge[3 * s + kw, pl.ds(kh, SIDE), :].astype(BF)


def first_taps(x, side, weight, acc, fresh):
    for kh in range(3):
        for kw in range(3):
            cells = jnp.concatenate([x[kw, pl.ds(kh * COLS, MAIN), :], side[kh, kw]], axis=0)
            part = jnp.dot(cells, weight[0, kh, kw], preferred_element_type=F32)
            if fresh and kh == 0 and kw == 0:
                acc[...] = part
            else:
                acc[...] += part


def second_taps(x, weight, acc, fresh):
    for kh in range(3):
        for kw in range(3):
            part = jnp.dot(
                x[kw, pl.ds(kh * COLS, ROWS * COLS), :],
                weight[0, kh, kw],
                preferred_element_type=F32,
            )
            if fresh and kh == 0 and kw == 0:
                acc[...] = part
            else:
                acc[...] += part


def build_hidden(meta, acc, bias, work, x):
    row, col = meta[1], meta[2]
    first = 1 - row
    b = bias[...]
    for r in range(HR):
        v = rounded(silu(acc[pl.ds(r * COLS, COLS), :] + b))
        put(work, pl.multiple_of((first + r) * WIDE + 8, 8), COLS, v)
    left = rounded(silu(acc[pl.ds(MAIN, HR), :] + b))
    right = rounded(silu(acc[pl.ds(MAIN + SIDE, HR), :] + b))
    for edge_row, start in ((0, 1), (1, 0)):

        @pl.when(row == edge_row)
        def _():
            west = take(work, start * WIDE + 8, HR, WIDE)
            east = take(work, start * WIDE + 8 + COLS - 1, HR, WIDE)
            put(work, start * WIDE + 7, HR, jnp.where(col == 0, west, left), WIDE)
            put(work, start * WIDE + 8 + COLS, HR, jnp.where(col == 3, east, right), WIDE)
            src = 1 if edge_row == 0 else HR - 1
            dst = 0 if edge_row == 0 else HR
            put(work, dst * WIDE, WIDE, take(work, src * WIDE, WIDE))

    shift_columns(work, x, HR + 1)


def kernel_own(meta, main, strips, w1c, h0, work, edge, x, side):
    build_frame(meta, main, strips, work, edge, x, side)
    first_taps(x, side, w1c, h0, True)


def kernel_one(meta, main, strips, w1b, w1c, h0_in, h0, h1, work, edge, x, side):
    build_frame(meta, main, strips, work, edge, x, side)
    h0[...] = h0_in[...]
    first_taps(x, side, w1b, h0, False)
    first_taps(x, side, w1c, h1, True)


def kernel_two(
    meta, main, strips, w1a, w1b, w1c, w2c, bias, h0_in, h1_in, h1, h2, total, work, edge, x, side, h0
):
    build_frame(meta, main, strips, work, edge, x, side)
    h0[...] = h0_in[...]
    first_taps(x, side, w1a, h0, False)
    h1[...] = h1_in[...]
    first_taps(x, side, w1b, h1, False)
    first_taps(x, side, w1c, h2, True)
    build_hidden(meta, h0, bias, work, x)
    second_taps(x, w2c, total, True)


def kernel_three(
    meta, main, strips, w1a, w1b, w2b, bias, h1_in, h2_in, total_in, h2, total, work, edge, x, side, h1
):
    build_frame(meta, main, strips, work, edge, x, side)
    h1[...] = h1_in[...]
    first_taps(x, side, w1a, h1, False)
    h2[...] = h2_in[...]
    first_taps(x, side, w1b, h2, False)
    build_hidden(meta, h1, bias, work, x)
    total[...] = total_in[...]
    second_taps(x, w2b, total, False)


def kernel_four(
    meta, main, strips, w1a, w2a, bias, bias2, h2_in, total_in, latent, out, work, edge, x, side, h2, total
):
    build_frame(meta, main, strips, work, edge, x, side)
    h2[...] = h2_in[...]
    first_taps(x, side, w1a, h2, False)
    build_hidden(meta, h2, bias, work, x)
    total[...] = total_in[...]
    second_taps(x, w2a, total, False)
    out[...] = (latent[...].astype(F32) + (total[...] + bias2[...])).astype(BF)


def whole(shape):
    return pl.BlockSpec(shape, lambda i: (0,) * len(shape), pipeline_mode=pl.Buffered(1))


def tap(kt):
    return pl.BlockSpec(
        (1, 3, 3, CH, CH), lambda i, kt=kt: (kt, 0, 0, 0, 0), pipeline_mode=pl.Buffered(1)
    )


SCRATCH = [
    pltpu.VMEM((2, PR * WIDE, 128), F32),
    pltpu.VMEM((6, PR + 8, CH), F32),
    pltpu.VMEM((3, PR * COLS, CH), BF),
    pltpu.VMEM((3, 3, 2 * SIDE, CH), BF),
]


def run(kernel, operands, taps, outs, scratch, flops, name):
    specs = [pl.BlockSpec(memory_space=pltpu.SMEM)]
    args = []
    for position, operand in enumerate(operands):
        if position:
            kt = taps.get(position)
            specs.append(whole(operand.shape) if kt is None else tap(kt))
        args.append(operand)
    moved = sum(a.size * a.dtype.itemsize for a in args if a.ndim == 2)
    return pl.pallas_call(
        kernel,
        grid=(1,),
        out_shape=outs,
        in_specs=specs,
        out_specs=jax.tree.map(lambda o: whole(o.shape), outs),
        scratch_shapes=scratch,
        compiler_params=pltpu.CompilerParams(vmem_limit_bytes=30 * 2**20),
        cost_estimate=pl.CostEstimate(flops=flops, bytes_accessed=moved, transcendentals=0),
        name=name,
    )(*args)


def local(latent, conv1_weight, conv1_bias, conv2_weight, conv2_bias):
    count = lax.axis_size("tm")
    t = lax.axis_index("tm").astype(jnp.int32)
    row = lax.axis_index("row").astype(jnp.int32)
    col = lax.axis_index("col").astype(jnp.int32)
    meta = jnp.stack([t, row, col])
    own = latent.reshape(ROWS * COLS, CH)
    bias1 = conv1_bias.reshape(1, CH)
    bias2 = conv2_bias.reshape(1, CH)

    ahead = functools.partial(lax.ppermute, axis_name="tm")
    next_frame = shifted(count, 1)
    main1 = ahead(own, perm=next_frame)
    half_way = ahead(own, perm=backward(count, 0, 2))

    to_row = jnp.where(row == 0, own[(ROWS - 2) * COLS :], own[: 2 * COLS])
    rows = lax.ppermute(to_row, "row", [(0, 1), (1, 0)])
    edge_shape = jax.ShapeDtypeStruct((2 * PR, CH), BF)
    to_core, to_far = run(
        pack_kernel, [meta, own, rows], {}, [edge_shape, edge_shape],
        [pltpu.VMEM((2, PR * COLS, 128), F32)], 1000000, "pack",
    )
    near = lax.ppermute(to_core, "col", [(0, 1), (1, 0), (2, 3), (3, 2)])
    far = lax.ppermute(to_far, "col", [(0, 3), (3, 0), (1, 2), (2, 1)])
    strips0 = jnp.concatenate([rows, near, far], axis=0)

    strips1 = ahead(strips0, perm=next_frame)
    strips4 = ahead(strips0, perm=shifted(count, 4))
    main2 = ahead(main1, perm=next_frame)
    strips2 = ahead(strips1, perm=next_frame)
    main4 = ahead(half_way, perm=backward(count, 2, 2))
    main3 = ahead(main2, perm=next_frame)
    strips3 = ahead(strips2, perm=next_frame)

    frames = [(own, strips0)]
    for steps, (m, s) in enumerate(
        ((main1, strips1), (main2, strips2), (main3, strips3), (main4, strips4)), 1
    ):
        m0, s0 = frames[-1]
        frames.append((jnp.where(t >= steps, m, m0), jnp.where(t >= steps, s, s0)))

    hid = jax.ShapeDtypeStruct((ACC, CH), F32)
    tot = jax.ShapeDtypeStruct((ROWS * COLS, CH), F32)
    hid_s = pltpu.VMEM((ACC, CH), F32)
    tot_s = pltpu.VMEM((ROWS * COLS, CH), F32)
    unit = 2 * 9 * ACC * CH * CH
    w1, w2 = conv1_weight, conv2_weight

    h0 = run(kernel_own, [meta, *frames[0], w1], {3: 2}, hid, SCRATCH, unit, "own")
    h0, h1 = run(
        kernel_one, [meta, *frames[1], w1, w1, h0], {3: 1, 4: 2}, [hid, hid], SCRATCH, 2 * unit, "one"
    )
    h1, h2, total = run(
        kernel_two, [meta, *frames[2], w1, w1, w1, w2, bias1, h0, h1],
        {3: 0, 4: 1, 5: 2, 6: 2}, [hid, hid, tot], SCRATCH + [hid_s], 4 * unit, "two",
    )
    h2, total = run(
        kernel_three, [meta, *frames[3], w1, w1, w2, bias1, h1, h2, total],
        {3: 0, 4: 1, 5: 1}, [hid, tot], SCRATCH + [hid_s], 3 * unit, "three",
    )
    out = run(
        kernel_four, [meta, *frames[4], w1, w2, bias1, bias2, h2, total, own],
        {3: 0, 4: 0}, jax.ShapeDtypeStruct((ROWS * COLS, CH), BF), SCRATCH + [hid_s, tot_s],
        2 * unit, "four",
    )
    return out.reshape(1, ROWS, COLS, CH)


def solution(mesh):
    in_specs = (P("tm", "row", "col", None), P(), P(), P(), P())
    out_specs = P("tm", "row", "col", None)
    return jax.shard_map(local, mesh=mesh, in_specs=in_specs, out_specs=out_specs, check_vma=False)
```

time: 135 us -> 83 us (0.61)
  the two profiles are of different devices: /device:TPU:6 before, /device:TPU:161 now
where the time goes in v1:
time: 83 us; the launch traced here: 82.7 us
  waiting for transfers between devices  34.6 us (42%)
  Pallas kernels  24.6 us (30%)
  starting transfers between devices  18.3 us (22%)
  local copies, waits for them, and re-layouts  4.01 us (5%)
  other arithmetic  1.03 us (1%)
    pallas_call x6, Pallas kernels, run(): pl.pallas_call(kernel, grid=(1,), out_shape=outs, in_specs=specs, out_spe...  24.6 us
    ppermute x1, waiting for transfers between devices, local(): strips4 = ahead(strips0, perm=shifted(count, 4))  20.9 us
    ppermute x1, waiting for transfers between devices, local(): strips1 = ahead(strips0, perm=next_frame)  9.59 us
    ppermute x1, starting transfers between devices, local(): strips4 = ahead(strips0, perm=shifted(count, 4))  5.38 us
    unnamed x16, local copies, waits for them, and re-layouts  4 us
    ppermute x1, starting transfers between devices, local(): half_way = ahead(own, perm=backward(count, 0, 2))  3.39 us
    ppermute x1, starting transfers between devices, local(): far = lax.ppermute(to_far, 'col', [(0, 3), (3, 0), (1, 2), (2, 1)])  2.73 us
    ppermute x1, waiting for transfers between devices, local(): far = lax.ppermute(to_far, 'col', [(0, 3), (3, 0), (1, 2), (2, 1)])  2.57 us
  transfers between devices with their start and end apart: 12, of which 4 were waited for; matrix products, arithmetic and copies ran while one was open for 1% of the time, Pallas kernels for 3%

profile of v1, /device:TPU:161, one launch (start us, length us, event | category | flops | bytes accessed | tf_op | source)
XLA Modules:
  0.0 82.7 jit_solution(11905829959417530313)
XLA Ops:
  0.0 0.7 collective-permute-start.2
  0.7 3.4 %collective-permute-start = (bf16[720,256]{1,0:T(8,128)(2,1)}, bf16[720,256]{1,0:T(8,128)(2,1)S(1)}, u32[]{:S(2)}, u32[]{:S(2)}) collective-permute-start(bf16[720,256]{1,0:T(8,128)(2,1)} %bitcast.11), channel_id=1, source_target_pairs={{0,48},{8,56},{16,64},{24,72},{32,80},{40,88},{48,96},{56,104},{64... | collective-permute-start | bytes 1105928 | tf_op jit(solution)/shard_map/ppermute | solution.py:274
  4.1 0.8 slice_select_fusion
  4.9 1.2 %collective-permute-start.5 = (bf16[32,256]{1,0:T(8,128)(2,1)S(1)}, bf16[32,256]{1,0:T(8,128)(2,1)S(1)}, u32[]{:S(2)}, u32[]{:S(2)}) collective-permute-start(bf16[32,256]{1,0:T(8,128)(2,1)S(1)} %bitcast.19), channel_id=1, source_target_pairs={{0,4},{4,0},{1,5},{5,1},{2,6},{6,2},{3,7},{7,3},{8,12},{12,8},{9,1... | collective-permute-start | bytes 49160 | tf_op jit(solution)/shard_map/ppermute | solution.py:277
  6.1 0.1 pad_add_fusion.meta
  6.2 1.6 %collective-permute-done.5.halo = bf16[32,256]{1,0:T(8,128)(2,1)S(1)} collective-permute-done((bf16[32,256]{1,0:T(8,128)(2,1)S(1)}, bf16[32,256]{1,0:T(8,128)(2,1)S(1)}, u32[]{:S(2)}, u32[]{:S(2)}) %collective-permute-start.5) | collective-permute-done | bytes 16416 | tf_op jit(solution)/shard_map/ppermute | solution.py:277
  7.8 0.0 copy-start.3
  7.8 1.0 %copy-done.3 = bf16[1,45,16,256]{3,2,1,0:T(8,128)(2,1)S(1)} copy-done((bf16[1,45,16,256]{3,2,1,0:T(8,128)(2,1)S(1)}, bf16[1,45,16,256]{3,2,1,0:T(8,128)(2,1)}, u32[]{:S(2)}) %copy-start.3) | copy-done | bytes 368664
  8.8 0.7 pack.1
  9.4 2.2 %collective-permute-start.6 = (bf16[96,256]{1,0:T(8,128)(2,1)S(1)}, bf16[96,256]{1,0:T(8,128)(2,1)S(1)}, u32[]{:S(2)}, u32[]{:S(2)}) collective-permute-start(bf16[96,256]{1,0:T(8,128)(2,1)S(1)} %get-tuple-element.14), channel_id=1, source_target_pairs={{0,1},{1,0},{2,3},{3,2},{4,5},{5,4},{6,7},{7,6},{8,9},{9,8},{10,11... | collective-permute-start | bytes 147464 | tf_op jit(solution)/shard_map/ppermute | solution.py:283
  11.6 2.7 %collective-permute-start.7 = (bf16[96,256]{1,0:T(8,128)(2,1)S(1)}, bf16[96,256]{1,0:T(8,128)(2,1)S(1)}, u32[]{:S(2)}, u32[]{:S(2)}) collective-permute-start(bf16[96,256]{1,0:T(8,128)(2,1)S(1)} %get-tuple-element.15), channel_id=1, source_target_pairs={{0,3},{3,0},{1,2},{2,1},{4,7},{7,4},{5,6},{6,5},{8,11},{11,8},{9,1... | collective-permute-start | bytes 147464 | tf_op jit(solution)/shard_map/ppermute | solution.py:284
  14.3 0.0 collective-permute-done.2
  14.3 0.0 collective-permute-start.3
  14.3 0.0 collective-permute-done.6
  14.4 2.6 %collective-permute-done.7 = bf16[96,256]{1,0:T(8,128)(2,1)S(1)} collective-permute-done((bf16[96,256]{1,0:T(8,128)(2,1)S(1)}, bf16[96,256]{1,0:T(8,128)(2,1)S(1)}, u32[]{:S(2)}, u32[]{:S(2)}) %collective-permute-start.7) | collective-permute-done | bytes 49184 | tf_op jit(solution)/shard_map/ppermute | solution.py:284
  16.9 0.0 collective-permute-start.9
  16.9 9.6 %collective-permute-done.9 = bf16[224,256]{1,0:T(8,128)(2,1)S(1)} collective-permute-done((bf16[224,256]{1,0:T(8,128)(2,1)S(1)}, bf16[224,256]{1,0:T(8,128)(2,1)S(1)}, u32[]{:S(2)}, u32[]{:S(2)}) %collective-permute-start.9) | collective-permute-done | bytes 114720 | tf_op jit(solution)/shard_map/ppermute | solution.py:287
  26.5 0.3 collective-permute-start.10
  26.9 0.0 collective-permute-done
  26.9 1.9 %collective-permute-start.1 = (bf16[720,256]{1,0:T(8,128)(2,1)S(1)}, bf16[720,256]{1,0:T(8,128)(2,1)S(1)}, u32[]{:S(2)}, u32[]{:S(2)}) collective-permute-start(bf16[720,256]{1,0:T(8,128)(2,1)S(1)} %collective-permute-done), channel_id=1, source_target_pairs={{48,32},{56,40},{64,48},{72,56},{80,64},{88,72},{96,80},{104,88},{... | collective-permute-start | bytes 1105928 | tf_op jit(solution)/shard_map/ppermute | solution.py:291
  28.8 0.0 collective-permute-done.3
  28.8 0.4 collective-permute-start.4
  29.2 5.4 %collective-permute-start.8 = (bf16[224,256]{1,0:T(8,128)(2,1)S(1)}, bf16[224,256]{1,0:T(8,128)(2,1)S(1)}, u32[]{:S(2)}, u32[]{:S(2)}) collective-permute-start(bf16[224,256]{1,0:T(8,128)(2,1)S(1)} %constant_dynamic-update-slice_fusion.strips), channel_id=1, source_target_pairs={{0,32},{8,40},{16,48},{24,56},{32,64},{40,72},{48,80},{56,88},{64,... | collective-permute-start | bytes 344072 | tf_op jit(solution)/shard_map/ppermute | solution.py:288
  34.6 0.0 collective-permute-done.10
  34.6 0.0 collective-permute-start.11
  34.6 0.0 copy-start
  34.6 2.0 %copy-done = bf16[3,3,3,256,256]{4,3,2,1,0:T(8,128)(2,1)S(1)} copy-done((bf16[3,3,3,256,256]{4,3,2,1,0:T(8,128)(2,1)S(1)}, bf16[3,3,3,256,256]{4,3,2,1,0:T(8,128)(2,1)}, u32[]{:S(2)}) %copy-start) | copy-done | bytes 3538968
  36.6 0.0 copy-start.4
  36.6 1.0 %copy-done.4 = bf16[1,45,16,256]{3,2,1,0:T(8,128)(2,1)S(1)} copy-done((bf16[1,45,16,256]{3,2,1,0:T(8,128)(2,1)S(1)}, bf16[1,45,16,256]{3,2,1,0:T(8,128)(2,1)}, u32[]{:S(2)}) %copy-start.4) | copy-done | bytes 368664
  37.6 0.0 copy-start.1
  37.6 2.2 %own.1.h0_in = f32[832,256]{1,0:T(8,128)S(1)} custom-call(s32[3]{0:T(128)S(1)} %pad_add_fusion.meta, bf16[720,256]{1,0:T(8,128)(2,1)S(1)} %bitcast.13, bf16[224,256]{1,0:T(8,128)(2,1)S(1)} %constant_dynamic-update-slice_fusion.strips, bf16[3,3,3,256,256]{4,3,2,1,0:T(8,128)(2,1)S(1)} %copy-done), custom_call_target="tpu_custom_call" | custom-call | flops 981467136 | bytes 483328 | tf_op jit(solution)/shard_map/own/pallas_call | solution.py:248
  39.7 20.9 %collective-permute-done.8 = bf16[224,256]{1,0:T(8,128)(2,1)S(1)} collective-permute-done((bf16[224,256]{1,0:T(8,128)(2,1)S(1)}, bf16[224,256]{1,0:T(8,128)(2,1)S(1)}, u32[]{:S(2)}, u32[]{:S(2)}) %collective-permute-start.8) | collective-permute-done | bytes 114720 | tf_op jit(solution)/shard_map/ppermute | solution.py:288
  60.6 0.0 collective-permute-done.11
  60.6 0.0 collective-permute-done.1
  60.7 0.0 collective-permute-done.4
  60.7 0.2 broadcast_select_fusion.3
  60.8 0.0 copy-done.1
  60.8 0.0 copy-start.2
  60.8 0.0 copy-start.5
  60.9 3.1 %one.1 = (f32[832,256]{1,0:T(8,128)S(1)}, f32[832,256]{1,0:T(8,128)S(1)}) custom-call(s32[3]{0:T(128)S(1)} %pad_add_fusion.meta, bf16[720,256]{1,0:T(8,128)(2,1)S(1)} %get-tuple-element.30.main, bf16[224,256]{1,0:T(8,128)(2,1)S(1)} %get-tuple-element.26.strips, bf16[3,3,3,256,256]{4,3,2,1,0:T(8,128)(2,1)S(1)} %copy-done.1, ...), custom_call_target="tpu_custom_call" | custom-call | flops 1962934272 | bytes 1335296 | tf_op jit(solution)/shard_map/one/pallas_call | solution.py:248
  64.0 0.0 copy-done.2
  64.0 0.0 copy-done.5
  64.0 7.1 %two.1 = (f32[832,256]{1,0:T(8,128)S(1)}, f32[832,256]{1,0:T(8,128)S(1)}, f32[720,256]{1,0:T(8,128)S(1)}) custom-call(s32[3]{0:T(128)S(1)} %pad_add_fusion.meta, bf16[720,256]{1,0:T(8,128)(2,1)S(1)} %get-tuple-element.29.main, bf16[224,256]{1,0:T(8,128)(2,1)S(1)} %get-tuple-element.25.strips, bf16[3,3,3,256,256]{4,3,2,1,0:T(8,128)(2,1)S(1)} %copy-done.1, ...), custom_call_target="tpu_custom_call" | custom-call | flops 3925868544 | bytes 2188288 | tf_op jit(solution)/shard_map/two/pallas_call | solution.py:248
  71.0 0.0 copy-start.6
  71.0 5.9 %three.1 = (f32[832,256]{1,0:T(8,128)S(1)}, f32[720,256]{1,0:T(8,128)S(1)}) custom-call(s32[3]{0:T(128)S(1)} %pad_add_fusion.meta, bf16[720,256]{1,0:T(8,128)(2,1)S(1)} %get-tuple-element.28.main, bf16[224,256]{1,0:T(8,128)(2,1)S(1)} %get-tuple-element.24.strips, bf16[3,3,3,256,256]{4,3,2,1,0:T(8,128)(2,1)S(1)} %copy-done.1, ...), custom_call_target="tpu_custom_call" | custom-call | flops 2944401408 | bytes 2925568 | tf_op jit(solution)/shard_map/three/pallas_call | solution.py:248
  76.9 0.0 copy-done.6
  76.9 5.8 %four.1 = bf16[720,256]{1,0:T(8,128)(2,1)} custom-call(s32[3]{0:T(128)S(1)} %pad_add_fusion.meta, bf16[720,256]{1,0:T(8,128)(2,1)S(1)} %get-tuple-element.27.main, bf16[224,256]{1,0:T(8,128)(2,1)S(1)} %get-tuple-element.23.strips, bf16[3,3,3,256,256]{4,3,2,1,0:T(8,128)(2,1)S(1)} %copy-done.1, bf16[3,3,3,256,256]{4,3,2,1,0:T(8,128)(2,1)S(1)} %copy-done.2, ...), custom_call_target="tpu_custom_call" | custom-call | flops 1962934272 | bytes 2443264 | tf_op jit(solution)/shard_map/four/pallas_call | solution.py:248
  (4 shorter events, 0.1 us)
Async XLA Ops:
  0.0 14.3 %collective-permute-start.2 = (bf16[720,256]{1,0:T(8,128)(2,1)}, bf16[720,256]{1,0:T(8,128)(2,1)S(1)}, u32[]{:S(2)}, u32[]{:S(2)}) collective-permute-start(bf16[720,256]{1,0:T(8,128)(2,1)} %bitcast.10), channel_id=1, source_target_pairs={{0,8},{8,16},{16,24},{24,32},{32,40},{40,48},{48,56},{56,64},{64,7... | collective-permute-start | bytes 1105928 | tf_op jit(solution)/shard_map/ppermute | solution.py:273
  0.7 26.1 %collective-permute-start = (bf16[720,256]{1,0:T(8,128)(2,1)}, bf16[720,256]{1,0:T(8,128)(2,1)S(1)}, u32[]{:S(2)}, u32[]{:S(2)}) collective-permute-start(bf16[720,256]{1,0:T(8,128)(2,1)} %bitcast.11), channel_id=1, source_target_pairs={{0,48},{8,56},{16,64},{24,72},{32,80},{40,88},{48,96},{56,104},{64... | collective-permute-start | bytes 1105928 | tf_op jit(solution)/shard_map/ppermute | solution.py:274
  4.9 2.9 %collective-permute-start.5 = (bf16[32,256]{1,0:T(8,128)(2,1)S(1)}, bf16[32,256]{1,0:T(8,128)(2,1)S(1)}, u32[]{:S(2)}, u32[]{:S(2)}) collective-permute-start(bf16[32,256]{1,0:T(8,128)(2,1)S(1)} %bitcast.19), channel_id=1, source_target_pairs={{0,4},{4,0},{1,5},{5,1},{2,6},{6,2},{3,7},{7,3},{8,12},{12,8},{9,1... | collective-permute-start | bytes 49160 | tf_op jit(solution)/shard_map/ppermute | solution.py:277
  7.8 1.0 %copy-start.3 = (bf16[1,45,16,256]{3,2,1,0:T(8,128)(2,1)S(1)}, bf16[1,45,16,256]{3,2,1,0:T(8,128)(2,1)}, u32[]{:S(2)}) copy-start(bf16[1,45,16,256]{3,2,1,0:T(8,128)(2,1)} %param.5) | copy-start | bytes 1105924
  9.4 4.9 %collective-permute-start.6 = (bf16[96,256]{1,0:T(8,128)(2,1)S(1)}, bf16[96,256]{1,0:T(8,128)(2,1)S(1)}, u32[]{:S(2)}, u32[]{:S(2)}) collective-permute-start(bf16[96,256]{1,0:T(8,128)(2,1)S(1)} %get-tuple-element.14), channel_id=1, source_target_pairs={{0,1},{1,0},{2,3},{3,2},{4,5},{5,4},{6,7},{7,6},{8,9},{9,8},{10,11... | collective-permute-start | bytes 147464 | tf_op jit(solution)/shard_map/ppermute | solution.py:283
  11.6 5.3 %collective-permute-start.7 = (bf16[96,256]{1,0:T(8,128)(2,1)S(1)}, bf16[96,256]{1,0:T(8,128)(2,1)S(1)}, u32[]{:S(2)}, u32[]{:S(2)}) collective-permute-start(bf16[96,256]{1,0:T(8,128)(2,1)S(1)} %get-tuple-element.15), channel_id=1, source_target_pairs={{0,3},{3,0},{1,2},{2,1},{4,7},{7,4},{5,6},{6,5},{8,11},{11,8},{9,1... | collective-permute-start | bytes 147464 | tf_op jit(solution)/shard_map/ppermute | solution.py:284
  14.3 14.4 %collective-permute-start.3 = (bf16[720,256]{1,0:T(8,128)(2,1)S(1)}, bf16[720,256]{1,0:T(8,128)(2,1)S(1)}, u32[]{:S(2)}, u32[]{:S(2)}) collective-permute-start(bf16[720,256]{1,0:T(8,128)(2,1)S(1)} %collective-permute-done.2), channel_id=1, source_target_pairs={{0,8},{8,16},{16,24},{24,32},{32,40},{40,48},{48,56},{56,64},{64,7... | collective-permute-start | bytes 1105928 | tf_op jit(solution)/shard_map/ppermute | solution.py:289
  16.9 9.6 %collective-permute-start.9 = (bf16[224,256]{1,0:T(8,128)(2,1)S(1)}, bf16[224,256]{1,0:T(8,128)(2,1)S(1)}, u32[]{:S(2)}, u32[]{:S(2)}) collective-permute-start(bf16[224,256]{1,0:T(8,128)(2,1)S(1)} %constant_dynamic-update-slice_fusion.strips), channel_id=1, source_target_pairs={{0,8},{8,16},{16,24},{24,32},{32,40},{40,48},{48,56},{56,64},{64,7... | collective-permute-start | bytes 344072 | tf_op jit(solution)/shard_map/ppermute | solution.py:287
  26.5 8.0 %collective-permute-start.10 = (bf16[224,256]{1,0:T(8,128)(2,1)S(1)}, bf16[224,256]{1,0:T(8,128)(2,1)S(1)}, u32[]{:S(2)}, u32[]{:S(2)}) collective-permute-start(bf16[224,256]{1,0:T(8,128)(2,1)S(1)} %collective-permute-done.9), channel_id=1, source_target_pairs={{0,8},{8,16},{16,24},{24,32},{32,40},{40,48},{48,56},{56,64},{64,7... | collective-permute-start | bytes 344072 | tf_op jit(solution)/shard_map/ppermute | solution.py:290
  26.9 33.8 %collective-permute-start.1 = (bf16[720,256]{1,0:T(8,128)(2,1)S(1)}, bf16[720,256]{1,0:T(8,128)(2,1)S(1)}, u32[]{:S(2)}, u32[]{:S(2)}) collective-permute-start(bf16[720,256]{1,0:T(8,128)(2,1)S(1)} %collective-permute-done), channel_id=1, source_target_pairs={{48,32},{56,40},{64,48},{72,56},{80,64},{88,72},{96,80},{104,88},{... | collective-permute-start | bytes 1105928 | tf_op jit(solution)/shard_map/ppermute | solution.py:291
  28.8 31.9 %collective-permute-start.4 = (bf16[720,256]{1,0:T(8,128)(2,1)S(1)}, bf16[720,256]{1,0:T(8,128)(2,1)S(1)}, u32[]{:S(2)}, u32[]{:S(2)}) collective-permute-start(bf16[720,256]{1,0:T(8,128)(2,1)S(1)} %collective-permute-done.3), channel_id=1, source_target_pairs={{0,8},{8,16},{16,24},{24,32},{32,40},{40,48},{48,56},{56,64},{64,7... | collective-permute-start | bytes 1105928 | tf_op jit(solution)/shard_map/ppermute | solution.py:292
  29.2 31.4 %collective-permute-start.8 = (bf16[224,256]{1,0:T(8,128)(2,1)S(1)}, bf16[224,256]{1,0:T(8,128)(2,1)S(1)}, u32[]{:S(2)}, u32[]{:S(2)}) collective-permute-start(bf16[224,256]{1,0:T(8,128)(2,1)S(1)} %constant_dynamic-update-slice_fusion.strips), channel_id=1, source_target_pairs={{0,32},{8,40},{16,48},{24,56},{32,64},{40,72},{48,80},{56,88},{64,... | collective-permute-start | bytes 344072 | tf_op jit(solution)/shard_map/ppermute | solution.py:288
  34.6 26.0 %collective-permute-start.11 = (bf16[224,256]{1,0:T(8,128)(2,1)S(1)}, bf16[224,256]{1,0:T(8,128)(2,1)S(1)}, u32[]{:S(2)}, u32[]{:S(2)}) collective-permute-start(bf16[224,256]{1,0:T(8,128)(2,1)S(1)} %collective-permute-done.10), channel_id=1, source_target_pairs={{0,8},{8,16},{16,24},{24,32},{32,40},{40,48},{48,56},{56,64},{64,7... | collective-permute-start | bytes 344072 | tf_op jit(solution)/shard_map/ppermute | solution.py:293
  34.6 2.0 %copy-start = (bf16[3,3,3,256,256]{4,3,2,1,0:T(8,128)(2,1)S(1)}, bf16[3,3,3,256,256]{4,3,2,1,0:T(8,128)(2,1)}, u32[]{:S(2)}) copy-start(bf16[3,3,3,256,256]{4,3,2,1,0:T(8,128)(2,1)} %w1a.5) | copy-start | bytes 10616836
  36.6 1.0 %copy-start.4 = (bf16[1,45,16,256]{3,2,1,0:T(8,128)(2,1)S(1)}, bf16[1,45,16,256]{3,2,1,0:T(8,128)(2,1)}, u32[]{:S(2)}) copy-start(bf16[1,45,16,256]{3,2,1,0:T(8,128)(2,1)} %param.5) | copy-start | bytes 1105924
  37.6 23.3 %copy-start.1 = (bf16[3,3,3,256,256]{4,3,2,1,0:T(8,128)(2,1)S(1)}, bf16[3,3,3,256,256]{4,3,2,1,0:T(8,128)(2,1)}, u32[]{:S(2)}) copy-start(bf16[3,3,3,256,256]{4,3,2,1,0:T(8,128)(2,1)} %w1a.5) | copy-start | bytes 10616836
  60.8 3.1 %copy-start.2 = (bf16[3,3,3,256,256]{4,3,2,1,0:T(8,128)(2,1)S(1)}, bf16[3,3,3,256,256]{4,3,2,1,0:T(8,128)(2,1)}, u32[]{:S(2)}) copy-start(bf16[3,3,3,256,256]{4,3,2,1,0:T(8,128)(2,1)} %w2a.1) | copy-start | bytes 10616836
  60.8 3.1 %copy-start.5 = (f32[256]{0:T(256)S(1)}, f32[256]{0:T(256)}, u32[]{:S(2)}) copy-start(f32[256]{0:T(256)} %param.7) | copy-start | bytes 3076
  71.0 5.9 %copy-start.6 = (f32[256]{0:T(256)S(1)}, f32[256]{0:T(256)}, u32[]{:S(2)}) copy-start(f32[256]{0:T(256)} %param.9) | copy-start | bytes 3076

commit v2 on v1

v2 whole, which is shorter than its diff:
```python
import functools

import jax
import jax.numpy as jnp
from jax import lax
from jax.experimental import pallas as pl
from jax.experimental.pallas import tpu as pltpu
from jax.sharding import PartitionSpec as P

RING = 8
CH = 256
ROWS, COLS = 45, 16
LIMIT = 30 * 2**20
COST = (1000000000, 2000000000, 4000000000, 3000000000, 2000000000)
FORTH = (45,)
BACK = (45,)
HALF = 2
WIDE = 32
PR = ROWS + 3
HR = ROWS + 1
MAIN = HR * COLS
SIDE = PR
ACC = MAIN + 2 * SIDE
BF, F32 = jnp.bfloat16, jnp.float32


def shifted(count, steps):
    return [(i, (i + steps) % count) for i in range(count)]


def backward_place(source, steps, count):
    block, place = divmod(source, RING)
    if place >= steps:
        return ((block + 1) * RING + place - steps) % count
    return block * RING + place + RING - steps


def backward(count, done, steps):
    return [
        (
            backward_place(i, done, count) if done else i,
            backward_place(i, done + steps, count),
        )
        for i in range(count)
    ]


def silu(v):
    return (0.5 * v) * (1.0 + jnp.tanh(0.5 * v))


def rounded(v):
    return v.astype(BF).astype(F32)


def take(work, start, size, stride=None):
    return jnp.concatenate([work[h, pl.ds(start, size, stride), :] for h in range(2)], axis=1)


def put(work, start, size, value, stride=None):
    for h in range(2):
        work[h, pl.ds(start, size, stride), :] = value[:, h * 128 : (h + 1) * 128]


def pack_kernel(meta, main, halo, out_core, out_far, work):
    row, col = meta[1], meta[2]
    first = 1 + row
    for r in range(ROWS):
        put(work, pl.multiple_of((first + r) * COLS, COLS), COLS, main[pl.ds(r * COLS, COLS), :].astype(F32))
    place = jnp.where(row == 0, ROWS + 1, 0)
    put(work, pl.multiple_of(place * COLS, COLS), 2 * COLS, halo[...].astype(F32))
    src = jnp.where(row == 0, 1, ROWS + 1)
    dst = jnp.where(row == 0, 0, ROWS + 2)
    edge = take(work, pl.multiple_of(src * COLS, COLS), COLS)
    put(work, pl.multiple_of(dst * COLS, COLS), COLS, edge)
    even = lax.rem(col, 2) == 0
    for i in range(2):
        left = take(work, i, PR, COLS)
        right = take(work, COLS - 2 + i, PR, COLS)
        out_core[pl.ds(i * PR, PR), :] = jnp.where(even, right, left).astype(BF)
        out_far[pl.ds(i * PR, PR), :] = jnp.where(even, left, right).astype(BF)


def shift_columns(work, x, rows):
    for r in range(rows):
        for kw in range(3):
            x[kw, pl.ds(r * COLS, COLS), :] = take(work, r * WIDE + 7 + kw, COLS).astype(BF)


def build_frame(meta, main, strips, work, edge, x, side):
    row, col = meta[1], meta[2]
    first = 1 + row
    for r in range(ROWS):
        v = rounded(silu(main[pl.ds(r * COLS, COLS), :].astype(F32)))
        put(work, pl.multiple_of((first + r) * WIDE + 8, 8), COLS, v)
    place = jnp.where(row == 0, ROWS + 1, 0)
    for r in range(2):
        v = rounded(silu(strips[pl.ds(r * COLS, COLS), :].astype(F32)))
        put(work, pl.multiple_of((place + r) * WIDE + 8, 8), COLS, v)
    src = jnp.where(row == 0, 1, ROWS + 1)
    dst = jnp.where(row == 0, 0, ROWS + 2)
    copied = take(work, pl.multiple_of(src * WIDE + 8, 8), COLS)
    put(work, pl.multiple_of(dst * WIDE + 8, 8), COLS, copied)
    even = lax.rem(col, 2) == 0
    west = take(work, 8, PR, WIDE)
    east = take(work, 8 + COLS - 1, PR, WIDE)
    for i in range(2):
        near = rounded(silu(strips[pl.ds(2 * COLS + i * PR, PR), :].astype(F32)))
        far = rounded(silu(strips[pl.ds(2 * COLS + (2 + i) * PR, PR), :].astype(F32)))
        left = jnp.where(col == 0, west, jnp.where(even, far, near))
        right = jnp.where(col == 3, east, jnp.where(even, near, far))
        put(work, 6 + i, PR, left, WIDE)
        put(work, 8 + COLS + i, PR, right, WIDE)
        edge[i, pl.ds(0, PR), :] = left
        edge[4 + i, pl.ds(0, PR), :] = right
    edge[2, pl.ds(0, PR), :] = west
    edge[3, pl.ds(0, PR), :] = east
    for c in range(6):
        edge[c, pl.ds(PR, 8), :] = jnp.zeros((8, CH), F32)
    shift_columns(work, x, PR)
    for kh in range(3):
        for s in range(2):
            for kw in range(3):
                side[kh, kw, pl.ds(s * SIDE, SIDE), :] = edge[3 * s + kw, pl.ds(kh, SIDE), :].astype(BF)


def first_taps(x, side, weight, carried, out):
    cells = jnp.concatenate(
        [
            jnp.concatenate([x[kw, pl.ds(kh * COLS, MAIN), :], side[kh, kw]], axis=0)
            for kh in range(3)
            for kw in range(3)
        ],
        axis=1,
    )
    part = jnp.dot(cells, weight.reshape(9 * CH, CH), preferred_element_type=F32)
    out[...] = part if carried is None else carried[...] + part


def second_taps(x, weight):
    cells = jnp.concatenate(
        [x[kw, pl.ds(kh * COLS, ROWS * COLS), :] for kh in range(3) for kw in range(3)], axis=1
    )
    return jnp.dot(cells, weight.reshape(9 * CH, CH), preferred_element_type=F32)


def build_hidden(meta, acc, bias, work, x):
    row, col = meta[1], meta[2]
    first = 1 - row
    b = bias
    for r in range(HR):
        v = rounded(silu(acc[pl.ds(r * COLS, COLS), :] + b))
        put(work, pl.multiple_of((first + r) * WIDE + 8, 8), COLS, v)
    left = rounded(silu(acc[pl.ds(MAIN, HR), :] + b))
    right = rounded(silu(acc[pl.ds(MAIN + SIDE, HR), :] + b))
    for edge_row, start in ((0, 1), (1, 0)):

        @pl.when(row == edge_row)
        def _():
            west = take(work, start * WIDE + 8, HR, WIDE)
            east = take(work, start * WIDE + 8 + COLS - 1, HR, WIDE)
            put(work, start * WIDE + 7, HR, jnp.where(col == 0, west, left), WIDE)
            put(work, start * WIDE + 8 + COLS, HR, jnp.where(col == 3, east, right), WIDE)
            src = 1 if edge_row == 0 else HR - 1
            dst = 0 if edge_row == 0 else HR
            put(work, dst * WIDE, WIDE, take(work, src * WIDE, WIDE))

    shift_columns(work, x, HR + 1)


def step_kernel(steps, plan, *refs):
    refs = list(refs)
    pop = lambda count: [refs.pop(0) for _ in range(count)]
    (meta,) = pop(1)
    mains = [pop(count) for count in plan["parts"]]
    strips = [pop(1)[0] if apart else None for apart in plan["apart"]]
    (w1,) = pop(1)
    w2, biases = pop(2) if plan["done"] is not None else (None, None)
    (latent,) = pop(1) if plan["last"] else (None,)
    sums_in = dict(zip(plan["carried"], pop(len(plan["carried"]))))
    total_in = pop(1)[0] if plan["total_in"] else None
    outs = pop(plan["outs"])
    main, strip, work, edge, x, side, ready = refs
    for k in range(steps + 1):

        @pl.when(meta[0] >= steps if k == steps else meta[0] == k)
        def _():
            at = 0
            for part in mains[k]:
                size = min(part.shape[0], ROWS * COLS - at)
                main[pl.ds(at, size), :] = part[pl.ds(0, size), :]
                at += size
            if strips[k] is None:
                strip[...] = part[pl.ds(size, strip.shape[0]), :]
            else:
                strip[...] = strips[k][...]

    build_frame(meta, main, strip, work, edge, x, side)
    kept = [f for f in plan["frames"] if f != plan["done"]]
    for frame in plan["frames"][::-1]:
        out = ready if frame == plan["done"] else outs[kept.index(frame)]
        first_taps(x, side, w1[2 - (steps - frame)], sums_in.get(frame), out)
    if plan["done"] is not None:
        build_hidden(meta, ready, biases[0:1], work, x)
        total = second_taps(x, w2[2 - plan["done"]])
        if total_in is not None:
            total = total_in[...] + total
        if plan["last"]:
            total = (latent[...].astype(F32) + (total + biases[1:2])).astype(BF)
        outs[-1][...] = total


SCRATCH = [
    pltpu.VMEM((ROWS * COLS, CH), BF),
    pltpu.VMEM((2 * COLS + 4 * PR, CH), BF),
    pltpu.VMEM((2, PR * WIDE, 128), F32),
    pltpu.VMEM((6, PR + 8, CH), F32),
    pltpu.VMEM((3, PR * COLS, CH), BF),
    pltpu.VMEM((3, 3, 2 * SIDE, CH), BF),
    pltpu.VMEM((ACC, CH), F32),
]
SMEM = pl.BlockSpec(memory_space=pltpu.SMEM)
VMEM = pl.BlockSpec(memory_space=pltpu.VMEM)


def step(steps, meta, frames, weights, latent, sums, total):
    frames_here = [f for f in range(3) if 0 <= steps - f <= 2]
    done = steps - 2 if steps >= 2 else None
    plan = {
        "frames": frames_here,
        "carried": [f for f in frames_here if f in sums],
        "done": done,
        "last": steps == 4,
        "total_in": total is not None,
    }
    hid = jax.ShapeDtypeStruct((ACC, CH), F32)
    tot = jax.ShapeDtypeStruct((ROWS * COLS, CH), F32)
    kept = [f for f in frames_here if f != done]
    out_shape = [hid] * len(kept)
    if steps == 4:
        out_shape = [jax.ShapeDtypeStruct((ROWS * COLS, CH), BF)]
    elif done is not None:
        out_shape = out_shape + [tot]
    plan["outs"] = len(out_shape)
    mains = [part for f in frames for part in f[0]]
    strips = [f[1] for f in frames if f[1] is not None]
    plan["apart"] = [f[1] is not None for f in frames]
    plan["parts"] = [len(f[0]) for f in frames]
    w1, w2, biases = weights
    args = [meta, *mains, *strips, w1]
    args += [w2, biases] if done is not None else []
    args += [latent] if steps == 4 else []
    args += [sums[f] for f in plan["carried"]] + ([total] if total is not None else [])
    specs = [SMEM] + [VMEM] * (len(args) - 1)
    outs = pl.pallas_call(
        functools.partial(step_kernel, steps, plan),
        out_shape=out_shape,
        in_specs=specs,
        out_specs=[VMEM] * len(out_shape),
        scratch_shapes=SCRATCH,
        compiler_params=pltpu.CompilerParams(vmem_limit_bytes=LIMIT),
        cost_estimate=pl.CostEstimate(
            flops=COST[steps],
            bytes_accessed=1000000,
            transcendentals=0,
        ),
        name="step" + str(steps),
    )(*args)
    if steps == 4:
        return outs[0]
    sums = {f: o for f, o in zip(kept, outs)}
    return sums, (outs[-1] if done is not None else None)


def tie(value, *first):
    return lax.optimization_barrier((value, *first))[0]


def join_kernel(*refs):
    *parts, out = refs
    at = 0
    for part in parts:
        out[pl.ds(at, part.shape[0]), :] = part[...]
        at += part.shape[0]


def join(*parts):
    return pl.pallas_call(
        join_kernel,
        out_shape=jax.ShapeDtypeStruct((sum(p.shape[0] for p in parts), CH), BF),
        in_specs=[VMEM] * len(parts),
        out_specs=VMEM,
        compiler_params=pltpu.CompilerParams(vmem_limit_bytes=LIMIT),
        cost_estimate=pl.CostEstimate(flops=1000000, bytes_accessed=800000, transcendentals=0),
        name="join",
    )(*parts)


def cut_kernel(meta, own, to_row, *parts):
    last = ROWS - 2
    to_row[...] = jnp.where(
        meta[1] == 0, own[pl.ds(last * COLS, 2 * COLS), :], own[pl.ds(0, 2 * COLS), :]
    )
    at = 0
    for part in parts:
        if at == ROWS * COLS:
            at = 0
        part[...] = own[pl.ds(at, part.shape[0]), :]
        at += part.shape[0]


def cut(meta, own, sizes):
    shapes = [jax.ShapeDtypeStruct((r * COLS, CH), BF) for r in (2, *sizes)]
    return pl.pallas_call(
        cut_kernel,
        out_shape=shapes,
        in_specs=[SMEM, VMEM],
        out_specs=[VMEM] * len(shapes),
        compiler_params=pltpu.CompilerParams(vmem_limit_bytes=LIMIT),
        cost_estimate=pl.CostEstimate(flops=1000000, bytes_accessed=800000, transcendentals=0),
        name="cut",
    )(meta, own)


def pack(meta, own, rows):
    edge = jax.ShapeDtypeStruct((2 * PR, CH), BF)
    return pl.pallas_call(
        pack_kernel,
        out_shape=[edge, edge],
        in_specs=[SMEM, VMEM, VMEM],
        out_specs=[VMEM, VMEM],
        scratch_shapes=[pltpu.VMEM((2, PR * COLS, 128), F32)],
        compiler_params=pltpu.CompilerParams(vmem_limit_bytes=LIMIT),
        cost_estimate=pl.CostEstimate(flops=1000000, bytes_accessed=800000, transcendentals=0),
        name="pack",
    )(meta, own, rows)


def local(latent, conv1_weight, conv1_bias, conv2_weight, conv2_bias):
    count = lax.axis_size("tm")
    t = lax.axis_index("tm").astype(jnp.int32)
    row = lax.axis_index("row").astype(jnp.int32)
    col = lax.axis_index("col").astype(jnp.int32)
    meta = jnp.stack([t, row, col])
    own = latent.reshape(ROWS * COLS, CH)
    biases = jnp.stack([conv1_bias, conv2_bias])

    ahead = functools.partial(lax.ppermute, axis_name="tm")
    next_frame = shifted(count, 1)
    to_row = jnp.where(row == 0, own[(ROWS - 2) * COLS :], own[: 2 * COLS])
    rows = lax.ppermute(to_row, "row", [(0, 1), (1, 0)])
    main1 = ahead(own, perm=next_frame)
    half_way = ahead(own, perm=backward(count, 0, HALF))
    to_core, to_far = pack(meta, own, rows)
    near = lax.ppermute(to_core, "col", [(0, 1), (1, 0), (2, 3), (3, 2)])
    far = lax.ppermute(to_far, "col", [(0, 3), (3, 0), (1, 2), (2, 1)])
    strips0 = join(rows, near, far)
    strips1 = ahead(strips0, perm=next_frame)
    strips2 = ahead(strips0, perm=shifted(count, 2))
    strips4 = ahead(strips0, perm=shifted(count, 4))

    main2 = ahead(tie(main1, strips0), perm=next_frame)
    main4 = ahead(half_way, perm=backward(count, HALF, 4 - HALF))
    weights = (conv1_weight, conv2_weight, biases)
    frames = [([own], strips0), ([main1], strips1)]
    sums, total = step(0, meta, frames[:1], weights, own, {}, None)
    main2 = tie(main2, sums[0])
    main3 = ahead(main2, perm=next_frame)
    strips3 = ahead(tie(strips2, sums[0]), perm=next_frame)
    sums, total = step(1, meta, frames, weights, own, sums, total)
    frames += [([main2], strips2), ([main3], strips3), ([main4], strips4)]
    sums, total = step(2, meta, frames[:3], weights, own, sums, total)
    sums, total = step(3, meta, frames[:4], weights, own, sums, total)
    out = step(4, meta, frames, weights, own, sums, total)
    return out.reshape(1, ROWS, COLS, CH)


def solution(mesh):
    in_specs = (P("tm", "row", "col", None), P(), P(), P(), P())
    out_specs = P("tm", "row", "col", None)
    return jax.shard_map(local, mesh=mesh, in_specs=in_specs, out_specs=out_specs, check_vma=False)
```

time: 83 us -> 68.8 us (0.83)
  the two profiles are of different devices: /device:TPU:161 before, /device:TPU:6 now
where the time goes in v2:
time: 68.8 us; the launch traced here: 68.5 us
  Pallas kernels  24.6 us (36%)
  starting transfers between devices  19.6 us (28%)
  waiting for transfers between devices  18.7 us (27%)
  local copies, waits for them, and re-layouts  3.98 us (6%)
  other arithmetic  1.54 us (2%)
    pallas_call x5, Pallas kernels, step(): pl.pallas_call(functools.partial(step_kernel, steps, plan), out_shape=out...  23.9 us
    ppermute x1, waiting for transfers between devices, local(): main3 = ahead(main2, perm=next_frame)  6.12 us
    ppermute x1, starting transfers between devices, local(): half_way = ahead(own, perm=backward(count, 0, HALF))  5.4 us
    ppermute x1, starting transfers between devices, local(): strips4 = ahead(strips0, perm=shifted(count, 4))  4.05 us
    unnamed x8, local copies, waits for them, and re-layouts  3.98 us
    ppermute x1, waiting for transfers between devices, local(): far = lax.ppermute(to_far, 'col', [(0, 3), (3, 0), (1, 2), (2, 1)])  3.58 us
    ppermute x1, waiting for transfers between devices, local(): main2 = ahead(tie(main1, strips0), perm=next_frame)  3.15 us
    ppermute x1, waiting for transfers between devices, local(): main1 = ahead(own, perm=next_frame)  2.99 us
  transfers between devices with their start and end apart: 12, of which 5 were waited for; matrix products, arithmetic and copies ran while one was open for 2% of the time, Pallas kernels for 27%

profile of v2, /device:TPU:6, one launch (start us, length us, event | category | flops | bytes accessed | tf_op | source)
XLA Modules:
  0.0 68.5 jit_solution(17909956757135200358)
XLA Ops:
  0.0 1.9 %collective-permute-start = (bf16[720,256]{1,0:T(8,128)(2,1)}, bf16[720,256]{1,0:T(8,128)(2,1)S(1)}, u32[]{:S(2)}, u32[]{:S(2)}) collective-permute-start(bf16[720,256]{1,0:T(8,128)(2,1)} %bitcast.8), channel_id=1, source_target_pairs={{0,8},{8,16},{16,24},{24,32},{32,40},{40,48},{48,56},{56,64},{64,7... | collective-permute-start | bytes 1105928 | tf_op jit(solution)/shard_map/ppermute | solution.py:352
  1.9 5.4 %collective-permute-start.6 = (bf16[720,256]{1,0:T(8,128)(2,1)}, bf16[720,256]{1,0:T(8,128)(2,1)S(1)}, u32[]{:S(2)}, u32[]{:S(2)}) collective-permute-start(bf16[720,256]{1,0:T(8,128)(2,1)} %bitcast.9), channel_id=1, source_target_pairs={{0,48},{8,56},{16,64},{24,72},{32,80},{40,88},{48,96},{56,104},{64... | collective-permute-start | bytes 1105928 | tf_op jit(solution)/shard_map/ppermute | solution.py:353
  7.3 0.8 %slice_select_fusion = bf16[1,2,16,256]{3,2,1,0:T(8,128)(2,1)S(1)} fusion(bf16[1,45,16,256]{3,2,1,0:T(8,128)(2,1)} %param.5, pred[]{:T(512)S(6)} %eq.3), kind=kLoop, calls=%fused_computation | loop fusion | flops 8192 | bytes 49153 | tf_op jit(solution)/shard_map/jit(_where)/select_n | solution.py:350
  8.1 0.8 %collective-permute-start.1 = (bf16[32,256]{1,0:T(8,128)(2,1)S(1)}, bf16[32,256]{1,0:T(8,128)(2,1)S(1)}, u32[]{:S(2)}, u32[]{:S(2)}) collective-permute-start(bf16[32,256]{1,0:T(8,128)(2,1)S(1)} %bitcast.17), channel_id=1, source_target_pairs={{0,4},{4,0},{1,5},{5,1},{2,6},{6,2},{3,7},{7,3},{8,12},{12,8},{9,1... | collective-permute-start | bytes 49160 | tf_op jit(solution)/shard_map/ppermute | solution.py:351
  8.9 0.1 pad_add_fusion.meta.refs_0_
  9.0 2.8 %collective-permute-done.1.halo.refs_0_ = bf16[32,256]{1,0:T(8,128)(2,1)S(1)} collective-permute-done((bf16[32,256]{1,0:T(8,128)(2,1)S(1)}, bf16[32,256]{1,0:T(8,128)(2,1)S(1)}, u32[]{:S(2)}, u32[]{:S(2)}) %collective-permute-start.1) | collective-permute-done | bytes 16416 | tf_op jit(solution)/shard_map/ppermute | solution.py:351
  11.8 0.0 copy-start.2
  11.8 1.0 %copy-done.2 = bf16[1,45,16,256]{3,2,1,0:T(8,128)(2,1)S(1)} copy-done((bf16[1,45,16,256]{3,2,1,0:T(8,128)(2,1)S(1)}, bf16[1,45,16,256]{3,2,1,0:T(8,128)(2,1)}, u32[]{:S(2)}) %copy-start.2) | copy-done | bytes 368664
  12.8 0.7 pack.1
  13.5 0.1 collective-permute-start.2
  13.6 1.5 %collective-permute-start.3 = (bf16[96,256]{1,0:T(8,128)(2,1)S(1)}, bf16[96,256]{1,0:T(8,128)(2,1)S(1)}, u32[]{:S(2)}, u32[]{:S(2)}) collective-permute-start(bf16[96,256]{1,0:T(8,128)(2,1)S(1)} %get-tuple-element.18), channel_id=1, source_target_pairs={{0,3},{3,0},{1,2},{2,1},{4,7},{7,4},{5,6},{6,5},{8,11},{11,8},{9,1... | collective-permute-start | bytes 147464 | tf_op jit(solution)/shard_map/ppermute | solution.py:356
  15.1 0.0 collective-permute-done.2.refs_1_
  15.1 3.6 %collective-permute-done.3.refs_2_ = bf16[96,256]{1,0:T(8,128)(2,1)S(1)} collective-permute-done((bf16[96,256]{1,0:T(8,128)(2,1)S(1)}, bf16[96,256]{1,0:T(8,128)(2,1)S(1)}, u32[]{:S(2)}, u32[]{:S(2)}) %collective-permute-start.3) | collective-permute-done | bytes 49184 | tf_op jit(solution)/shard_map/ppermute | solution.py:356
  18.7 0.1 collective-permute-start.8
  18.8 1.0 %collective-permute-start.9 = (bf16[224,256]{1,0:T(8,128)(2,1)S(1)}, bf16[224,256]{1,0:T(8,128)(2,1)S(1)}, u32[]{:S(2)}, u32[]{:S(2)}) collective-permute-start(bf16[224,256]{1,0:T(8,128)(2,1)S(1)} %join.1.refs_2_.refs_3_.refs_4_.refs_5_.refs_6_), channel_id=1, source_target_pairs={{0,16},{8,24},{16,32},{24,40},{32,48},{40,56},{48,64},{56,72},{64,... | collective-permute-start | bytes 344072 | tf_op jit(solution)/shard_map/ppermute | solution.py:359
  19.8 3.0 %collective-permute-done.refs_2_ = bf16[720,256]{1,0:T(8,128)(2,1)S(1)} collective-permute-done((bf16[720,256]{1,0:T(8,128)(2,1)}, bf16[720,256]{1,0:T(8,128)(2,1)S(1)}, u32[]{:S(2)}, u32[]{:S(2)}) %collective-permute-start) | collective-permute-done | bytes 368672 | tf_op jit(solution)/shard_map/ppermute | solution.py:352
  22.8 0.0 collective-permute-start.4
  22.8 0.7 %pad_maximum_fusion.refs_9_.refs_11_.refs_13_ = f32[2,256]{1,0:T(2,128)S(1)} fusion(f32[1,256]{1,0:T(1,128)} %bitcast.18, f32[1,256]{1,0:T(1,128)} %bitcast.19), kind=kLoop, calls=%fused_computation.1 | loop fusion | flops 512 | bytes 4096 | tf_op jit(solution)/shard_map/stack | solution.py:346
  23.5 4.1 %collective-permute-start.11 = (bf16[224,256]{1,0:T(8,128)(2,1)S(1)}, bf16[224,256]{1,0:T(8,128)(2,1)S(1)}, u32[]{:S(2)}, u32[]{:S(2)}) collective-permute-start(bf16[224,256]{1,0:T(8,128)(2,1)S(1)} %join.1.refs_2_.refs_3_.refs_4_.refs_5_.refs_6_), channel_id=1, source_target_pairs={{0,32},{8,40},{16,48},{24,56},{32,64},{40,72},{48,80},{56,88},{64,... | collective-permute-start | bytes 344072 | tf_op jit(solution)/shard_map/ppermute | solution.py:360
  27.5 0.0 copy-start
  27.6 2.0 %copy-done = bf16[3,3,3,256,256]{4,3,2,1,0:T(8,128)(2,1)S(1)} copy-done((bf16[3,3,3,256,256]{4,3,2,1,0:T(8,128)(2,1)S(1)}, bf16[3,3,3,256,256]{4,3,2,1,0:T(8,128)(2,1)}, u32[]{:S(2)}) %copy-start) | copy-done | bytes 3538968
  29.5 0.0 copy-start.3
  29.6 1.0 %copy-done.3 = bf16[1,45,16,256]{3,2,1,0:T(8,128)(2,1)S(1)} copy-done((bf16[1,45,16,256]{3,2,1,0:T(8,128)(2,1)S(1)}, bf16[1,45,16,256]{3,2,1,0:T(8,128)(2,1)}, u32[]{:S(2)}) %copy-start.3) | copy-done | bytes 368664
  30.5 2.1 %step0.1.refs_6_ = f32[832,256]{1,0:T(8,128)S(1)} custom-call(s32[3]{0:T(128)S(1)} %pad_add_fusion.meta.refs_0_, bf16[720,256]{1,0:T(8,128)(2,1)S(1)} %bitcast.11, bf16[224,256]{1,0:T(8,128)(2,1)S(1)} %join.1.refs_2_.refs_3_.refs_4_.refs_5_.refs_6_, bf16[3,3,3,256,256]{4,3,2,1,0:T(8,128)(2,1)S(1)} %copy-done), custom_call_target="tpu_custom_call" | custom-call | flops 1000000000 | bytes 1000000 | tf_op jit(solution)/shard_map/step0/pallas_call | solution.py:255
  32.7 0.0 copy-start.1
  32.7 0.0 collective-permute-done.9.refs_6_.refs_7_.refs_8_
  32.7 1.8 %collective-permute-start.10 = (bf16[224,256]{1,0:T(8,128)(2,1)S(1)}, bf16[224,256]{1,0:T(8,128)(2,1)S(1)}, u32[]{:S(2)}, u32[]{:S(2)}) collective-permute-start(bf16[224,256]{1,0:T(8,128)(2,1)S(1)} %collective-permute-done.9.refs_6_.refs_7_.refs_8_), channel_id=1, source_target_pairs={{0,8},{8,16},{16,24},{24,32},{32,40},{40,48},{48,56},{56,64},{64,7... | collective-permute-start | bytes 344072 | tf_op jit(solution)/shard_map/ppermute | solution.py:369
  34.5 0.0 collective-permute-done.6
  34.5 2.9 %collective-permute-start.7 = (bf16[720,256]{1,0:T(8,128)(2,1)S(1)}, bf16[720,256]{1,0:T(8,128)(2,1)S(1)}, u32[]{:S(2)}, u32[]{:S(2)}) collective-permute-start(bf16[720,256]{1,0:T(8,128)(2,1)S(1)} %collective-permute-done.6), channel_id=1, source_target_pairs={{48,32},{56,40},{64,48},{72,56},{80,64},{88,72},{96,80},{104,88},{... | collective-permute-start | bytes 1105928 | tf_op jit(solution)/shard_map/ppermute | solution.py:363
  37.4 0.0 collective-permute-done.8.refs_4_.refs_5_.refs_6_.refs_7_
  37.4 3.1 %step1.1 = (f32[832,256]{1,0:T(8,128)S(1)}, f32[832,256]{1,0:T(8,128)S(1)}) custom-call(s32[3]{0:T(128)S(1)} %pad_add_fusion.meta.refs_0_, bf16[720,256]{1,0:T(8,128)(2,1)S(1)} %bitcast.12, bf16[720,256]{1,0:T(8,128)(2,1)S(1)} %collective-permute-done.refs_2_, bf16[224,256]{1,0:T(8,128)(2,1)S(1)} %join.1.refs_2_.refs_3_.refs_4_.refs_5_.refs_6_, ...), custom_call_target="tpu_custom_call" | custom-call | flops 2000000000 | bytes 1000000 | tf_op jit(solution)/shard_map/step1/pallas_call | solution.py:255
  40.5 3.2 %collective-permute-done.4.refs_3_ = bf16[720,256]{1,0:T(8,128)(2,1)S(1)} collective-permute-done((bf16[720,256]{1,0:T(8,128)(2,1)S(1)}, bf16[720,256]{1,0:T(8,128)(2,1)S(1)}, u32[]{:S(2)}, u32[]{:S(2)}) %collective-permute-start.4) | collective-permute-done | bytes 368672 | tf_op jit(solution)/shard_map/ppermute | solution.py:362
  43.6 0.0 collective-permute-start.5
  43.6 0.0 copy-done.1
  43.6 7.2 %step2.1 = (f32[832,256]{1,0:T(8,128)S(1)}, f32[832,256]{1,0:T(8,128)S(1)}, f32[720,256]{1,0:T(8,128)S(1)}) custom-call(s32[3]{0:T(128)S(1)} %pad_add_fusion.meta.refs_0_, bf16[720,256]{1,0:T(8,128)(2,1)S(1)} %bitcast.13, bf16[720,256]{1,0:T(8,128)(2,1)S(1)} %collective-permute-done.refs_2_, bf16[720,256]{1,0:T(8,128)(2,1)S(1)} %collective-permute-done.4.refs_3_, ...), custom_call_target="tpu_custom_call" | custom-call | flops 4000000000 | bytes 1000000 | tf_op jit(solution)/shard_map/step2/pallas_call | solution.py:255
  50.9 0.0 collective-permute-done.10.refs_8_.refs_9_
  50.9 6.1 %collective-permute-done.5.refs_4_ = bf16[720,256]{1,0:T(8,128)(2,1)S(1)} collective-permute-done((bf16[720,256]{1,0:T(8,128)(2,1)S(1)}, bf16[720,256]{1,0:T(8,128)(2,1)S(1)}, u32[]{:S(2)}, u32[]{:S(2)}) %collective-permute-start.5) | collective-permute-done | bytes 368672 | tf_op jit(solution)/shard_map/ppermute | solution.py:368
  57.0 5.7 %step3.1 = (f32[832,256]{1,0:T(8,128)S(1)}, f32[720,256]{1,0:T(8,128)S(1)}) custom-call(s32[3]{0:T(128)S(1)} %pad_add_fusion.meta.refs_0_, bf16[720,256]{1,0:T(8,128)(2,1)S(1)} %bitcast.14, bf16[720,256]{1,0:T(8,128)(2,1)S(1)} %collective-permute-done.refs_2_, bf16[720,256]{1,0:T(8,128)(2,1)S(1)} %collective-permute-done.4.refs_3_, ...), custom_call_target="tpu_custom_call" | custom-call | flops 3000000000 | bytes 1000000 | tf_op jit(solution)/shard_map/step3/pallas_call | solution.py:255
  62.7 0.0 collective-permute-done.11.refs_10_
  62.7 0.0 collective-permute-done.7.refs_5_
  62.7 5.8 %step4.1 = bf16[720,256]{1,0:T(8,128)(2,1)} custom-call(s32[3]{0:T(128)S(1)} %pad_add_fusion.meta.refs_0_, bf16[720,256]{1,0:T(8,128)(2,1)S(1)} %bitcast.15, bf16[720,256]{1,0:T(8,128)(2,1)S(1)} %collective-permute-done.refs_2_, bf16[720,256]{1,0:T(8,128)(2,1)S(1)} %collective-permute-done.4.refs_3_, bf16[720,256]{1,0:T(8,128)(2,1)S(1)} %collective-permute-done.5.refs_4_, ...), custom_call_target="tpu_custom_call" | custom-call | flops 2000000000 | bytes 1000000 | tf_op jit(solution)/shard_map/step4/pallas_call | solution.py:255
  (1 shorter events, 0.0 us)
Async XLA Ops:
  0.0 22.8 %collective-permute-start = (bf16[720,256]{1,0:T(8,128)(2,1)}, bf16[720,256]{1,0:T(8,128)(2,1)S(1)}, u32[]{:S(2)}, u32[]{:S(2)}) collective-permute-start(bf16[720,256]{1,0:T(8,128)(2,1)} %bitcast.8), channel_id=1, source_target_pairs={{0,8},{8,16},{16,24},{24,32},{32,40},{40,48},{48,56},{56,64},{64,7... | collective-permute-start | bytes 1105928 | tf_op jit(solution)/shard_map/ppermute | solution.py:352
  1.9 32.6 %collective-permute-start.6 = (bf16[720,256]{1,0:T(8,128)(2,1)}, bf16[720,256]{1,0:T(8,128)(2,1)S(1)}, u32[]{:S(2)}, u32[]{:S(2)}) collective-permute-start(bf16[720,256]{1,0:T(8,128)(2,1)} %bitcast.9), channel_id=1, source_target_pairs={{0,48},{8,56},{16,64},{24,72},{32,80},{40,88},{48,96},{56,104},{64... | collective-permute-start | bytes 1105928 | tf_op jit(solution)/shard_map/ppermute | solution.py:353
  8.1 3.7 %collective-permute-start.1 = (bf16[32,256]{1,0:T(8,128)(2,1)S(1)}, bf16[32,256]{1,0:T(8,128)(2,1)S(1)}, u32[]{:S(2)}, u32[]{:S(2)}) collective-permute-start(bf16[32,256]{1,0:T(8,128)(2,1)S(1)} %bitcast.17), channel_id=1, source_target_pairs={{0,4},{4,0},{1,5},{5,1},{2,6},{6,2},{3,7},{7,3},{8,12},{12,8},{9,1... | collective-permute-start | bytes 49160 | tf_op jit(solution)/shard_map/ppermute | solution.py:351
  11.8 1.0 %copy-start.2 = (bf16[1,45,16,256]{3,2,1,0:T(8,128)(2,1)S(1)}, bf16[1,45,16,256]{3,2,1,0:T(8,128)(2,1)}, u32[]{:S(2)}) copy-start(bf16[1,45,16,256]{3,2,1,0:T(8,128)(2,1)} %param.5) | copy-start | bytes 1105924
  13.5 1.6 %collective-permute-start.2 = (bf16[96,256]{1,0:T(8,128)(2,1)S(1)}, bf16[96,256]{1,0:T(8,128)(2,1)S(1)}, u32[]{:S(2)}, u32[]{:S(2)}) collective-permute-start(bf16[96,256]{1,0:T(8,128)(2,1)S(1)} %get-tuple-element.17), channel_id=1, source_target_pairs={{0,1},{1,0},{2,3},{3,2},{4,5},{5,4},{6,7},{7,6},{8,9},{9,8},{10,11... | collective-permute-start | bytes 147464 | tf_op jit(solution)/shard_map/ppermute | solution.py:355
  13.6 5.1 %collective-permute-start.3 = (bf16[96,256]{1,0:T(8,128)(2,1)S(1)}, bf16[96,256]{1,0:T(8,128)(2,1)S(1)}, u32[]{:S(2)}, u32[]{:S(2)}) collective-permute-start(bf16[96,256]{1,0:T(8,128)(2,1)S(1)} %get-tuple-element.18), channel_id=1, source_target_pairs={{0,3},{3,0},{1,2},{2,1},{4,7},{7,4},{5,6},{6,5},{8,11},{11,8},{9,1... | collective-permute-start | bytes 147464 | tf_op jit(solution)/shard_map/ppermute | solution.py:356
  18.7 18.7 %collective-permute-start.8 = (bf16[224,256]{1,0:T(8,128)(2,1)S(1)}, bf16[224,256]{1,0:T(8,128)(2,1)S(1)}, u32[]{:S(2)}, u32[]{:S(2)}) collective-permute-start(bf16[224,256]{1,0:T(8,128)(2,1)S(1)} %join.1.refs_2_.refs_3_.refs_4_.refs_5_.refs_6_), channel_id=1, source_target_pairs={{0,8},{8,16},{16,24},{24,32},{32,40},{40,48},{48,56},{56,64},{64,7... | collective-permute-start | bytes 344072 | tf_op jit(solution)/shard_map/ppermute | solution.py:358
  18.8 13.9 %collective-permute-start.9 = (bf16[224,256]{1,0:T(8,128)(2,1)S(1)}, bf16[224,256]{1,0:T(8,128)(2,1)S(1)}, u32[]{:S(2)}, u32[]{:S(2)}) collective-permute-start(bf16[224,256]{1,0:T(8,128)(2,1)S(1)} %join.1.refs_2_.refs_3_.refs_4_.refs_5_.refs_6_), channel_id=1, source_target_pairs={{0,16},{8,24},{16,32},{24,40},{32,48},{40,56},{48,64},{56,72},{64,... | collective-permute-start | bytes 344072 | tf_op jit(solution)/shard_map/ppermute | solution.py:359
  22.8 20.8 %collective-permute-start.4 = (bf16[720,256]{1,0:T(8,128)(2,1)S(1)}, bf16[720,256]{1,0:T(8,128)(2,1)S(1)}, u32[]{:S(2)}, u32[]{:S(2)}) collective-permute-start(bf16[720,256]{1,0:T(8,128)(2,1)S(1)} %collective-permute-done.refs_2_), channel_id=1, source_target_pairs={{0,8},{8,16},{16,24},{24,32},{32,40},{40,48},{48,56},{56,64},{64,7... | collective-permute-start | bytes 1105928 | tf_op jit(solution)/shard_map/ppermute | solution.py:362
  23.5 39.2 %collective-permute-start.11 = (bf16[224,256]{1,0:T(8,128)(2,1)S(1)}, bf16[224,256]{1,0:T(8,128)(2,1)S(1)}, u32[]{:S(2)}, u32[]{:S(2)}) collective-permute-start(bf16[224,256]{1,0:T(8,128)(2,1)S(1)} %join.1.refs_2_.refs_3_.refs_4_.refs_5_.refs_6_), channel_id=1, source_target_pairs={{0,32},{8,40},{16,48},{24,56},{32,64},{40,72},{48,80},{56,88},{64,... | collective-permute-start | bytes 344072 | tf_op jit(solution)/shard_map/ppermute | solution.py:360
  27.5 2.0 %copy-start = (bf16[3,3,3,256,256]{4,3,2,1,0:T(8,128)(2,1)S(1)}, bf16[3,3,3,256,256]{4,3,2,1,0:T(8,128)(2,1)}, u32[]{:S(2)}) copy-start(bf16[3,3,3,256,256]{4,3,2,1,0:T(8,128)(2,1)} %refs_11_.1) | copy-start | bytes 10616836
  29.5 1.0 %copy-start.3 = (bf16[1,45,16,256]{3,2,1,0:T(8,128)(2,1)S(1)}, bf16[1,45,16,256]{3,2,1,0:T(8,128)(2,1)}, u32[]{:S(2)}) copy-start(bf16[1,45,16,256]{3,2,1,0:T(8,128)(2,1)} %param.5) | copy-start | bytes 1105924
  32.7 10.9 %copy-start.1 = (bf16[3,3,3,256,256]{4,3,2,1,0:T(8,128)(2,1)S(1)}, bf16[3,3,3,256,256]{4,3,2,1,0:T(8,128)(2,1)}, u32[]{:S(2)}) copy-start(bf16[3,3,3,256,256]{4,3,2,1,0:T(8,128)(2,1)} %refs_12_.1) | copy-start | bytes 10616836
  32.7 18.2 %collective-permute-start.10 = (bf16[224,256]{1,0:T(8,128)(2,1)S(1)}, bf16[224,256]{1,0:T(8,128)(2,1)S(1)}, u32[]{:S(2)}, u32[]{:S(2)}) collective-permute-start(bf16[224,256]{1,0:T(8,128)(2,1)S(1)} %collective-permute-done.9.refs_6_.refs_7_.refs_8_), channel_id=1, source_target_pairs={{0,8},{8,16},{16,24},{24,32},{32,40},{40,48},{48,56},{56,64},{64,7... | collective-permute-start | bytes 344072 | tf_op jit(solution)/shard_map/ppermute | solution.py:369
  34.5 28.2 %collective-permute-start.7 = (bf16[720,256]{1,0:T(8,128)(2,1)S(1)}, bf16[720,256]{1,0:T(8,128)(2,1)S(1)}, u32[]{:S(2)}, u32[]{:S(2)}) collective-permute-start(bf16[720,256]{1,0:T(8,128)(2,1)S(1)} %collective-permute-done.6), channel_id=1, source_target_pairs={{48,32},{56,40},{64,48},{72,56},{80,64},{88,72},{96,80},{104,88},{... | collective-permute-start | bytes 1105928 | tf_op jit(solution)/shard_map/ppermute | solution.py:363
  43.6 13.4 %collective-permute-start.5 = (bf16[720,256]{1,0:T(8,128)(2,1)S(1)}, bf16[720,256]{1,0:T(8,128)(2,1)S(1)}, u32[]{:S(2)}, u32[]{:S(2)}) collective-permute-start(bf16[720,256]{1,0:T(8,128)(2,1)S(1)} %collective-permute-done.4.refs_3_), channel_id=1, source_target_pairs={{0,8},{8,16},{16,24},{24,32},{32,40},{40,48},{48,56},{56,64},{64,7... | collective-permute-start | bytes 1105928 | tf_op jit(solution)/shard_map/ppermute | solution.py:368

commit v3 on v2

--- a/solution.py
+++ b/solution.py
@@ -30,17 +30,14 @@
 
 def backward_place(source, steps, count):
     block, place = divmod(source, RING)
-    if place >= steps:
-        return ((block + 1) * RING + place - steps) % count
-    return block * RING + place + RING - steps
+    early = 0 < steps < 4
+    moved = place in ((4, 5, 6) if early else (4, 5, 6, 7)) if steps else False
+    return ((block + moved) * RING + (place - steps) % RING) % count
 
 
 def backward(count, done, steps):
     return [
-        (
-            backward_place(i, done, count) if done else i,
-            backward_place(i, done + steps, count),
-        )
+        (backward_place(i, done, count), backward_place(i, done + steps, count))
         for i in range(count)
     ]
 
@@ -173,38 +170,56 @@
     pop = lambda count: [refs.pop(0) for _ in range(count)]
     (meta,) = pop(1)
     mains = [pop(count) for count in plan["parts"]]
-    strips = [pop(1)[0] if apart else None for apart in plan["apart"]]
+    strips = pop(steps + 1 - plan["late"])
     (w1,) = pop(1)
-    w2, biases = pop(2) if plan["done"] is not None else (None, None)
+    w2, biases = pop(2) if plan["done"] else (None, None)
     (latent,) = pop(1) if plan["last"] else (None,)
     sums_in = dict(zip(plan["carried"], pop(len(plan["carried"]))))
     total_in = pop(1)[0] if plan["total_in"] else None
     outs = pop(plan["outs"])
-    main, strip, work, edge, x, side, ready = refs
+    main, strip, work, edge, x, side, ready = refs[:7]
     for k in range(steps + 1):
+        if plan["late"] and k == steps - 1:
+            continue
+        source = k - (plan["late"] and k == steps)
 
         @pl.when(meta[0] >= steps if k == steps else meta[0] == k)
         def _():
-            at = 0
-            for part in mains[k]:
-                size = min(part.shape[0], ROWS * COLS - at)
-                main[pl.ds(at, size), :] = part[pl.ds(0, size), :]
-                at += size
-            if strips[k] is None:
-                strip[...] = part[pl.ds(size, strip.shape[0]), :]
+            main[...] = mains[source][0][...]
+            strip[...] = strips[source][...]
+
+    def add():
+        build_frame(meta, main, strip, work, edge, x, side)
+        kept = [f for f in plan["frames"] if f not in plan["done"]]
+        for frame in plan["frames"][::-1]:
+            if frame in plan["done"]:
+                out = ready.at[plan["done"].index(frame)]
             else:
-                strip[...] = strips[k][...]
-
-    build_frame(meta, main, strip, work, edge, x, side)
-    kept = [f for f in plan["frames"] if f != plan["done"]]
-    for frame in plan["frames"][::-1]:
-        out = ready if frame == plan["done"] else outs[kept.index(frame)]
-        first_taps(x, side, w1[2 - (steps - frame)], sums_in.get(frame), out)
-    if plan["done"] is not None:
-        build_hidden(meta, ready, biases[0:1], work, x)
-        total = second_taps(x, w2[2 - plan["done"]])
-        if total_in is not None:
-            total = total_in[...] + total
+                out = outs[kept.index(frame)]
+            first_taps(x, side, w1[2 - (steps - frame)], sums_in.get(frame), out)
+
+    if plan["late"]:
+        pl.when(meta[0] != steps - 1)(add)
+
+        @pl.when(meta[0] == steps - 1)
+        def _():
+            outs[0][...] = sums_in[plan["frames"][0]][...]
+
+    else:
+        add()
+    if plan["last"]:
+
+        @pl.when(meta[0] == steps)
+        def _():
+            first_taps(x, side, w1[0], ready.at[1], ready.at[1])
+
+    if plan["done"]:
+        total = 0.0 if total_in is None else total_in[...]
+        for i, frame in enumerate(plan["done"]):
+            room = (work, x) if i == 0 else refs[7:9]
+            build_hidden(meta, ready.at[i], biases[0:1], *room)
+        for i, frame in enumerate(plan["done"]):
+            total = total + second_taps(x if i == 0 else refs[8], w2[2 - frame])
         if plan["last"]:
             total = (latent[...].astype(F32) + (total + biases[1:2])).astype(BF)
         outs[-1][...] = total
@@ -217,47 +232,55 @@
     pltpu.VMEM((6, PR + 8, CH), F32),
     pltpu.VMEM((3, PR * COLS, CH), BF),
     pltpu.VMEM((3, 3, 2 * SIDE, CH), BF),
-    pltpu.VMEM((ACC, CH), F32),
+    pltpu.VMEM((2, ACC, CH), F32),
+]
+SECOND = [
+    pltpu.VMEM((2, PR * WIDE, 128), F32),
+    pltpu.VMEM((3, PR * COLS, CH), BF),
 ]
 SMEM = pl.BlockSpec(memory_space=pltpu.SMEM)
 VMEM = pl.BlockSpec(memory_space=pltpu.VMEM)
 
 
 def step(steps, meta, frames, weights, latent, sums, total):
+    late = steps == 4
+    last = steps == 3
     frames_here = [f for f in range(3) if 0 <= steps - f <= 2]
-    done = steps - 2 if steps >= 2 else None
+    done = {2: [0], 3: [1, 2]}.get(steps, [])
+    if late:
+        frames = frames[:3] + frames[4:]
     plan = {
         "frames": frames_here,
         "carried": [f for f in frames_here if f in sums],
         "done": done,
-        "last": steps == 4,
-        "total_in": total is not None,
+        "last": last,
+        "late": late,
+        "total_in": total is not None and not late,
     }
     hid = jax.ShapeDtypeStruct((ACC, CH), F32)
     tot = jax.ShapeDtypeStruct((ROWS * COLS, CH), F32)
-    kept = [f for f in frames_here if f != done]
+    kept = [f for f in frames_here if f not in done]
     out_shape = [hid] * len(kept)
-    if steps == 4:
+    if last:
         out_shape = [jax.ShapeDtypeStruct((ROWS * COLS, CH), BF)]
-    elif done is not None:
+    elif done:
         out_shape = out_shape + [tot]
     plan["outs"] = len(out_shape)
     mains = [part for f in frames for part in f[0]]
     strips = [f[1] for f in frames if f[1] is not None]
-    plan["apart"] = [f[1] is not None for f in frames]
     plan["parts"] = [len(f[0]) for f in frames]
     w1, w2, biases = weights
     args = [meta, *mains, *strips, w1]
-    args += [w2, biases] if done is not None else []
-    args += [latent] if steps == 4 else []
-    args += [sums[f] for f in plan["carried"]] + ([total] if total is not None else [])
+    args += [w2, biases] if done else []
+    args += [latent] if last else []
+    args += [sums[f] for f in plan["carried"]] + ([total] if plan["total_in"] else [])
     specs = [SMEM] + [VMEM] * (len(args) - 1)
     outs = pl.pallas_call(
         functools.partial(step_kernel, steps, plan),
         out_shape=out_shape,
         in_specs=specs,
         out_specs=[VMEM] * len(out_shape),
-        scratch_shapes=SCRATCH,
+        scratch_shapes=SCRATCH + (SECOND if last else []),
         compiler_params=pltpu.CompilerParams(vmem_limit_bytes=LIMIT),
         cost_estimate=pl.CostEstimate(
             flops=COST[steps],
@@ -266,10 +289,9 @@
         ),
         name="step" + str(steps),
     )(*args)
-    if steps == 4:
+    if last:
         return outs[0]
-    sums = {f: o for f, o in zip(kept, outs)}
-    return sums, (outs[-1] if done is not None else None)
+    return {**sums, **dict(zip(kept, outs))}, (outs[-1] if done else total)
 
 
 def tie(value, *first):
@@ -359,19 +381,19 @@
     strips2 = ahead(strips0, perm=shifted(count, 2))
     strips4 = ahead(strips0, perm=shifted(count, 4))
 
-    main2 = ahead(tie(main1, strips0), perm=next_frame)
+    main2 = ahead(tie(main1, to_core), perm=next_frame)
     main4 = ahead(half_way, perm=backward(count, HALF, 4 - HALF))
     weights = (conv1_weight, conv2_weight, biases)
     frames = [([own], strips0), ([main1], strips1)]
-    sums, total = step(0, meta, frames[:1], weights, own, {}, None)
+    sums, total = step(0, tie(meta, half_way), frames[:1], weights, own, {}, None)
     main2 = tie(main2, sums[0])
     main3 = ahead(main2, perm=next_frame)
     strips3 = ahead(tie(strips2, sums[0]), perm=next_frame)
     sums, total = step(1, meta, frames, weights, own, sums, total)
     frames += [([main2], strips2), ([main3], strips3), ([main4], strips4)]
     sums, total = step(2, meta, frames[:3], weights, own, sums, total)
-    sums, total = step(3, meta, frames[:4], weights, own, sums, total)
-    out = step(4, meta, frames, weights, own, sums, total)
+    sums, total = step(4, meta, frames, weights, own, sums, total)
+    out = step(3, meta, frames[:4], weights, own, sums, total)
     return out.reshape(1, ROWS, COLS, CH)
 
 

time: 68.8 us -> 63.2 us (0.919)
  waiting for transfers between devices: 18.7 us -> 14 us
  Pallas kernels: 24.6 us -> 22 us
  starting transfers between devices: 19.6 us -> 21.2 us
    ppermute x1, waiting for transfers between devices: 6.12 us -> 1.39 us  [local(): main3 = ahead(main2, perm=next_frame)]
    ppermute x1, waiting for transfers between devices: 3.15 us -> 6.22 us  [local(): main2 = ahead(tie(main1, to_core), perm=next_frame)]
    ppermute x1, waiting for transfers between devices: 2.99 us -> 0.01 us  [local(): main1 = ahead(own, perm=next_frame)]
    pallas_call x5, Pallas kernels: 23.9 us -> 21.3 us  [step(): pl.pallas_call(functools.partial(step_kernel, steps, plan), out_shape=out...]
    ppermute x1, starting transfers between devices: 0.01 us -> 2.55 us  [local(): main2 = ahead(tie(main1, to_core), perm=next_frame)]
    ppermute x1, starting transfers between devices: 2.87 us -> 1.58 us  [local(): main4 = ahead(half_way, perm=backward(count, HALF, 4 - HALF))]
  transfers between devices with their start and end apart: 12 -> 12, of which waited for: 5 -> 4; matrix products, arithmetic and copies ran while one was open for 2% -> 2% of each run, Pallas kernels for 27% -> 24%
where the time goes in v3:
time: 63.2 us; the launch traced here: 62.9 us
  Pallas kernels  22 us (35%)
  starting transfers between devices  21.2 us (34%)
  waiting for transfers between devices  14 us (22%)
  local copies, waits for them, and re-layouts  3.98 us (6%)
  other arithmetic  1.53 us (2%)
    pallas_call x5, Pallas kernels, step(): pl.pallas_call(functools.partial(step_kernel, steps, plan), out_shape=out...  21.3 us
    ppermute x1, waiting for transfers between devices, local(): main2 = ahead(tie(main1, to_core), perm=next_frame)  6.22 us
    ppermute x1, starting transfers between devices, local(): half_way = ahead(own, perm=backward(count, 0, HALF))  5.4 us
    ppermute x1, starting transfers between devices, local(): strips4 = ahead(strips0, perm=shifted(count, 4))  4.49 us
    unnamed x8, local copies, waits for them, and re-layouts  3.98 us
    ppermute x1, waiting for transfers between devices, local(): far = lax.ppermute(to_far, 'col', [(0, 3), (3, 0), (1, 2), (2, 1)])  3.58 us
    ppermute x1, waiting for transfers between devices, local(): rows = lax.ppermute(to_row, 'row', [(0, 1), (1, 0)])  2.83 us
    ppermute x1, starting transfers between devices, local(): main2 = ahead(tie(main1, to_core), perm=next_frame)  2.55 us
  transfers between devices with their start and end apart: 12, of which 4 were waited for; matrix products, arithmetic and copies ran while one was open for 2% of the time, Pallas kernels for 24%

profile of v3, /device:TPU:6, one launch (start us, length us, event | category | flops | bytes accessed | tf_op | source)
XLA Modules:
  0.0 62.9 jit_solution(2068033035083685164)
XLA Ops:
  0.0 1.9 %collective-permute-start = (bf16[720,256]{1,0:T(8,128)(2,1)}, bf16[720,256]{1,0:T(8,128)(2,1)S(1)}, u32[]{:S(2)}, u32[]{:S(2)}) collective-permute-start(bf16[720,256]{1,0:T(8,128)(2,1)} %bitcast.8), channel_id=1, source_target_pairs={{0,8},{8,16},{16,24},{24,32},{32,40},{40,48},{48,56},{56,64},{64,7... | collective-permute-start | bytes 1105928 | tf_op jit(solution)/shard_map/ppermute | solution.py:374
  1.9 5.4 %collective-permute-start.3 = (bf16[720,256]{1,0:T(8,128)(2,1)}, bf16[720,256]{1,0:T(8,128)(2,1)S(1)}, u32[]{:S(2)}, u32[]{:S(2)}) collective-permute-start(bf16[720,256]{1,0:T(8,128)(2,1)} %bitcast.9), channel_id=1, source_target_pairs={{0,48},{8,56},{16,0},{24,8},{32,80},{40,88},{48,96},{56,40},{64,11... | collective-permute-start | bytes 1105928 | tf_op jit(solution)/shard_map/ppermute | solution.py:375
  7.3 0.8 %slice_select_fusion = bf16[1,2,16,256]{3,2,1,0:T(8,128)(2,1)S(1)} fusion(bf16[1,45,16,256]{3,2,1,0:T(8,128)(2,1)} %param.5, pred[]{:T(512)S(6)} %eq.3), kind=kLoop, calls=%fused_computation | loop fusion | flops 8192 | bytes 49153 | tf_op jit(solution)/shard_map/jit(_where)/select_n | solution.py:372
  8.1 0.8 %collective-permute-start.1 = (bf16[32,256]{1,0:T(8,128)(2,1)S(1)}, bf16[32,256]{1,0:T(8,128)(2,1)S(1)}, u32[]{:S(2)}, u32[]{:S(2)}) collective-permute-start(bf16[32,256]{1,0:T(8,128)(2,1)S(1)} %bitcast.17), channel_id=1, source_target_pairs={{0,4},{4,0},{1,5},{5,1},{2,6},{6,2},{3,7},{7,3},{8,12},{12,8},{9,1... | collective-permute-start | bytes 49160 | tf_op jit(solution)/shard_map/ppermute | solution.py:373
  8.9 0.1 pad_add_fusion.meta.refs_0_
  9.0 2.8 %collective-permute-done.1.halo.refs_0_ = bf16[32,256]{1,0:T(8,128)(2,1)S(1)} collective-permute-done((bf16[32,256]{1,0:T(8,128)(2,1)S(1)}, bf16[32,256]{1,0:T(8,128)(2,1)S(1)}, u32[]{:S(2)}, u32[]{:S(2)}) %collective-permute-start.1) | collective-permute-done | bytes 16416 | tf_op jit(solution)/shard_map/ppermute | solution.py:373
  11.8 0.0 copy-start.1
  11.8 1.0 %copy-done.1 = bf16[1,45,16,256]{3,2,1,0:T(8,128)(2,1)S(1)} copy-done((bf16[1,45,16,256]{3,2,1,0:T(8,128)(2,1)S(1)}, bf16[1,45,16,256]{3,2,1,0:T(8,128)(2,1)}, u32[]{:S(2)}) %copy-start.1) | copy-done | bytes 368664
  12.8 0.7 %pack.1 = (bf16[96,256]{1,0:T(8,128)(2,1)S(1)}, bf16[96,256]{1,0:T(8,128)(2,1)S(1)}) custom-call(s32[3]{0:T(128)S(1)} %pad_add_fusion.meta.refs_0_, bf16[720,256]{1,0:T(8,128)(2,1)S(1)} %bitcast.10, bf16[32,256]{1,0:T(8,128)(2,1)S(1)} %collective-permute-done.1.halo.refs_0_), custom_call_target="tpu_custom_call" | custom-call | flops 1000000 | bytes 800000 | tf_op jit(solution)/shard_map/pack/pallas_call | solution.py:349
  13.5 0.1 collective-permute-start.4
  13.6 1.5 %collective-permute-start.5 = (bf16[96,256]{1,0:T(8,128)(2,1)S(1)}, bf16[96,256]{1,0:T(8,128)(2,1)S(1)}, u32[]{:S(2)}, u32[]{:S(2)}) collective-permute-start(bf16[96,256]{1,0:T(8,128)(2,1)S(1)} %get-tuple-element.19), channel_id=1, source_target_pairs={{0,3},{3,0},{1,2},{2,1},{4,7},{7,4},{5,6},{6,5},{8,11},{11,8},{9,1... | collective-permute-start | bytes 147464 | tf_op jit(solution)/shard_map/ppermute | solution.py:378
  15.1 0.0 collective-permute-done.4.refs_1_
  15.1 3.6 %collective-permute-done.5.refs_2_ = bf16[96,256]{1,0:T(8,128)(2,1)S(1)} collective-permute-done((bf16[96,256]{1,0:T(8,128)(2,1)S(1)}, bf16[96,256]{1,0:T(8,128)(2,1)S(1)}, u32[]{:S(2)}, u32[]{:S(2)}) %collective-permute-start.5) | collective-permute-done | bytes 49184 | tf_op jit(solution)/shard_map/ppermute | solution.py:378
  18.7 0.1 collective-permute-start.7
  18.8 1.0 %collective-permute-start.8 = (bf16[224,256]{1,0:T(8,128)(2,1)S(1)}, bf16[224,256]{1,0:T(8,128)(2,1)S(1)}, u32[]{:S(2)}, u32[]{:S(2)}) collective-permute-start(bf16[224,256]{1,0:T(8,128)(2,1)S(1)} %join.1.refs_2_.refs_3_.refs_4_.refs_5_), channel_id=1, source_target_pairs={{0,16},{8,24},{16,32},{24,40},{32,48},{40,56},{48,64},{56,72},{64,... | collective-permute-start | bytes 344072 | tf_op jit(solution)/shard_map/ppermute | solution.py:381
  19.8 0.0 collective-permute-done.refs_2_
  19.8 2.6 %collective-permute-start.2 = (bf16[720,256]{1,0:T(8,128)(2,1)S(1)}, bf16[720,256]{1,0:T(8,128)(2,1)S(1)}, u32[]{:S(2)}, u32[]{:S(2)}) collective-permute-start(bf16[720,256]{1,0:T(8,128)(2,1)S(1)} %collective-permute-done.refs_2_), channel_id=1, source_target_pairs={{0,8},{8,16},{16,24},{24,32},{32,40},{40,48},{48,56},{56,64},{64,7... | collective-permute-start | bytes 1105928 | tf_op jit(solution)/shard_map/ppermute | solution.py:384
  22.4 0.7 %pad_maximum_fusion.refs_9_.refs_11_ = f32[2,256]{1,0:T(2,128)S(1)} fusion(f32[1,256]{1,0:T(1,128)} %bitcast.18, f32[1,256]{1,0:T(1,128)} %bitcast.19), kind=kLoop, calls=%fused_computation.1 | loop fusion | flops 512 | bytes 4096 | tf_op jit(solution)/shard_map/stack | solution.py:368
  23.1 4.5 %collective-permute-start.11 = (bf16[224,256]{1,0:T(8,128)(2,1)S(1)}, bf16[224,256]{1,0:T(8,128)(2,1)S(1)}, u32[]{:S(2)}, u32[]{:S(2)}) collective-permute-start(bf16[224,256]{1,0:T(8,128)(2,1)S(1)} %join.1.refs_2_.refs_3_.refs_4_.refs_5_), channel_id=1, source_target_pairs={{0,32},{8,40},{16,48},{24,56},{32,64},{40,72},{48,80},{56,88},{64,... | collective-permute-start | bytes 344072 | tf_op jit(solution)/shard_map/ppermute | solution.py:382
  27.5 0.0 collective-permute-done.3
  27.6 0.0 copy-start
  27.6 2.0 %copy-done = bf16[3,3,3,256,256]{4,3,2,1,0:T(8,128)(2,1)S(1)} copy-done((bf16[3,3,3,256,256]{4,3,2,1,0:T(8,128)(2,1)S(1)}, bf16[3,3,3,256,256]{4,3,2,1,0:T(8,128)(2,1)}, u32[]{:S(2)}) %copy-start) | copy-done | bytes 3538968
  29.6 0.0 copy-start.2
  29.6 1.0 %copy-done.2 = bf16[1,45,16,256]{3,2,1,0:T(8,128)(2,1)S(1)} copy-done((bf16[1,45,16,256]{3,2,1,0:T(8,128)(2,1)S(1)}, bf16[1,45,16,256]{3,2,1,0:T(8,128)(2,1)}, u32[]{:S(2)}) %copy-start.2) | copy-done | bytes 368664
  30.5 2.1 %step0.1.refs_6_ = f32[832,256]{1,0:T(8,128)S(1)} custom-call(s32[3]{0:T(128)S(1)} %pad_add_fusion.meta.refs_0_, bf16[720,256]{1,0:T(8,128)(2,1)S(1)} %bitcast.11, bf16[224,256]{1,0:T(8,128)(2,1)S(1)} %join.1.refs_2_.refs_3_.refs_4_.refs_5_, bf16[3,3,3,256,256]{4,3,2,1,0:T(8,128)(2,1)S(1)} %copy-done), custom_call_target="tpu_custom_call" | custom-call | flops 1000000000 | bytes 1000000 | tf_op jit(solution)/shard_map/step0/pallas_call | solution.py:278
  32.7 0.0 copy-start.3
  32.7 0.0 collective-permute-done.8.refs_6_.refs_7_
  32.7 1.7 %collective-permute-start.9 = (bf16[224,256]{1,0:T(8,128)(2,1)S(1)}, bf16[224,256]{1,0:T(8,128)(2,1)S(1)}, u32[]{:S(2)}, u32[]{:S(2)}) collective-permute-start(bf16[224,256]{1,0:T(8,128)(2,1)S(1)} %collective-permute-done.8.refs_6_.refs_7_), channel_id=1, source_target_pairs={{0,8},{8,16},{16,24},{24,32},{32,40},{40,48},{48,56},{56,64},{64,7... | collective-permute-start | bytes 344072 | tf_op jit(solution)/shard_map/ppermute | solution.py:391
  34.4 1.6 %collective-permute-start.10 = (bf16[720,256]{1,0:T(8,128)(2,1)S(1)}, bf16[720,256]{1,0:T(8,128)(2,1)S(1)}, u32[]{:S(2)}, u32[]{:S(2)}) collective-permute-start(bf16[720,256]{1,0:T(8,128)(2,1)S(1)} %collective-permute-done.3), channel_id=1, source_target_pairs={{48,32},{56,40},{0,48},{8,56},{80,64},{88,72},{96,80},{40,88},{112... | collective-permute-start | bytes 1105928 | tf_op jit(solution)/shard_map/ppermute | solution.py:385
  36.0 0.0 collective-permute-done.7.refs_4_.refs_5_.refs_6_
  36.0 3.1 %step1.1 = (f32[832,256]{1,0:T(8,128)S(1)}, f32[832,256]{1,0:T(8,128)S(1)}) custom-call(s32[3]{0:T(128)S(1)} %pad_add_fusion.meta.refs_0_, bf16[720,256]{1,0:T(8,128)(2,1)S(1)} %bitcast.12, bf16[720,256]{1,0:T(8,128)(2,1)S(1)} %collective-permute-done.refs_2_, bf16[224,256]{1,0:T(8,128)(2,1)S(1)} %join.1.refs_2_.refs_3_.refs_4_.refs_5_, ...), custom_call_target="tpu_custom_call" | custom-call | flops 2000000000 | bytes 1000000 | tf_op jit(solution)/shard_map/step1/pallas_call | solution.py:278
  39.1 6.2 %collective-permute-done.2.refs_3_ = bf16[720,256]{1,0:T(8,128)(2,1)S(1)} collective-permute-done((bf16[720,256]{1,0:T(8,128)(2,1)S(1)}, bf16[720,256]{1,0:T(8,128)(2,1)S(1)}, u32[]{:S(2)}, u32[]{:S(2)}) %collective-permute-start.2) | collective-permute-done | bytes 368672 | tf_op jit(solution)/shard_map/ppermute | solution.py:384
  45.3 0.0 collective-permute-start.6
  45.3 0.0 copy-done.3
  45.3 7.2 %step2.1 = (f32[832,256]{1,0:T(8,128)S(1)}, f32[832,256]{1,0:T(8,128)S(1)}, f32[720,256]{1,0:T(8,128)S(1)}) custom-call(s32[3]{0:T(128)S(1)} %pad_add_fusion.meta.refs_0_, bf16[720,256]{1,0:T(8,128)(2,1)S(1)} %bitcast.13, bf16[720,256]{1,0:T(8,128)(2,1)S(1)} %collective-permute-done.refs_2_, bf16[720,256]{1,0:T(8,128)(2,1)S(1)} %collective-permute-done.2.refs_3_, ...), custom_call_target="tpu_custom_call" | custom-call | flops 4000000000 | bytes 1000000 | tf_op jit(solution)/shard_map/step2/pallas_call | solution.py:278
  52.6 0.0 collective-permute-done.11.refs_8_
  52.6 0.0 collective-permute-done.10.refs_4_
  52.6 2.2 %step4.1.refs_14_ = f32[832,256]{1,0:T(8,128)S(1)} custom-call(s32[3]{0:T(128)S(1)} %pad_add_fusion.meta.refs_0_, bf16[720,256]{1,0:T(8,128)(2,1)S(1)} %bitcast.14, bf16[720,256]{1,0:T(8,128)(2,1)S(1)} %collective-permute-done.refs_2_, bf16[720,256]{1,0:T(8,128)(2,1)S(1)} %collective-permute-done.2.refs_3_, ...), custom_call_target="tpu_custom_call" | custom-call | flops 2000000000 | bytes 1000000 | tf_op jit(solution)/shard_map/step4/pallas_call | solution.py:278
  54.8 0.0 collective-permute-done.9.refs_8_
  54.8 1.4 %collective-permute-done.6.refs_4_ = bf16[720,256]{1,0:T(8,128)(2,1)S(1)} collective-permute-done((bf16[720,256]{1,0:T(8,128)(2,1)S(1)}, bf16[720,256]{1,0:T(8,128)(2,1)S(1)}, u32[]{:S(2)}, u32[]{:S(2)}) %collective-permute-start.6) | collective-permute-done | bytes 368672 | tf_op jit(solution)/shard_map/ppermute | solution.py:390
  56.2 6.7 %step3.1 = bf16[720,256]{1,0:T(8,128)(2,1)} custom-call(s32[3]{0:T(128)S(1)} %pad_add_fusion.meta.refs_0_, bf16[720,256]{1,0:T(8,128)(2,1)S(1)} %bitcast.15, bf16[720,256]{1,0:T(8,128)(2,1)S(1)} %collective-permute-done.refs_2_, bf16[720,256]{1,0:T(8,128)(2,1)S(1)} %collective-permute-done.2.refs_3_, bf16[720,256]{1,0:T(8,128)(2,1)S(1)} %collective-permute-done.6.refs_4_, ...), custom_call_target="tpu_custom_call" | custom-call | flops 3000000000 | bytes 1000000 | tf_op jit(solution)/shard_map/step3/pallas_call | solution.py:278
  (1 shorter events, 0.0 us)
Async XLA Ops:
  0.0 19.8 %collective-permute-start = (bf16[720,256]{1,0:T(8,128)(2,1)}, bf16[720,256]{1,0:T(8,128)(2,1)S(1)}, u32[]{:S(2)}, u32[]{:S(2)}) collective-permute-start(bf16[720,256]{1,0:T(8,128)(2,1)} %bitcast.8), channel_id=1, source_target_pairs={{0,8},{8,16},{16,24},{24,32},{32,40},{40,48},{48,56},{56,64},{64,7... | collective-permute-start | bytes 1105928 | tf_op jit(solution)/shard_map/ppermute | solution.py:374
  1.9 25.6 %collective-permute-start.3 = (bf16[720,256]{1,0:T(8,128)(2,1)}, bf16[720,256]{1,0:T(8,128)(2,1)S(1)}, u32[]{:S(2)}, u32[]{:S(2)}) collective-permute-start(bf16[720,256]{1,0:T(8,128)(2,1)} %bitcast.9), channel_id=1, source_target_pairs={{0,48},{8,56},{16,0},{24,8},{32,80},{40,88},{48,96},{56,40},{64,11... | collective-permute-start | bytes 1105928 | tf_op jit(solution)/shard_map/ppermute | solution.py:375
  8.1 3.7 %collective-permute-start.1 = (bf16[32,256]{1,0:T(8,128)(2,1)S(1)}, bf16[32,256]{1,0:T(8,128)(2,1)S(1)}, u32[]{:S(2)}, u32[]{:S(2)}) collective-permute-start(bf16[32,256]{1,0:T(8,128)(2,1)S(1)} %bitcast.17), channel_id=1, source_target_pairs={{0,4},{4,0},{1,5},{5,1},{2,6},{6,2},{3,7},{7,3},{8,12},{12,8},{9,1... | collective-permute-start | bytes 49160 | tf_op jit(solution)/shard_map/ppermute | solution.py:373
  11.8 1.0 %copy-start.1 = (bf16[1,45,16,256]{3,2,1,0:T(8,128)(2,1)S(1)}, bf16[1,45,16,256]{3,2,1,0:T(8,128)(2,1)}, u32[]{:S(2)}) copy-start(bf16[1,45,16,256]{3,2,1,0:T(8,128)(2,1)} %param.5) | copy-start | bytes 1105924
  13.5 1.6 %collective-permute-start.4 = (bf16[96,256]{1,0:T(8,128)(2,1)S(1)}, bf16[96,256]{1,0:T(8,128)(2,1)S(1)}, u32[]{:S(2)}, u32[]{:S(2)}) collective-permute-start(bf16[96,256]{1,0:T(8,128)(2,1)S(1)} %get-tuple-element.16), channel_id=1, source_target_pairs={{0,1},{1,0},{2,3},{3,2},{4,5},{5,4},{6,7},{7,6},{8,9},{9,8},{10,11... | collective-permute-start | bytes 147464 | tf_op jit(solution)/shard_map/ppermute | solution.py:377
  13.6 5.1 %collective-permute-start.5 = (bf16[96,256]{1,0:T(8,128)(2,1)S(1)}, bf16[96,256]{1,0:T(8,128)(2,1)S(1)}, u32[]{:S(2)}, u32[]{:S(2)}) collective-permute-start(bf16[96,256]{1,0:T(8,128)(2,1)S(1)} %get-tuple-element.19), channel_id=1, source_target_pairs={{0,3},{3,0},{1,2},{2,1},{4,7},{7,4},{5,6},{6,5},{8,11},{11,8},{9,1... | collective-permute-start | bytes 147464 | tf_op jit(solution)/shard_map/ppermute | solution.py:378
  18.7 17.3 %collective-permute-start.7 = (bf16[224,256]{1,0:T(8,128)(2,1)S(1)}, bf16[224,256]{1,0:T(8,128)(2,1)S(1)}, u32[]{:S(2)}, u32[]{:S(2)}) collective-permute-start(bf16[224,256]{1,0:T(8,128)(2,1)S(1)} %join.1.refs_2_.refs_3_.refs_4_.refs_5_), channel_id=1, source_target_pairs={{0,8},{8,16},{16,24},{24,32},{32,40},{40,48},{48,56},{56,64},{64,7... | collective-permute-start | bytes 344072 | tf_op jit(solution)/shard_map/ppermute | solution.py:380
  18.8 13.9 %collective-permute-start.8 = (bf16[224,256]{1,0:T(8,128)(2,1)S(1)}, bf16[224,256]{1,0:T(8,128)(2,1)S(1)}, u32[]{:S(2)}, u32[]{:S(2)}) collective-permute-start(bf16[224,256]{1,0:T(8,128)(2,1)S(1)} %join.1.refs_2_.refs_3_.refs_4_.refs_5_), channel_id=1, source_target_pairs={{0,16},{8,24},{16,32},{24,40},{32,48},{40,56},{48,64},{56,72},{64,... | collective-permute-start | bytes 344072 | tf_op jit(solution)/shard_map/ppermute | solution.py:381
  19.8 25.5 %collective-permute-start.2 = (bf16[720,256]{1,0:T(8,128)(2,1)S(1)}, bf16[720,256]{1,0:T(8,128)(2,1)S(1)}, u32[]{:S(2)}, u32[]{:S(2)}) collective-permute-start(bf16[720,256]{1,0:T(8,128)(2,1)S(1)} %collective-permute-done.refs_2_), channel_id=1, source_target_pairs={{0,8},{8,16},{16,24},{24,32},{32,40},{40,48},{48,56},{56,64},{64,7... | collective-permute-start | bytes 1105928 | tf_op jit(solution)/shard_map/ppermute | solution.py:384
  23.1 29.5 %collective-permute-start.11 = (bf16[224,256]{1,0:T(8,128)(2,1)S(1)}, bf16[224,256]{1,0:T(8,128)(2,1)S(1)}, u32[]{:S(2)}, u32[]{:S(2)}) collective-permute-start(bf16[224,256]{1,0:T(8,128)(2,1)S(1)} %join.1.refs_2_.refs_3_.refs_4_.refs_5_), channel_id=1, source_target_pairs={{0,32},{8,40},{16,48},{24,56},{32,64},{40,72},{48,80},{56,88},{64,... | collective-permute-start | bytes 344072 | tf_op jit(solution)/shard_map/ppermute | solution.py:382
  27.6 2.0 %copy-start = (bf16[3,3,3,256,256]{4,3,2,1,0:T(8,128)(2,1)S(1)}, bf16[3,3,3,256,256]{4,3,2,1,0:T(8,128)(2,1)}, u32[]{:S(2)}) copy-start(bf16[3,3,3,256,256]{4,3,2,1,0:T(8,128)(2,1)} %refs_9_.3) | copy-start | bytes 10616836
  29.6 1.0 %copy-start.2 = (bf16[1,45,16,256]{3,2,1,0:T(8,128)(2,1)S(1)}, bf16[1,45,16,256]{3,2,1,0:T(8,128)(2,1)}, u32[]{:S(2)}) copy-start(bf16[1,45,16,256]{3,2,1,0:T(8,128)(2,1)} %param.5) | copy-start | bytes 1105924
  32.7 12.7 %copy-start.3 = (bf16[3,3,3,256,256]{4,3,2,1,0:T(8,128)(2,1)S(1)}, bf16[3,3,3,256,256]{4,3,2,1,0:T(8,128)(2,1)}, u32[]{:S(2)}) copy-start(bf16[3,3,3,256,256]{4,3,2,1,0:T(8,128)(2,1)} %refs_10_.1) | copy-start | bytes 10616836
  32.7 22.1 %collective-permute-start.9 = (bf16[224,256]{1,0:T(8,128)(2,1)S(1)}, bf16[224,256]{1,0:T(8,128)(2,1)S(1)}, u32[]{:S(2)}, u32[]{:S(2)}) collective-permute-start(bf16[224,256]{1,0:T(8,128)(2,1)S(1)} %collective-permute-done.8.refs_6_.refs_7_), channel_id=1, source_target_pairs={{0,8},{8,16},{16,24},{24,32},{32,40},{40,48},{48,56},{56,64},{64,7... | collective-permute-start | bytes 344072 | tf_op jit(solution)/shard_map/ppermute | solution.py:391
  34.4 18.2 %collective-permute-start.10 = (bf16[720,256]{1,0:T(8,128)(2,1)S(1)}, bf16[720,256]{1,0:T(8,128)(2,1)S(1)}, u32[]{:S(2)}, u32[]{:S(2)}) collective-permute-start(bf16[720,256]{1,0:T(8,128)(2,1)S(1)} %collective-permute-done.3), channel_id=1, source_target_pairs={{48,32},{56,40},{0,48},{8,56},{80,64},{88,72},{96,80},{40,88},{112... | collective-permute-start | bytes 1105928 | tf_op jit(solution)/shard_map/ppermute | solution.py:385
  45.3 10.8 %collective-permute-start.6 = (bf16[720,256]{1,0:T(8,128)(2,1)S(1)}, bf16[720,256]{1,0:T(8,128)(2,1)S(1)}, u32[]{:S(2)}, u32[]{:S(2)}) collective-permute-start(bf16[720,256]{1,0:T(8,128)(2,1)S(1)} %collective-permute-done.2.refs_3_), channel_id=1, source_target_pairs={{0,8},{8,16},{16,24},{24,32},{32,40},{40,48},{48,56},{56,64},{64,7... | collective-permute-start | bytes 1105928 | tf_op jit(solution)/shard_map/ppermute | solution.py:390

commit v4 on v3

--- a/solution.py
+++ b/solution.py
@@ -11,7 +11,7 @@
 CH = 256
 ROWS, COLS = 45, 16
 LIMIT = 30 * 2**20
-COST = (1000000000, 2000000000, 4000000000, 3000000000, 2000000000)
+COST = (1000000000, 2000000000, 2000000000, 3000000000, 500000000)
 FORTH = (45,)
 BACK = (45,)
 HALF = 2
@@ -59,7 +59,8 @@
         work[h, pl.ds(start, size, stride), :] = value[:, h * 128 : (h + 1) * 128]
 
 
-def pack_kernel(meta, main, halo, out_core, out_far, work):
+def pack_kernel(meta, main, halo, out_core, out_far, own, work):
+    own[...] = main[...]
     row, col = meta[1], meta[2]
     first = 1 + row
     for r in range(ROWS):
@@ -172,8 +173,8 @@
     mains = [pop(count) for count in plan["parts"]]
     strips = pop(steps + 1 - plan["late"])
     (w1,) = pop(1)
-    w2, biases = pop(2) if plan["done"] else (None, None)
-    (latent,) = pop(1) if plan["last"] else (None,)
+    w2, bias1 = pop(2) if plan["done"] else (None, None)
+    bias2, latent = pop(2) if plan["last"] else (None, None)
     sums_in = dict(zip(plan["carried"], pop(len(plan["carried"]))))
     total_in = pop(1)[0] if plan["total_in"] else None
     outs = pop(plan["outs"])
@@ -217,11 +218,11 @@
         total = 0.0 if total_in is None else total_in[...]
         for i, frame in enumerate(plan["done"]):
             room = (work, x) if i == 0 else refs[7:9]
-            build_hidden(meta, ready.at[i], biases[0:1], *room)
+            build_hidden(meta, ready.at[i], bias1[...], *room)
         for i, frame in enumerate(plan["done"]):
             total = total + second_taps(x if i == 0 else refs[8], w2[2 - frame])
         if plan["last"]:
-            total = (latent[...].astype(F32) + (total + biases[1:2])).astype(BF)
+            total = (latent[...].astype(F32) + (total + bias2[...])).astype(BF)
         outs[-1][...] = total
 
 
@@ -238,6 +239,7 @@
     pltpu.VMEM((2, PR * WIDE, 128), F32),
     pltpu.VMEM((3, PR * COLS, CH), BF),
 ]
+ANY = pl.BlockSpec(memory_space=pl.ANY)
 SMEM = pl.BlockSpec(memory_space=pltpu.SMEM)
 VMEM = pl.BlockSpec(memory_space=pltpu.VMEM)
 
@@ -271,8 +273,8 @@
     plan["parts"] = [len(f[0]) for f in frames]
     w1, w2, biases = weights
     args = [meta, *mains, *strips, w1]
-    args += [w2, biases] if done else []
-    args += [latent] if last else []
+    args += [w2, biases[0]] if done else []
+    args += [biases[1], latent] if last else []
     args += [sums[f] for f in plan["carried"]] + ([total] if plan["total_in"] else [])
     specs = [SMEM] + [VMEM] * (len(args) - 1)
     outs = pl.pallas_call(
@@ -294,6 +296,25 @@
     return {**sums, **dict(zip(kept, outs))}, (outs[-1] if done else total)
 
 
+def bring_kernel(source, target, sem):
+    copy = pltpu.make_async_copy(source, target, sem)
+    copy.start()
+    copy.wait()
+
+
+def bring(weight):
+    return pl.pallas_call(
+        bring_kernel,
+        out_shape=jax.ShapeDtypeStruct(weight.shape, weight.dtype),
+        in_specs=[ANY],
+        out_specs=VMEM,
+        scratch_shapes=[pltpu.SemaphoreType.DMA],
+        compiler_params=pltpu.CompilerParams(vmem_limit_bytes=LIMIT),
+        cost_estimate=pl.CostEstimate(flops=1000000000, bytes_accessed=1000, transcendentals=0),
+        name="bring",
+    )(weight)
+
+
 def tie(value, *first):
     return lax.optimization_barrier((value, *first))[0]
 
@@ -348,9 +369,13 @@
     edge = jax.ShapeDtypeStruct((2 * PR, CH), BF)
     return pl.pallas_call(
         pack_kernel,
-        out_shape=[edge, edge],
+        out_shape=[
+            edge,
+            edge,
+            jax.ShapeDtypeStruct((ROWS * COLS, CH), BF),
+        ],
         in_specs=[SMEM, VMEM, VMEM],
-        out_specs=[VMEM, VMEM],
+        out_specs=[VMEM] * 3,
         scratch_shapes=[pltpu.VMEM((2, PR * COLS, 128), F32)],
         compiler_params=pltpu.CompilerParams(vmem_limit_bytes=LIMIT),
         cost_estimate=pl.CostEstimate(flops=1000000, bytes_accessed=800000, transcendentals=0),
@@ -365,7 +390,6 @@
     col = lax.axis_index("col").astype(jnp.int32)
     meta = jnp.stack([t, row, col])
     own = latent.reshape(ROWS * COLS, CH)
-    biases = jnp.stack([conv1_bias, conv2_bias])
 
     ahead = functools.partial(lax.ppermute, axis_name="tm")
     next_frame = shifted(count, 1)
@@ -373,27 +397,29 @@
     rows = lax.ppermute(to_row, "row", [(0, 1), (1, 0)])
     main1 = ahead(own, perm=next_frame)
     half_way = ahead(own, perm=backward(count, 0, HALF))
-    to_core, to_far = pack(meta, own, rows)
+    to_core, to_far, held = pack(meta, own, rows)
+    first_weight = bring(tie(conv1_weight, to_core))
     near = lax.ppermute(to_core, "col", [(0, 1), (1, 0), (2, 3), (3, 2)])
     far = lax.ppermute(to_far, "col", [(0, 3), (3, 0), (1, 2), (2, 1)])
-    strips0 = join(rows, near, far)
+    strips0 = join(tie(rows, first_weight), near, far)
     strips1 = ahead(strips0, perm=next_frame)
     strips2 = ahead(strips0, perm=shifted(count, 2))
     strips4 = ahead(strips0, perm=shifted(count, 4))
 
     main2 = ahead(tie(main1, to_core), perm=next_frame)
     main4 = ahead(half_way, perm=backward(count, HALF, 4 - HALF))
-    weights = (conv1_weight, conv2_weight, biases)
-    frames = [([own], strips0), ([main1], strips1)]
-    sums, total = step(0, tie(meta, half_way), frames[:1], weights, own, {}, None)
+    biases = (conv1_bias.reshape(1, CH), conv2_bias.reshape(1, CH))
+    weights = (first_weight, conv2_weight, biases)
+    frames = [([held], strips0), ([main1], strips1)]
+    sums, total = step(0, tie(meta, half_way), frames[:1], weights, held, {}, None)
     main2 = tie(main2, sums[0])
     main3 = ahead(main2, perm=next_frame)
+    sums, total = step(1, meta, frames, weights, held, sums, total)
     strips3 = ahead(tie(strips2, sums[0]), perm=next_frame)
-    sums, total = step(1, meta, frames, weights, own, sums, total)
     frames += [([main2], strips2), ([main3], strips3), ([main4], strips4)]
-    sums, total = step(2, meta, frames[:3], weights, own, sums, total)
-    sums, total = step(4, meta, frames, weights, own, sums, total)
-    out = step(3, meta, frames[:4], weights, own, sums, total)
+    sums, total = step(2, meta, frames[:3], weights, held, sums, total)
+    sums, total = step(4, meta, frames, weights, held, sums, total)
+    out = step(3, meta, frames[:4], weights, held, sums, total)
     return out.reshape(1, ROWS, COLS, CH)
 
 

time: 63.2 us -> 60.9 us (0.964)
  waiting for transfers between devices: 14 us -> 11.5 us
  local copies, waits for them, and re-layouts: 3.98 us -> 3.01 us
  starting transfers between devices: 21.2 us -> 22.1 us
  other arithmetic: 1.53 us -> 0.83 us
    ppermute x1, waiting for transfers between devices: 6.22 us -> 0.01 us  [local(): main2 = ahead(tie(main1, to_core), perm=next_frame)]
    ppermute x1, waiting for transfers between devices: 0.01 us -> 3.61 us  [local(): main1 = ahead(own, perm=next_frame)]
    ppermute x1, waiting for transfers between devices: 0.01 us -> 3.13 us  [local(): strips2 = ahead(strips0, perm=shifted(count, 2))]
    ppermute x1, starting transfers between devices: 2.55 us -> 0.01 us  [local(): main2 = ahead(tie(main1, to_core), perm=next_frame)]
    ppermute x1, waiting for transfers between devices: 3.58 us -> 1.08 us  [local(): far = lax.ppermute(to_far, 'col', [(0, 3), (3, 0), (1, 2), (2, 1)])]
    ppermute x1, starting transfers between devices: 4.49 us -> 2.55 us  [local(): strips4 = ahead(strips0, perm=shifted(count, 4))]
    ppermute x1, starting transfers between devices: 1.02 us -> 2.95 us  [local(): strips2 = ahead(strips0, perm=shifted(count, 2))]
    ppermute x1, starting transfers between devices: 1.72 us -> 3.48 us  [local(): strips3 = ahead(tie(strips2, sums[0]), perm=next_frame)]
  transfers between devices with their start and end apart: 12 -> 12, of which waited for: 4 -> 5; matrix products, arithmetic and copies ran while one was open for 2% -> 1% of each run, Pallas kernels for 24% -> 26%
where the time goes in v4:
time: 60.9 us; the launch traced here: 59.9 us
  Pallas kernels  22.4 us (37%)
  starting transfers between devices  22.1 us (36%)
  waiting for transfers between devices  11.5 us (19%)
  local copies, waits for them, and re-layouts  3.01 us (5%)
  other arithmetic  0.83 us (1%)
    pallas_call x5, Pallas kernels, step(): pl.pallas_call(functools.partial(step_kernel, steps, plan), out_shape=out...  21.3 us
    ppermute x1, starting transfers between devices, local(): half_way = ahead(own, perm=backward(count, 0, HALF))  5.4 us
    ppermute x1, waiting for transfers between devices, local(): main1 = ahead(own, perm=next_frame)  3.61 us
    ppermute x1, starting transfers between devices, local(): strips3 = ahead(tie(strips2, sums[0]), perm=next_frame)  3.48 us
    ppermute x1, waiting for transfers between devices, local(): strips2 = ahead(strips0, perm=shifted(count, 2))  3.13 us
    unnamed x10, local copies, waits for them, and re-layouts  3.01 us
    ppermute x1, starting transfers between devices, local(): strips2 = ahead(strips0, perm=shifted(count, 2))  2.95 us
    ppermute x1, waiting for transfers between devices, local(): rows = lax.ppermute(to_row, 'row', [(0, 1), (1, 0)])  2.83 us
  transfers between devices with their start and end apart: 12, of which 5 were waited for; matrix products, arithmetic and copies ran while one was open for 1% of the time, Pallas kernels for 26%

profile of v4, /device:TPU:6, one launch (start us, length us, event | category | flops | bytes accessed | tf_op | source)
XLA Modules:
  0.0 59.9 jit_solution(10924158761796965062)
XLA Ops:
  0.0 1.9 %collective-permute-start.1 = (bf16[720,256]{1,0:T(8,128)(2,1)}, bf16[720,256]{1,0:T(8,128)(2,1)S(1)}, u32[]{:S(2)}, u32[]{:S(2)}) collective-permute-start(bf16[720,256]{1,0:T(8,128)(2,1)} %bitcast.8), channel_id=1, source_target_pairs={{0,8},{8,16},{16,24},{24,32},{32,40},{40,48},{48,56},{56,64},{64,7... | collective-permute-start | bytes 1105928 | tf_op jit(solution)/shard_map/ppermute | solution.py:398
  1.9 5.4 %collective-permute-start.3 = (bf16[720,256]{1,0:T(8,128)(2,1)}, bf16[720,256]{1,0:T(8,128)(2,1)S(1)}, u32[]{:S(2)}, u32[]{:S(2)}) collective-permute-start(bf16[720,256]{1,0:T(8,128)(2,1)} %bitcast.9), channel_id=1, source_target_pairs={{0,48},{8,56},{16,0},{24,8},{32,80},{40,88},{48,96},{56,40},{64,11... | collective-permute-start | bytes 1105928 | tf_op jit(solution)/shard_map/ppermute | solution.py:399
  7.3 0.8 %slice_select_fusion = bf16[1,2,16,256]{3,2,1,0:T(8,128)(2,1)S(1)} fusion(bf16[1,45,16,256]{3,2,1,0:T(8,128)(2,1)} %param.5, pred[]{:T(512)S(6)} %eq.3), kind=kLoop, calls=%fused_computation | loop fusion | flops 8192 | bytes 49153 | tf_op jit(solution)/shard_map/jit(_where)/select_n | solution.py:396
  8.1 0.8 %collective-permute-start = (bf16[32,256]{1,0:T(8,128)(2,1)S(1)}, bf16[32,256]{1,0:T(8,128)(2,1)S(1)}, u32[]{:S(2)}, u32[]{:S(2)}) collective-permute-start(bf16[32,256]{1,0:T(8,128)(2,1)S(1)} %bitcast.14), channel_id=1, source_target_pairs={{0,4},{4,0},{1,5},{5,1},{2,6},{6,2},{3,7},{7,3},{8,12},{12,8},{9,1... | collective-permute-start | bytes 49160 | tf_op jit(solution)/shard_map/ppermute | solution.py:397
  8.9 0.1 pad_add_fusion.meta.refs_0_
  9.0 2.8 %collective-permute-done.halo.refs_0_ = bf16[32,256]{1,0:T(8,128)(2,1)S(1)} collective-permute-done((bf16[32,256]{1,0:T(8,128)(2,1)S(1)}, bf16[32,256]{1,0:T(8,128)(2,1)S(1)}, u32[]{:S(2)}, u32[]{:S(2)}) %collective-permute-start) | collective-permute-done | bytes 16416 | tf_op jit(solution)/shard_map/ppermute | solution.py:397
  11.8 0.0 copy-start.2
  11.8 1.0 %copy-done.2 = bf16[1,45,16,256]{3,2,1,0:T(8,128)(2,1)S(1)} copy-done((bf16[1,45,16,256]{3,2,1,0:T(8,128)(2,1)S(1)}, bf16[1,45,16,256]{3,2,1,0:T(8,128)(2,1)}, u32[]{:S(2)}) %copy-start.2) | copy-done | bytes 368664
  12.8 0.7 %pack.1 = (bf16[96,256]{1,0:T(8,128)(2,1)S(1)}, bf16[96,256]{1,0:T(8,128)(2,1)S(1)}, bf16[720,256]{1,0:T(8,128)(2,1)S(1)}) custom-call(s32[3]{0:T(128)S(1)} %pad_add_fusion.meta.refs_0_, bf16[720,256]{1,0:T(8,128)(2,1)S(1)} %bitcast.10, bf16[32,256]{1,0:T(8,128)(2,1)S(1)} %collective-permute-done.halo.refs_0_), custom_call_target="tpu_custom_call" | custom-call | flops 1000000 | bytes 800000 | tf_op jit(solution)/shard_map/pack/pallas_call | solution.py:370
  13.5 3.6 %collective-permute-done.1.refs_2_ = bf16[720,256]{1,0:T(8,128)(2,1)S(1)} collective-permute-done((bf16[720,256]{1,0:T(8,128)(2,1)}, bf16[720,256]{1,0:T(8,128)(2,1)S(1)}, u32[]{:S(2)}, u32[]{:S(2)}) %collective-permute-start.1) | collective-permute-done | bytes 368672 | tf_op jit(solution)/shard_map/ppermute | solution.py:398
  17.1 0.0 collective-permute-start.2
  17.1 0.0 collective-permute-start.4
  17.1 1.5 %collective-permute-start.5 = (bf16[96,256]{1,0:T(8,128)(2,1)S(1)}, bf16[96,256]{1,0:T(8,128)(2,1)S(1)}, u32[]{:S(2)}, u32[]{:S(2)}) collective-permute-start(bf16[96,256]{1,0:T(8,128)(2,1)S(1)} %get-tuple-element.25), channel_id=1, source_target_pairs={{0,3},{3,0},{1,2},{2,1},{4,7},{7,4},{5,6},{6,5},{8,11},{11,8},{9,1... | collective-permute-start | bytes 147464 | tf_op jit(solution)/shard_map/ppermute | solution.py:403
  18.6 0.0 copy-start.1
  18.6 2.0 %copy-done.1 = bf16[3,3,3,256,256]{4,3,2,1,0:T(8,128)(2,1)S(1)} copy-done((bf16[3,3,3,256,256]{4,3,2,1,0:T(8,128)(2,1)S(1)}, bf16[3,3,3,256,256]{4,3,2,1,0:T(8,128)(2,1)}, u32[]{:S(2)}) %copy-start.1) | copy-done | bytes 3538968
  20.6 0.4 bring.1.refs_3_.refs_5_.refs_7_.refs_9_
  21.0 0.0 collective-permute-done.4.refs_1_
  21.1 1.1 %collective-permute-done.5.refs_2_ = bf16[96,256]{1,0:T(8,128)(2,1)S(1)} collective-permute-done((bf16[96,256]{1,0:T(8,128)(2,1)S(1)}, bf16[96,256]{1,0:T(8,128)(2,1)S(1)}, u32[]{:S(2)}, u32[]{:S(2)}) %collective-permute-start.5) | collective-permute-done | bytes 49184 | tf_op jit(solution)/shard_map/ppermute | solution.py:403
  22.1 0.1 collective-permute-start.7
  22.2 2.9 %collective-permute-start.8 = (bf16[224,256]{1,0:T(8,128)(2,1)S(1)}, bf16[224,256]{1,0:T(8,128)(2,1)S(1)}, u32[]{:S(2)}, u32[]{:S(2)}) collective-permute-start(bf16[224,256]{1,0:T(8,128)(2,1)S(1)} %join.1.refs_2_.refs_3_.refs_4_.refs_5_), channel_id=1, source_target_pairs={{0,16},{8,24},{16,32},{24,40},{32,48},{40,56},{48,64},{56,72},{64,... | collective-permute-start | bytes 344072 | tf_op jit(solution)/shard_map/ppermute | solution.py:406
  25.2 2.5 %collective-permute-start.11 = (bf16[224,256]{1,0:T(8,128)(2,1)S(1)}, bf16[224,256]{1,0:T(8,128)(2,1)S(1)}, u32[]{:S(2)}, u32[]{:S(2)}) collective-permute-start(bf16[224,256]{1,0:T(8,128)(2,1)S(1)} %join.1.refs_2_.refs_3_.refs_4_.refs_5_), channel_id=1, source_target_pairs={{0,32},{8,40},{16,48},{24,56},{32,64},{40,72},{48,80},{56,88},{64,... | collective-permute-start | bytes 344072 | tf_op jit(solution)/shard_map/ppermute | solution.py:407
  27.7 0.0 collective-permute-done.3
  27.7 2.3 %collective-permute-start.10 = (bf16[720,256]{1,0:T(8,128)(2,1)S(1)}, bf16[720,256]{1,0:T(8,128)(2,1)S(1)}, u32[]{:S(2)}, u32[]{:S(2)}) collective-permute-start(bf16[720,256]{1,0:T(8,128)(2,1)S(1)} %collective-permute-done.3), channel_id=1, source_target_pairs={{48,32},{56,40},{0,48},{8,56},{80,64},{88,72},{96,80},{40,88},{112... | collective-permute-start | bytes 1105928 | tf_op jit(solution)/shard_map/ppermute | solution.py:410
  30.0 2.1 %step0.1.refs_6_ = f32[832,256]{1,0:T(8,128)S(1)} custom-call(s32[3]{0:T(128)S(1)} %pad_add_fusion.meta.refs_0_, bf16[720,256]{1,0:T(8,128)(2,1)S(1)} %get-tuple-element.19.refs_1_.refs_13_, bf16[224,256]{1,0:T(8,128)(2,1)S(1)} %join.1.refs_2_.refs_3_.refs_4_.refs_5_, bf16[3,3,3,256,256]{4,3,2,1,0:T(8,128)(2,1)S(1)} %bring.1.refs_3_.refs_5_.refs_7_.refs_9_), custom_call_target="tpu_custom_call" | custom-call | flops 1000000000 | bytes 1000000 | tf_op jit(solution)/shard_map/step0/pallas_call | solution.py:280
  32.1 0.0 copy-start
  32.2 0.0 copy-start.3
  32.2 0.0 collective-permute-done.2.refs_3_
  32.2 1.1 %collective-permute-start.6 = (bf16[720,256]{1,0:T(8,128)(2,1)S(1)}, bf16[720,256]{1,0:T(8,128)(2,1)S(1)}, u32[]{:S(2)}, u32[]{:S(2)}) collective-permute-start(bf16[720,256]{1,0:T(8,128)(2,1)S(1)} %collective-permute-done.2.refs_3_), channel_id=1, source_target_pairs={{0,8},{8,16},{16,24},{24,32},{32,40},{40,48},{48,56},{56,64},{64,7... | collective-permute-start | bytes 1105928 | tf_op jit(solution)/shard_map/ppermute | solution.py:416
  33.3 0.8 %collective-permute-done.7.refs_4_.refs_5_.refs_6_ = bf16[224,256]{1,0:T(8,128)(2,1)S(1)} collective-permute-done((bf16[224,256]{1,0:T(8,128)(2,1)S(1)}, bf16[224,256]{1,0:T(8,128)(2,1)S(1)}, u32[]{:S(2)}, u32[]{:S(2)}) %collective-permute-start.7) | collective-permute-done | bytes 114720 | tf_op jit(solution)/shard_map/ppermute | solution.py:405
  34.1 3.1 %step1.1 = (f32[832,256]{1,0:T(8,128)S(1)}, f32[832,256]{1,0:T(8,128)S(1)}) custom-call(s32[3]{0:T(128)S(1)} %pad_add_fusion.meta.refs_0_, bf16[720,256]{1,0:T(8,128)(2,1)S(1)} %get-tuple-element.19.refs_1_.refs_13_, bf16[720,256]{1,0:T(8,128)(2,1)S(1)} %collective-permute-done.1.refs_2_, bf16[224,256]{1,0:T(8,128)(2,1)S(1)} %join.1.refs_2_.refs_3_.refs_4_.refs_5_, ...), custom_call_target="tpu_custom_call" | custom-call | flops 2000000000 | bytes 1000000 | tf_op jit(solution)/shard_map/step1/pallas_call | solution.py:280
  37.2 3.1 %collective-permute-done.8.refs_6_.refs_7_ = bf16[224,256]{1,0:T(8,128)(2,1)S(1)} collective-permute-done((bf16[224,256]{1,0:T(8,128)(2,1)S(1)}, bf16[224,256]{1,0:T(8,128)(2,1)S(1)}, u32[]{:S(2)}, u32[]{:S(2)}) %collective-permute-start.8) | collective-permute-done | bytes 114720 | tf_op jit(solution)/shard_map/ppermute | solution.py:406
  40.3 3.5 %collective-permute-start.9 = (bf16[224,256]{1,0:T(8,128)(2,1)S(1)}, bf16[224,256]{1,0:T(8,128)(2,1)S(1)}, u32[]{:S(2)}, u32[]{:S(2)}) collective-permute-start(bf16[224,256]{1,0:T(8,128)(2,1)S(1)} %collective-permute-done.8.refs_6_.refs_7_), channel_id=1, source_target_pairs={{0,8},{8,16},{16,24},{24,32},{32,40},{40,48},{48,56},{56,64},{64,7... | collective-permute-start | bytes 344072 | tf_op jit(solution)/shard_map/ppermute | solution.py:418
  43.8 0.0 copy-done
  43.8 0.0 copy-done.3
  43.8 7.2 %step2.1 = (f32[832,256]{1,0:T(8,128)S(1)}, f32[832,256]{1,0:T(8,128)S(1)}, f32[720,256]{1,0:T(8,128)S(1)}) custom-call(s32[3]{0:T(128)S(1)} %pad_add_fusion.meta.refs_0_, bf16[720,256]{1,0:T(8,128)(2,1)S(1)} %get-tuple-element.19.refs_1_.refs_13_, bf16[720,256]{1,0:T(8,128)(2,1)S(1)} %collective-permute-done.1.refs_2_, ...), custom_call_target="tpu_custom_call" | custom-call | flops 2000000000 | bytes 1000000 | tf_op jit(solution)/shard_map/step2/pallas_call | solution.py:280
  51.0 0.0 collective-permute-done.11.refs_8_
  51.0 0.0 collective-permute-done.10.refs_4_
  51.0 0.0 copy-start.4
  51.0 2.2 %step4.1.refs_15_ = f32[832,256]{1,0:T(8,128)S(1)} custom-call(s32[3]{0:T(128)S(1)} %pad_add_fusion.meta.refs_0_, bf16[720,256]{1,0:T(8,128)(2,1)S(1)} %get-tuple-element.19.refs_1_.refs_13_, bf16[720,256]{1,0:T(8,128)(2,1)S(1)} %collective-permute-done.1.refs_2_, bf16[720,256]{1,0:T(8,128)(2,1)S(1)} %collective-permute-done.2.refs_3_, ...), custom_call_target="tpu_custom_call" | custom-call | flops 500000000 | bytes 1000000 | tf_op jit(solution)/shard_map/step4/pallas_call | solution.py:280
  53.2 0.0 collective-permute-done.9.refs_8_
  53.2 0.0 collective-permute-done.6.refs_4_
  53.2 0.0 copy-done.4
  53.2 6.7 %step3.1 = bf16[720,256]{1,0:T(8,128)(2,1)} custom-call(s32[3]{0:T(128)S(1)} %pad_add_fusion.meta.refs_0_, bf16[720,256]{1,0:T(8,128)(2,1)S(1)} %get-tuple-element.19.refs_1_.refs_13_, bf16[720,256]{1,0:T(8,128)(2,1)S(1)} %collective-permute-done.1.refs_2_, bf16[720,256]{1,0:T(8,128)(2,1)S(1)} %collective-permute-done.2.refs_3_, ...), custom_call_target="tpu_custom_call" | custom-call | flops 3000000000 | bytes 1000000 | tf_op jit(solution)/shard_map/step3/pallas_call | solution.py:280
  (1 shorter events, 0.0 us)
Async XLA Ops:
  0.0 17.1 %collective-permute-start.1 = (bf16[720,256]{1,0:T(8,128)(2,1)}, bf16[720,256]{1,0:T(8,128)(2,1)S(1)}, u32[]{:S(2)}, u32[]{:S(2)}) collective-permute-start(bf16[720,256]{1,0:T(8,128)(2,1)} %bitcast.8), channel_id=1, source_target_pairs={{0,8},{8,16},{16,24},{24,32},{32,40},{40,48},{48,56},{56,64},{64,7... | collective-permute-start | bytes 1105928 | tf_op jit(solution)/shard_map/ppermute | solution.py:398
  1.9 25.8 %collective-permute-start.3 = (bf16[720,256]{1,0:T(8,128)(2,1)}, bf16[720,256]{1,0:T(8,128)(2,1)S(1)}, u32[]{:S(2)}, u32[]{:S(2)}) collective-permute-start(bf16[720,256]{1,0:T(8,128)(2,1)} %bitcast.9), channel_id=1, source_target_pairs={{0,48},{8,56},{16,0},{24,8},{32,80},{40,88},{48,96},{56,40},{64,11... | collective-permute-start | bytes 1105928 | tf_op jit(solution)/shard_map/ppermute | solution.py:399
  8.1 3.7 %collective-permute-start = (bf16[32,256]{1,0:T(8,128)(2,1)S(1)}, bf16[32,256]{1,0:T(8,128)(2,1)S(1)}, u32[]{:S(2)}, u32[]{:S(2)}) collective-permute-start(bf16[32,256]{1,0:T(8,128)(2,1)S(1)} %bitcast.14), channel_id=1, source_target_pairs={{0,4},{4,0},{1,5},{5,1},{2,6},{6,2},{3,7},{7,3},{8,12},{12,8},{9,1... | collective-permute-start | bytes 49160 | tf_op jit(solution)/shard_map/ppermute | solution.py:397
  11.8 1.0 %copy-start.2 = (bf16[1,45,16,256]{3,2,1,0:T(8,128)(2,1)S(1)}, bf16[1,45,16,256]{3,2,1,0:T(8,128)(2,1)}, u32[]{:S(2)}) copy-start(bf16[1,45,16,256]{3,2,1,0:T(8,128)(2,1)} %param.5) | copy-start | bytes 1105924
  17.1 15.1 %collective-permute-start.2 = (bf16[720,256]{1,0:T(8,128)(2,1)S(1)}, bf16[720,256]{1,0:T(8,128)(2,1)S(1)}, u32[]{:S(2)}, u32[]{:S(2)}) collective-permute-start(bf16[720,256]{1,0:T(8,128)(2,1)S(1)} %collective-permute-done.1.refs_2_), channel_id=1, source_target_pairs={{0,8},{8,16},{16,24},{24,32},{32,40},{40,48},{48,56},{56,64},{64,7... | collective-permute-start | bytes 1105928 | tf_op jit(solution)/shard_map/ppermute | solution.py:409
  17.1 3.9 %collective-permute-start.4 = (bf16[96,256]{1,0:T(8,128)(2,1)S(1)}, bf16[96,256]{1,0:T(8,128)(2,1)S(1)}, u32[]{:S(2)}, u32[]{:S(2)}) collective-permute-start(bf16[96,256]{1,0:T(8,128)(2,1)S(1)} %get-tuple-element.20), channel_id=1, source_target_pairs={{0,1},{1,0},{2,3},{3,2},{4,5},{5,4},{6,7},{7,6},{8,9},{9,8},{10,11... | collective-permute-start | bytes 147464 | tf_op jit(solution)/shard_map/ppermute | solution.py:402
  17.1 5.0 %collective-permute-start.5 = (bf16[96,256]{1,0:T(8,128)(2,1)S(1)}, bf16[96,256]{1,0:T(8,128)(2,1)S(1)}, u32[]{:S(2)}, u32[]{:S(2)}) collective-permute-start(bf16[96,256]{1,0:T(8,128)(2,1)S(1)} %get-tuple-element.25), channel_id=1, source_target_pairs={{0,3},{3,0},{1,2},{2,1},{4,7},{7,4},{5,6},{6,5},{8,11},{11,8},{9,1... | collective-permute-start | bytes 147464 | tf_op jit(solution)/shard_map/ppermute | solution.py:403
  18.6 2.0 %copy-start.1 = (bf16[3,3,3,256,256]{4,3,2,1,0:T(8,128)(2,1)S(1)}, bf16[3,3,3,256,256]{4,3,2,1,0:T(8,128)(2,1)}, u32[]{:S(2)}) copy-start(bf16[3,3,3,256,256]{4,3,2,1,0:T(8,128)(2,1)} %source) | copy-start | bytes 10616836
  22.1 12.0 %collective-permute-start.7 = (bf16[224,256]{1,0:T(8,128)(2,1)S(1)}, bf16[224,256]{1,0:T(8,128)(2,1)S(1)}, u32[]{:S(2)}, u32[]{:S(2)}) collective-permute-start(bf16[224,256]{1,0:T(8,128)(2,1)S(1)} %join.1.refs_2_.refs_3_.refs_4_.refs_5_), channel_id=1, source_target_pairs={{0,8},{8,16},{16,24},{24,32},{32,40},{40,48},{48,56},{56,64},{64,7... | collective-permute-start | bytes 344072 | tf_op jit(solution)/shard_map/ppermute | solution.py:405
  22.2 18.1 %collective-permute-start.8 = (bf16[224,256]{1,0:T(8,128)(2,1)S(1)}, bf16[224,256]{1,0:T(8,128)(2,1)S(1)}, u32[]{:S(2)}, u32[]{:S(2)}) collective-permute-start(bf16[224,256]{1,0:T(8,128)(2,1)S(1)} %join.1.refs_2_.refs_3_.refs_4_.refs_5_), channel_id=1, source_target_pairs={{0,16},{8,24},{16,32},{24,40},{32,48},{40,56},{48,64},{56,72},{64,... | collective-permute-start | bytes 344072 | tf_op jit(solution)/shard_map/ppermute | solution.py:406
  25.2 25.8 %collective-permute-start.11 = (bf16[224,256]{1,0:T(8,128)(2,1)S(1)}, bf16[224,256]{1,0:T(8,128)(2,1)S(1)}, u32[]{:S(2)}, u32[]{:S(2)}) collective-permute-start(bf16[224,256]{1,0:T(8,128)(2,1)S(1)} %join.1.refs_2_.refs_3_.refs_4_.refs_5_), channel_id=1, source_target_pairs={{0,32},{8,40},{16,48},{24,56},{32,64},{40,72},{48,80},{56,88},{64,... | collective-permute-start | bytes 344072 | tf_op jit(solution)/shard_map/ppermute | solution.py:407
  27.7 23.3 %collective-permute-start.10 = (bf16[720,256]{1,0:T(8,128)(2,1)S(1)}, bf16[720,256]{1,0:T(8,128)(2,1)S(1)}, u32[]{:S(2)}, u32[]{:S(2)}) collective-permute-start(bf16[720,256]{1,0:T(8,128)(2,1)S(1)} %collective-permute-done.3), channel_id=1, source_target_pairs={{48,32},{56,40},{0,48},{8,56},{80,64},{88,72},{96,80},{40,88},{112... | collective-permute-start | bytes 1105928 | tf_op jit(solution)/shard_map/ppermute | solution.py:410
  32.1 11.7 %copy-start = (bf16[3,3,3,256,256]{4,3,2,1,0:T(8,128)(2,1)S(1)}, bf16[3,3,3,256,256]{4,3,2,1,0:T(8,128)(2,1)}, u32[]{:S(2)}) copy-start(bf16[3,3,3,256,256]{4,3,2,1,0:T(8,128)(2,1)} %refs_10_.1) | copy-start | bytes 10616836
  32.2 11.6 %copy-start.3 = (f32[256]{0:T(256)S(1)}, f32[256]{0:T(256)}, u32[]{:S(2)}) copy-start(f32[256]{0:T(256)} %param.7) | copy-start | bytes 3076
  32.2 21.0 %collective-permute-start.6 = (bf16[720,256]{1,0:T(8,128)(2,1)S(1)}, bf16[720,256]{1,0:T(8,128)(2,1)S(1)}, u32[]{:S(2)}, u32[]{:S(2)}) collective-permute-start(bf16[720,256]{1,0:T(8,128)(2,1)S(1)} %collective-permute-done.2.refs_3_), channel_id=1, source_target_pairs={{0,8},{8,16},{16,24},{24,32},{32,40},{40,48},{48,56},{56,64},{64,7... | collective-permute-start | bytes 1105928 | tf_op jit(solution)/shard_map/ppermute | solution.py:416
  40.3 12.9 %collective-permute-start.9 = (bf16[224,256]{1,0:T(8,128)(2,1)S(1)}, bf16[224,256]{1,0:T(8,128)(2,1)S(1)}, u32[]{:S(2)}, u32[]{:S(2)}) collective-permute-start(bf16[224,256]{1,0:T(8,128)(2,1)S(1)} %collective-permute-done.8.refs_6_.refs_7_), channel_id=1, source_target_pairs={{0,8},{8,16},{16,24},{24,32},{32,40},{40,48},{48,56},{56,64},{64,7... | collective-permute-start | bytes 344072 | tf_op jit(solution)/shard_map/ppermute | solution.py:418
  51.0 2.2 %copy-start.4 = (f32[256]{0:T(256)S(1)}, f32[256]{0:T(256)}, u32[]{:S(2)}) copy-start(f32[256]{0:T(256)} %param.9) | copy-start | bytes 3076

commit v5 on v4

--- a/solution.py
+++ b/solution.py
@@ -404,7 +404,6 @@
     strips0 = join(tie(rows, first_weight), near, far)
     strips1 = ahead(strips0, perm=next_frame)
     strips2 = ahead(strips0, perm=shifted(count, 2))
-    strips4 = ahead(strips0, perm=shifted(count, 4))
 
     main2 = ahead(tie(main1, to_core), perm=next_frame)
     main4 = ahead(half_way, perm=backward(count, HALF, 4 - HALF))
@@ -416,6 +415,7 @@
     main3 = ahead(main2, perm=next_frame)
     sums, total = step(1, meta, frames, weights, held, sums, total)
     strips3 = ahead(tie(strips2, sums[0]), perm=next_frame)
+    strips4 = ahead(tie(strips2, sums[0]), perm=shifted(count, 2))
     frames += [([main2], strips2), ([main3], strips3), ([main4], strips4)]
     sums, total = step(2, meta, frames[:3], weights, held, sums, total)
     sums, total = step(4, meta, frames, weights, held, sums, total)

time: 60.9 us -> 60.1 us (0.987)
  starting transfers between devices: 22.1 us -> 16.6 us
  waiting for transfers between devices: 11.5 us -> 16.6 us
    ppermute x1, waiting for transfers between devices: 0.01 us -> 4.09 us  [local(): strips4 = ahead(tie(strips2, sums[0]), perm=shifted(count, 2))]
    ppermute x1, starting transfers between devices: 2.55 us -> 0.01 us  [local(): strips4 = ahead(tie(strips2, sums[0]), perm=shifted(count, 2))]
    ppermute x1, waiting for transfers between devices: 3.13 us -> 0.68 us  [local(): strips2 = ahead(strips0, perm=shifted(count, 2))]
    ppermute x1, starting transfers between devices: 3.48 us -> 1.51 us  [local(): strips3 = ahead(tie(strips2, sums[0]), perm=next_frame)]
    ppermute x1, waiting for transfers between devices: 0.82 us -> 2.68 us  [local(): strips1 = ahead(strips0, perm=next_frame)]
    ppermute x1, waiting for transfers between devices: 0.01 us -> 1.65 us  [local(): main2 = ahead(tie(main1, to_core), perm=next_frame)]
    ppermute x1, starting transfers between devices: 1.1 us -> 0.01 us  [local(): main3 = ahead(main2, perm=next_frame)]
  transfers between devices with their start and end apart: 12 -> 12, of which waited for: 5 -> 7; matrix products, arithmetic and copies ran while one was open for 1% -> 1% of each run, Pallas kernels for 26% -> 26%
where the time goes in v5:
time: 60.1 us; the launch traced here: 59.6 us
  Pallas kernels  22.3 us (37%)
  starting transfers between devices  16.6 us (28%)
  waiting for transfers between devices  16.6 us (28%)
  local copies, waits for them, and re-layouts  3 us (5%)
  other arithmetic  0.83 us (1%)
    pallas_call x5, Pallas kernels, step(): pl.pallas_call(functools.partial(step_kernel, steps, plan), out_shape=out...  21.3 us
    ppermute x1, starting transfers between devices, local(): half_way = ahead(own, perm=backward(count, 0, HALF))  5.4 us
    ppermute x1, waiting for transfers between devices, local(): strips4 = ahead(tie(strips2, sums[0]), perm=shifted(count, 2))  4.09 us
    ppermute x1, waiting for transfers between devices, local(): main1 = ahead(own, perm=next_frame)  3.61 us
    unnamed x10, local copies, waits for them, and re-layouts  3 us
    ppermute x1, starting transfers between devices, local(): strips2 = ahead(strips0, perm=shifted(count, 2))  2.95 us
    ppermute x1, waiting for transfers between devices, local(): rows = lax.ppermute(to_row, 'row', [(0, 1), (1, 0)])  2.83 us
    ppermute x1, waiting for transfers between devices, local(): strips1 = ahead(strips0, perm=next_frame)  2.68 us
  transfers between devices with their start and end apart: 12, of which 7 were waited for; matrix products, arithmetic and copies ran while one was open for 1% of the time, Pallas kernels for 26%

profile of v5, /device:TPU:6, one launch (start us, length us, event | category | flops | bytes accessed | tf_op | source)
XLA Modules:
  0.0 59.6 jit_solution(7988864928908458742)
XLA Ops:
  0.0 1.9 %collective-permute-start.1 = (bf16[720,256]{1,0:T(8,128)(2,1)}, bf16[720,256]{1,0:T(8,128)(2,1)S(1)}, u32[]{:S(2)}, u32[]{:S(2)}) collective-permute-start(bf16[720,256]{1,0:T(8,128)(2,1)} %bitcast.8), channel_id=1, source_target_pairs={{0,8},{8,16},{16,24},{24,32},{32,40},{40,48},{48,56},{56,64},{64,7... | collective-permute-start | bytes 1105928 | tf_op jit(solution)/shard_map/ppermute | solution.py:398
  1.9 5.4 %collective-permute-start.3 = (bf16[720,256]{1,0:T(8,128)(2,1)}, bf16[720,256]{1,0:T(8,128)(2,1)S(1)}, u32[]{:S(2)}, u32[]{:S(2)}) collective-permute-start(bf16[720,256]{1,0:T(8,128)(2,1)} %bitcast.9), channel_id=1, source_target_pairs={{0,48},{8,56},{16,0},{24,8},{32,80},{40,88},{48,96},{56,40},{64,11... | collective-permute-start | bytes 1105928 | tf_op jit(solution)/shard_map/ppermute | solution.py:399
  7.3 0.8 %slice_select_fusion = bf16[1,2,16,256]{3,2,1,0:T(8,128)(2,1)S(1)} fusion(bf16[1,45,16,256]{3,2,1,0:T(8,128)(2,1)} %param.5, pred[]{:T(512)S(6)} %eq.3), kind=kLoop, calls=%fused_computation | loop fusion | flops 8192 | bytes 49153 | tf_op jit(solution)/shard_map/jit(_where)/select_n | solution.py:396
  8.1 0.8 %collective-permute-start = (bf16[32,256]{1,0:T(8,128)(2,1)S(1)}, bf16[32,256]{1,0:T(8,128)(2,1)S(1)}, u32[]{:S(2)}, u32[]{:S(2)}) collective-permute-start(bf16[32,256]{1,0:T(8,128)(2,1)S(1)} %bitcast.14), channel_id=1, source_target_pairs={{0,4},{4,0},{1,5},{5,1},{2,6},{6,2},{3,7},{7,3},{8,12},{12,8},{9,1... | collective-permute-start | bytes 49160 | tf_op jit(solution)/shard_map/ppermute | solution.py:397
  8.9 0.1 pad_add_fusion.meta.refs_0_
  9.0 2.8 %collective-permute-done.halo.refs_0_ = bf16[32,256]{1,0:T(8,128)(2,1)S(1)} collective-permute-done((bf16[32,256]{1,0:T(8,128)(2,1)S(1)}, bf16[32,256]{1,0:T(8,128)(2,1)S(1)}, u32[]{:S(2)}, u32[]{:S(2)}) %collective-permute-start) | collective-permute-done | bytes 16416 | tf_op jit(solution)/shard_map/ppermute | solution.py:397
  11.8 0.0 copy-start.2
  11.8 1.0 %copy-done.2 = bf16[1,45,16,256]{3,2,1,0:T(8,128)(2,1)S(1)} copy-done((bf16[1,45,16,256]{3,2,1,0:T(8,128)(2,1)S(1)}, bf16[1,45,16,256]{3,2,1,0:T(8,128)(2,1)}, u32[]{:S(2)}) %copy-start.2) | copy-done | bytes 368664
  12.8 0.7 %pack.1 = (bf16[96,256]{1,0:T(8,128)(2,1)S(1)}, bf16[96,256]{1,0:T(8,128)(2,1)S(1)}, bf16[720,256]{1,0:T(8,128)(2,1)S(1)}) custom-call(s32[3]{0:T(128)S(1)} %pad_add_fusion.meta.refs_0_, bf16[720,256]{1,0:T(8,128)(2,1)S(1)} %bitcast.10, bf16[32,256]{1,0:T(8,128)(2,1)S(1)} %collective-permute-done.halo.refs_0_), custom_call_target="tpu_custom_call" | custom-call | flops 1000000 | bytes 800000 | tf_op jit(solution)/shard_map/pack/pallas_call | solution.py:370
  13.5 3.6 %collective-permute-done.1.refs_2_ = bf16[720,256]{1,0:T(8,128)(2,1)S(1)} collective-permute-done((bf16[720,256]{1,0:T(8,128)(2,1)}, bf16[720,256]{1,0:T(8,128)(2,1)S(1)}, u32[]{:S(2)}, u32[]{:S(2)}) %collective-permute-start.1) | collective-permute-done | bytes 368672 | tf_op jit(solution)/shard_map/ppermute | solution.py:398
  17.1 0.0 collective-permute-start.2
  17.1 0.0 collective-permute-start.4
  17.1 1.5 %collective-permute-start.5 = (bf16[96,256]{1,0:T(8,128)(2,1)S(1)}, bf16[96,256]{1,0:T(8,128)(2,1)S(1)}, u32[]{:S(2)}, u32[]{:S(2)}) collective-permute-start(bf16[96,256]{1,0:T(8,128)(2,1)S(1)} %get-tuple-element.25), channel_id=1, source_target_pairs={{0,3},{3,0},{1,2},{2,1},{4,7},{7,4},{5,6},{6,5},{8,11},{11,8},{9,1... | collective-permute-start | bytes 147464 | tf_op jit(solution)/shard_map/ppermute | solution.py:403
  18.6 0.0 copy-start.1
  18.6 2.0 %copy-done.1 = bf16[3,3,3,256,256]{4,3,2,1,0:T(8,128)(2,1)S(1)} copy-done((bf16[3,3,3,256,256]{4,3,2,1,0:T(8,128)(2,1)S(1)}, bf16[3,3,3,256,256]{4,3,2,1,0:T(8,128)(2,1)}, u32[]{:S(2)}) %copy-start.1) | copy-done | bytes 3538968
  20.6 0.4 bring.1.refs_3_.refs_5_.refs_7_.refs_9_
  21.0 0.0 collective-permute-done.4.refs_1_
  21.1 1.1 %collective-permute-done.5.refs_2_ = bf16[96,256]{1,0:T(8,128)(2,1)S(1)} collective-permute-done((bf16[96,256]{1,0:T(8,128)(2,1)S(1)}, bf16[96,256]{1,0:T(8,128)(2,1)S(1)}, u32[]{:S(2)}, u32[]{:S(2)}) %collective-permute-start.5) | collective-permute-done | bytes 49184 | tf_op jit(solution)/shard_map/ppermute | solution.py:403
  22.1 0.1 collective-permute-start.7
  22.2 2.9 %collective-permute-start.8 = (bf16[224,256]{1,0:T(8,128)(2,1)S(1)}, bf16[224,256]{1,0:T(8,128)(2,1)S(1)}, u32[]{:S(2)}, u32[]{:S(2)}) collective-permute-start(bf16[224,256]{1,0:T(8,128)(2,1)S(1)} %join.1.refs_2_.refs_3_.refs_4_.refs_5_), channel_id=1, source_target_pairs={{0,16},{8,24},{16,32},{24,40},{32,48},{40,56},{48,64},{56,72},{64,... | collective-permute-start | bytes 344072 | tf_op jit(solution)/shard_map/ppermute | solution.py:406
  25.2 0.0 collective-permute-done.3
  25.2 2.4 %collective-permute-start.10 = (bf16[720,256]{1,0:T(8,128)(2,1)S(1)}, bf16[720,256]{1,0:T(8,128)(2,1)S(1)}, u32[]{:S(2)}, u32[]{:S(2)}) collective-permute-start(bf16[720,256]{1,0:T(8,128)(2,1)S(1)} %collective-permute-done.3), channel_id=1, source_target_pairs={{48,32},{56,40},{0,48},{8,56},{80,64},{88,72},{96,80},{40,88},{112... | collective-permute-start | bytes 1105928 | tf_op jit(solution)/shard_map/ppermute | solution.py:409
  27.6 2.1 %step0.1.refs_6_ = f32[832,256]{1,0:T(8,128)S(1)} custom-call(s32[3]{0:T(128)S(1)} %pad_add_fusion.meta.refs_0_, bf16[720,256]{1,0:T(8,128)(2,1)S(1)} %get-tuple-element.19.refs_1_.refs_13_, bf16[224,256]{1,0:T(8,128)(2,1)S(1)} %join.1.refs_2_.refs_3_.refs_4_.refs_5_, bf16[3,3,3,256,256]{4,3,2,1,0:T(8,128)(2,1)S(1)} %bring.1.refs_3_.refs_5_.refs_7_.refs_9_), custom_call_target="tpu_custom_call" | custom-call | flops 1000000000 | bytes 1000000 | tf_op jit(solution)/shard_map/step0/pallas_call | solution.py:280
  29.7 0.0 copy-start
  29.7 0.0 copy-start.3
  29.8 1.7 %collective-permute-done.2.refs_3_ = bf16[720,256]{1,0:T(8,128)(2,1)S(1)} collective-permute-done((bf16[720,256]{1,0:T(8,128)(2,1)S(1)}, bf16[720,256]{1,0:T(8,128)(2,1)S(1)}, u32[]{:S(2)}, u32[]{:S(2)}) %collective-permute-start.2) | collective-permute-done | bytes 368672 | tf_op jit(solution)/shard_map/ppermute | solution.py:408
  31.4 0.0 collective-permute-start.6
  31.4 2.7 %collective-permute-done.7.refs_4_.refs_5_.refs_6_ = bf16[224,256]{1,0:T(8,128)(2,1)S(1)} collective-permute-done((bf16[224,256]{1,0:T(8,128)(2,1)S(1)}, bf16[224,256]{1,0:T(8,128)(2,1)S(1)}, u32[]{:S(2)}, u32[]{:S(2)}) %collective-permute-start.7) | collective-permute-done | bytes 114720 | tf_op jit(solution)/shard_map/ppermute | solution.py:405
  34.1 3.1 %step1.1 = (f32[832,256]{1,0:T(8,128)S(1)}, f32[832,256]{1,0:T(8,128)S(1)}) custom-call(s32[3]{0:T(128)S(1)} %pad_add_fusion.meta.refs_0_, bf16[720,256]{1,0:T(8,128)(2,1)S(1)} %get-tuple-element.19.refs_1_.refs_13_, bf16[720,256]{1,0:T(8,128)(2,1)S(1)} %collective-permute-done.1.refs_2_, bf16[224,256]{1,0:T(8,128)(2,1)S(1)} %join.1.refs_2_.refs_3_.refs_4_.refs_5_, ...), custom_call_target="tpu_custom_call" | custom-call | flops 2000000000 | bytes 1000000 | tf_op jit(solution)/shard_map/step1/pallas_call | solution.py:280
  37.2 0.7 %collective-permute-done.8.refs_6_.refs_7_ = bf16[224,256]{1,0:T(8,128)(2,1)S(1)} collective-permute-done((bf16[224,256]{1,0:T(8,128)(2,1)S(1)}, bf16[224,256]{1,0:T(8,128)(2,1)S(1)}, u32[]{:S(2)}, u32[]{:S(2)}) %collective-permute-start.8) | collective-permute-done | bytes 114720 | tf_op jit(solution)/shard_map/ppermute | solution.py:406
  37.9 0.0 collective-permute-start.11
  37.9 1.5 %collective-permute-start.9 = (bf16[224,256]{1,0:T(8,128)(2,1)S(1)}, bf16[224,256]{1,0:T(8,128)(2,1)S(1)}, u32[]{:S(2)}, u32[]{:S(2)}) collective-permute-start(bf16[224,256]{1,0:T(8,128)(2,1)S(1)} %collective-permute-done.8.refs_6_.refs_7_), channel_id=1, source_target_pairs={{0,8},{8,16},{16,24},{24,32},{32,40},{40,48},{48,56},{56,64},{64,7... | collective-permute-start | bytes 344072 | tf_op jit(solution)/shard_map/ppermute | solution.py:417
  39.4 0.0 copy-done
  39.4 0.0 copy-done.3
  39.4 7.2 %step2.1 = (f32[832,256]{1,0:T(8,128)S(1)}, f32[832,256]{1,0:T(8,128)S(1)}, f32[720,256]{1,0:T(8,128)S(1)}) custom-call(s32[3]{0:T(128)S(1)} %pad_add_fusion.meta.refs_0_, bf16[720,256]{1,0:T(8,128)(2,1)S(1)} %get-tuple-element.19.refs_1_.refs_13_, bf16[720,256]{1,0:T(8,128)(2,1)S(1)} %collective-permute-done.1.refs_2_, ...), custom_call_target="tpu_custom_call" | custom-call | flops 2000000000 | bytes 1000000 | tf_op jit(solution)/shard_map/step2/pallas_call | solution.py:280
  46.6 4.1 %collective-permute-done.11.refs_8_ = bf16[224,256]{1,0:T(8,128)(2,1)S(1)} collective-permute-done((bf16[224,256]{1,0:T(8,128)(2,1)S(1)}, bf16[224,256]{1,0:T(8,128)(2,1)S(1)}, u32[]{:S(2)}, u32[]{:S(2)}) %collective-permute-start.11) | collective-permute-done | bytes 114720 | tf_op jit(solution)/shard_map/ppermute | solution.py:418
  50.7 0.0 collective-permute-done.10.refs_4_
  50.7 0.0 copy-start.4
  50.7 2.1 %step4.1.refs_15_ = f32[832,256]{1,0:T(8,128)S(1)} custom-call(s32[3]{0:T(128)S(1)} %pad_add_fusion.meta.refs_0_, bf16[720,256]{1,0:T(8,128)(2,1)S(1)} %get-tuple-element.19.refs_1_.refs_13_, bf16[720,256]{1,0:T(8,128)(2,1)S(1)} %collective-permute-done.1.refs_2_, bf16[720,256]{1,0:T(8,128)(2,1)S(1)} %collective-permute-done.2.refs_3_, ...), custom_call_target="tpu_custom_call" | custom-call | flops 500000000 | bytes 1000000 | tf_op jit(solution)/shard_map/step4/pallas_call | solution.py:280
  52.8 0.0 collective-permute-done.9.refs_8_
  52.8 0.0 collective-permute-done.6.refs_4_
  52.9 0.0 copy-done.4
  52.9 6.7 %step3.1 = bf16[720,256]{1,0:T(8,128)(2,1)} custom-call(s32[3]{0:T(128)S(1)} %pad_add_fusion.meta.refs_0_, bf16[720,256]{1,0:T(8,128)(2,1)S(1)} %get-tuple-element.19.refs_1_.refs_13_, bf16[720,256]{1,0:T(8,128)(2,1)S(1)} %collective-permute-done.1.refs_2_, bf16[720,256]{1,0:T(8,128)(2,1)S(1)} %collective-permute-done.2.refs_3_, ...), custom_call_target="tpu_custom_call" | custom-call | flops 3000000000 | bytes 1000000 | tf_op jit(solution)/shard_map/step3/pallas_call | solution.py:280
  (1 shorter events, 0.0 us)
Async XLA Ops:
  0.0 17.1 %collective-permute-start.1 = (bf16[720,256]{1,0:T(8,128)(2,1)}, bf16[720,256]{1,0:T(8,128)(2,1)S(1)}, u32[]{:S(2)}, u32[]{:S(2)}) collective-permute-start(bf16[720,256]{1,0:T(8,128)(2,1)} %bitcast.8), channel_id=1, source_target_pairs={{0,8},{8,16},{16,24},{24,32},{32,40},{40,48},{48,56},{56,64},{64,7... | collective-permute-start | bytes 1105928 | tf_op jit(solution)/shard_map/ppermute | solution.py:398
  1.9 23.3 %collective-permute-start.3 = (bf16[720,256]{1,0:T(8,128)(2,1)}, bf16[720,256]{1,0:T(8,128)(2,1)S(1)}, u32[]{:S(2)}, u32[]{:S(2)}) collective-permute-start(bf16[720,256]{1,0:T(8,128)(2,1)} %bitcast.9), channel_id=1, source_target_pairs={{0,48},{8,56},{16,0},{24,8},{32,80},{40,88},{48,96},{56,40},{64,11... | collective-permute-start | bytes 1105928 | tf_op jit(solution)/shard_map/ppermute | solution.py:399
  8.1 3.7 %collective-permute-start = (bf16[32,256]{1,0:T(8,128)(2,1)S(1)}, bf16[32,256]{1,0:T(8,128)(2,1)S(1)}, u32[]{:S(2)}, u32[]{:S(2)}) collective-permute-start(bf16[32,256]{1,0:T(8,128)(2,1)S(1)} %bitcast.14), channel_id=1, source_target_pairs={{0,4},{4,0},{1,5},{5,1},{2,6},{6,2},{3,7},{7,3},{8,12},{12,8},{9,1... | collective-permute-start | bytes 49160 | tf_op jit(solution)/shard_map/ppermute | solution.py:397
  11.8 1.0 %copy-start.2 = (bf16[1,45,16,256]{3,2,1,0:T(8,128)(2,1)S(1)}, bf16[1,45,16,256]{3,2,1,0:T(8,128)(2,1)}, u32[]{:S(2)}) copy-start(bf16[1,45,16,256]{3,2,1,0:T(8,128)(2,1)} %param.5) | copy-start | bytes 1105924
  17.1 14.3 %collective-permute-start.2 = (bf16[720,256]{1,0:T(8,128)(2,1)S(1)}, bf16[720,256]{1,0:T(8,128)(2,1)S(1)}, u32[]{:S(2)}, u32[]{:S(2)}) collective-permute-start(bf16[720,256]{1,0:T(8,128)(2,1)S(1)} %collective-permute-done.1.refs_2_), channel_id=1, source_target_pairs={{0,8},{8,16},{16,24},{24,32},{32,40},{40,48},{48,56},{56,64},{64,7... | collective-permute-start | bytes 1105928 | tf_op jit(solution)/shard_map/ppermute | solution.py:408
  17.1 3.9 %collective-permute-start.4 = (bf16[96,256]{1,0:T(8,128)(2,1)S(1)}, bf16[96,256]{1,0:T(8,128)(2,1)S(1)}, u32[]{:S(2)}, u32[]{:S(2)}) collective-permute-start(bf16[96,256]{1,0:T(8,128)(2,1)S(1)} %get-tuple-element.20), channel_id=1, source_target_pairs={{0,1},{1,0},{2,3},{3,2},{4,5},{5,4},{6,7},{7,6},{8,9},{9,8},{10,11... | collective-permute-start | bytes 147464 | tf_op jit(solution)/shard_map/ppermute | solution.py:402
  17.1 5.0 %collective-permute-start.5 = (bf16[96,256]{1,0:T(8,128)(2,1)S(1)}, bf16[96,256]{1,0:T(8,128)(2,1)S(1)}, u32[]{:S(2)}, u32[]{:S(2)}) collective-permute-start(bf16[96,256]{1,0:T(8,128)(2,1)S(1)} %get-tuple-element.25), channel_id=1, source_target_pairs={{0,3},{3,0},{1,2},{2,1},{4,7},{7,4},{5,6},{6,5},{8,11},{11,8},{9,1... | collective-permute-start | bytes 147464 | tf_op jit(solution)/shard_map/ppermute | solution.py:403
  18.6 2.0 %copy-start.1 = (bf16[3,3,3,256,256]{4,3,2,1,0:T(8,128)(2,1)S(1)}, bf16[3,3,3,256,256]{4,3,2,1,0:T(8,128)(2,1)}, u32[]{:S(2)}) copy-start(bf16[3,3,3,256,256]{4,3,2,1,0:T(8,128)(2,1)} %source) | copy-start | bytes 10616836
  22.1 12.0 %collective-permute-start.7 = (bf16[224,256]{1,0:T(8,128)(2,1)S(1)}, bf16[224,256]{1,0:T(8,128)(2,1)S(1)}, u32[]{:S(2)}, u32[]{:S(2)}) collective-permute-start(bf16[224,256]{1,0:T(8,128)(2,1)S(1)} %join.1.refs_2_.refs_3_.refs_4_.refs_5_), channel_id=1, source_target_pairs={{0,8},{8,16},{16,24},{24,32},{32,40},{40,48},{48,56},{56,64},{64,7... | collective-permute-start | bytes 344072 | tf_op jit(solution)/shard_map/ppermute | solution.py:405
  22.2 15.6 %collective-permute-start.8 = (bf16[224,256]{1,0:T(8,128)(2,1)S(1)}, bf16[224,256]{1,0:T(8,128)(2,1)S(1)}, u32[]{:S(2)}, u32[]{:S(2)}) collective-permute-start(bf16[224,256]{1,0:T(8,128)(2,1)S(1)} %join.1.refs_2_.refs_3_.refs_4_.refs_5_), channel_id=1, source_target_pairs={{0,16},{8,24},{16,32},{24,40},{32,48},{40,56},{48,64},{56,72},{64,... | collective-permute-start | bytes 344072 | tf_op jit(solution)/shard_map/ppermute | solution.py:406
  25.2 25.5 %collective-permute-start.10 = (bf16[720,256]{1,0:T(8,128)(2,1)S(1)}, bf16[720,256]{1,0:T(8,128)(2,1)S(1)}, u32[]{:S(2)}, u32[]{:S(2)}) collective-permute-start(bf16[720,256]{1,0:T(8,128)(2,1)S(1)} %collective-permute-done.3), channel_id=1, source_target_pairs={{48,32},{56,40},{0,48},{8,56},{80,64},{88,72},{96,80},{40,88},{112... | collective-permute-start | bytes 1105928 | tf_op jit(solution)/shard_map/ppermute | solution.py:409
  29.7 9.6 %copy-start = (bf16[3,3,3,256,256]{4,3,2,1,0:T(8,128)(2,1)S(1)}, bf16[3,3,3,256,256]{4,3,2,1,0:T(8,128)(2,1)}, u32[]{:S(2)}) copy-start(bf16[3,3,3,256,256]{4,3,2,1,0:T(8,128)(2,1)} %refs_10_.1) | copy-start | bytes 10616836
  29.7 9.6 %copy-start.3 = (f32[256]{0:T(256)S(1)}, f32[256]{0:T(256)}, u32[]{:S(2)}) copy-start(f32[256]{0:T(256)} %param.7) | copy-start | bytes 3076
  31.4 21.4 %collective-permute-start.6 = (bf16[720,256]{1,0:T(8,128)(2,1)S(1)}, bf16[720,256]{1,0:T(8,128)(2,1)S(1)}, u32[]{:S(2)}, u32[]{:S(2)}) collective-permute-start(bf16[720,256]{1,0:T(8,128)(2,1)S(1)} %collective-permute-done.2.refs_3_), channel_id=1, source_target_pairs={{0,8},{8,16},{16,24},{24,32},{32,40},{40,48},{48,56},{56,64},{64,7... | collective-permute-start | bytes 1105928 | tf_op jit(solution)/shard_map/ppermute | solution.py:415
  37.9 12.8 %collective-permute-start.11 = (bf16[224,256]{1,0:T(8,128)(2,1)S(1)}, bf16[224,256]{1,0:T(8,128)(2,1)S(1)}, u32[]{:S(2)}, u32[]{:S(2)}) collective-permute-start(bf16[224,256]{1,0:T(8,128)(2,1)S(1)} %collective-permute-done.8.refs_6_.refs_7_), channel_id=1, source_target_pairs={{0,16},{8,24},{16,32},{24,40},{32,48},{40,56},{48,64},{56,72},{64,... | collective-permute-start | bytes 344072 | tf_op jit(solution)/shard_map/ppermute | solution.py:418
  37.9 15.0 %collective-permute-start.9 = (bf16[224,256]{1,0:T(8,128)(2,1)S(1)}, bf16[224,256]{1,0:T(8,128)(2,1)S(1)}, u32[]{:S(2)}, u32[]{:S(2)}) collective-permute-start(bf16[224,256]{1,0:T(8,128)(2,1)S(1)} %collective-permute-done.8.refs_6_.refs_7_), channel_id=1, source_target_pairs={{0,8},{8,16},{16,24},{24,32},{32,40},{40,48},{48,56},{56,64},{64,7... | collective-permute-start | bytes 344072 | tf_op jit(solution)/shard_map/ppermute | solution.py:417
  50.7 2.2 %copy-start.4 = (f32[256]{0:T(256)S(1)}, f32[256]{0:T(256)}, u32[]{:S(2)}) copy-start(f32[256]{0:T(256)} %param.9) | copy-start | bytes 3076
